TPU v7x, 128 devices: a whole 4x4x4 slice. The times are simulated.
128 devices in a mesh: grp: 4 (over x), tp: 32 (over z, y, core).
Axes of the slice: x: 4, y: 4, z: 4, core: 2. Of those that a mesh axis runs over, the one named last changes fastest.
Arguments:
- tokens: bfloat16 [4096, 8192], P('grp', 'tp'), may hold values from -6 to 6
- norm_gain: bfloat16 [8192], P('tp'), may hold values from 0.5 to 1.5
- w_query: bfloat16 [8192, 8192], P(None, 'tp'), may hold values from -0.0625 to 0.0625
- key_value_weight: bfloat16 [8192, 2, 1024], P(None, None, 'tp'), may hold values from -0.0625 to 0.0625
- w_out: bfloat16 [8192, 8192], P('tp'), may hold values from -0.0625 to 0.0625
- doc_lengths: int32 [4, 4], P('grp'), may hold values from 1 to 512, 1024 in all within a row
- holder: int32 [256, 1], replicated, may hold values from 0 to 127; in each aligned block of 64 rows (0 to 63, 64 to 127, ...) at most 2 rows name the same one
Outputs:
- mixed: bfloat16 [4096, 8192], P('grp', 'tp')
- kv_store: bfloat16 [128, 4, 2, 2, 128, 128], P(('grp', 'tp'))
Inputs may be any that keep to these rules, and one draw needn't show every extreme that they name: holder names a device by its index over grp and tp together, grp slowest. Within the 64 rows of one group no device is named more than 2 times, and some device exactly 2 times. `doc_lengths`: each row lists whole document lengths summing to 1024.
All inputs are finite; a program needn't handle non-finite values.
Results may differ from a plain program's by a relative error of at most 0.01.
Values may be sent and summed in bfloat16 or wider, within the bound.
No kernel may reach another device: no remote copies, remote signals or barrier semaphores. Data moves between devices by JAX's collectives and lax.ppermute only.
A program may use at most 128 MiB of HBM per device.

v0:
```python
import math

import jax
import jax.numpy as jnp
from jax import lax
from jax.sharding import PartitionSpec as P

MODEL_WIDTH = 8192
QUERY_HEADS = 64
KEY_VALUE_HEADS = 8
HEAD_SIZE = 128
BLOCK_TOKENS = 128
HOLD = 2


rope_base = 500000.0
norm_eps = 1e-05
mask_fill = -1e30


def doc_starts(lengths_row, sequence_length):
    ends = jnp.cumsum(lengths_row)
    indices = jnp.arange(sequence_length, dtype=jnp.int32)
    passed = (indices[:, None] >= ends[None, :]).astype(jnp.int32)
    return jnp.sum(passed * lengths_row[None, :], axis=1)


def rotate(vectors, token_positions):
    half_dim = vectors.shape[-1] // 2
    frequency = jnp.exp(
        jnp.arange(half_dim, dtype=jnp.float32) * (-2.0 * math.log(rope_base) / vectors.shape[-1])
    )
    angles = token_positions.astype(jnp.float32)[:, None, None] * frequency[None, None, :]
    cosine = jnp.cos(angles)
    sine = jnp.sin(angles)
    first = vectors[..., :half_dim]
    second = vectors[..., half_dim:]
    return jnp.concatenate(
        [first * cosine - second * sine, second * cosine + first * sine], axis=-1
    )


def local(tokens, norm_gain, w_query, key_value_weight, w_out, doc_lengths, holder):
    groups = lax.axis_size("grp")
    width = lax.axis_size("tp")
    tp_index = lax.axis_index("tp")
    grp_index = lax.axis_index("grp")
    sequence_length = tokens.shape[0]
    tok_float = tokens.astype(jnp.float32)
    local_squares = jnp.sum(tok_float * tok_float, axis=1)
    total_squares = lax.psum(local_squares, "tp")
    factor = lax.rsqrt(total_squares / MODEL_WIDTH + norm_eps)[:, None]
    normalized_input = (tok_float * factor * norm_gain.astype(jnp.float32)[None, :]).astype(
        jnp.bfloat16
    )
    query_cols = w_query.shape[1]
    kv_cols = key_value_weight.shape[2]
    flat_keyval = key_value_weight.reshape(MODEL_WIDTH, 2 * kv_cols)
    piece = lax.all_gather(normalized_input, "tp", axis=1, tiled=True)
    projected = jnp.concatenate(
        [
            jnp.dot(piece, w_query, preferred_element_type=jnp.float32),
            jnp.dot(piece, flat_keyval, preferred_element_type=jnp.float32),
        ],
        axis=1,
    )
    starts = doc_starts(doc_lengths[0], sequence_length)
    token_positions = jnp.arange(sequence_length, dtype=jnp.int32) - starts
    heads_here = query_cols // HEAD_SIZE
    queries = rotate(
        projected[:, :query_cols].reshape(sequence_length, heads_here, HEAD_SIZE), token_positions
    ).astype(jnp.bfloat16)
    keyval_part = (
        projected[:, query_cols:].astype(jnp.bfloat16).reshape(sequence_length, 2, kv_cols)
    )
    key_value_rows = lax.all_gather(keyval_part, "tp", axis=2, tiled=True)
    rotary_keys = rotate(
        key_value_rows[:, 0]
        .reshape(sequence_length, KEY_VALUE_HEADS, HEAD_SIZE)
        .astype(jnp.float32),
        token_positions,
    ).astype(jnp.bfloat16)
    value_rows = key_value_rows[:, 1].reshape(sequence_length, KEY_VALUE_HEADS, HEAD_SIZE)
    device_portion = QUERY_HEADS // KEY_VALUE_HEADS
    kv_index = tp_index * heads_here // device_portion
    key_slice = lax.dynamic_index_in_dim(rotary_keys, kv_index, 1, keepdims=False)
    value_slice = lax.dynamic_index_in_dim(value_rows, kv_index, 1, keepdims=False)
    indices = jnp.arange(sequence_length, dtype=jnp.int32)
    allowed = (indices[None, :] <= indices[:, None]) & (indices[None, :] >= starts[:, None])
    scores = jnp.einsum("qhd,kd->hqk", queries, key_slice, preferred_element_type=jnp.float32)
    scores = scores * (1.0 / math.sqrt(HEAD_SIZE))
    scores = jnp.where(allowed[None], scores, mask_fill)
    peak = jnp.max(scores, axis=-1, keepdims=True)
    weights = jnp.exp(scores - peak)
    probs = (weights / jnp.sum(weights, axis=-1, keepdims=True)).astype(jnp.bfloat16)
    attention_output = jnp.einsum(
        "hqk,kd->qhd", probs, value_slice, preferred_element_type=jnp.float32
    )
    attention_output = attention_output.astype(jnp.bfloat16).reshape(sequence_length, query_cols)
    term = jnp.dot(attention_output, w_out, preferred_element_type=jnp.float32)
    own_cols = lax.psum_scatter(
        term.astype(jnp.bfloat16), "tp", scatter_dimension=1, tiled=True
    ).astype(jnp.float32)
    mixed = (tok_float + own_cols).astype(jnp.bfloat16)
    head_block_count = sequence_length // BLOCK_TOKENS * KEY_VALUE_HEADS
    paged_blocks = jnp.stack([rotary_keys, value_rows], axis=1).reshape(
        sequence_length // BLOCK_TOKENS, BLOCK_TOKENS, 2, KEY_VALUE_HEADS, HEAD_SIZE
    )
    paged_blocks = paged_blocks.transpose(0, 3, 2, 1, 4).reshape(
        head_block_count, 2, BLOCK_TOKENS, HEAD_SIZE
    )
    owners = lax.dynamic_slice_in_dim(
        holder[:, 0], grp_index * head_block_count, head_block_count, 0
    )
    targets = jnp.arange(groups, dtype=jnp.int32) * width + tp_index
    onehot = (owners[:, None] == targets[None, :]).astype(jnp.int32)
    slot_rank = jnp.cumsum(onehot, axis=0) - onehot
    chooser = jnp.stack(
        [onehot * (slot_rank == slot).astype(jnp.int32) for slot in range(HOLD)], axis=0
    )
    payload = jnp.einsum(
        "rbg,bkxd->grkxd",
        chooser.astype(jnp.bfloat16),
        paged_blocks,
        preferred_element_type=jnp.float32,
    )
    payload = payload.astype(jnp.bfloat16)
    received = lax.all_to_all(payload, "grp", split_axis=0, concat_axis=0, tiled=True)
    return (mixed, received[None])


def solution(mesh):
    return jax.shard_map(
        local,
        mesh=mesh,
        in_specs=(
            P("grp", "tp"),
            P("tp"),
            P(None, "tp"),
            P(None, None, "tp"),
            P("tp", None),
            P("grp", None),
            P(),
        ),
        out_specs=(P("grp", "tp"), P(("grp", "tp"), None, None, None, None, None)),
        check_vma=False,
    )
```

profile of v0, /device:TPU:0, one launch (start us, length us, event | category | flops | bytes accessed | tf_op | source)
XLA Modules:
  0.0 383.5 jit_solution(17703257076062091742)
XLA Ops:
  7.2 0.7 convert_element_type.81
  8.0 1.3 fusion.15
  9.2 68.7 %psum.7 = f32[1024]{0:T(1024)S(1)} all-reduce(f32[1024]{0:T(1024)S(1)} %fusion.15), channel_id=1, replica_groups=mesh['grp'=4,'tp'=32] {'tp'}, use_global_device_ids=true, to_apply=%region_1.0 | all-reduce | flops 1024 | bytes 8192 | tf_op jit(solution)/shard_map/psum | solution.py:51
  77.9 2.0 fusion.17
  80.0 77.6 %all-gather.3.cloned.1.call-done = bf16[1024,8192]{1,0:T(8,128)(2,1)} async-done(((bf16[1024,256]{1,0:T(8,128)(2,1)}), bf16[1024,8192]{1,0:T(8,128)(2,1)}) %all-gather.3.cloned.1.call-update) | async-done | bytes 16777232 | tf_op jit(solution)/shard_map/all_gather | solution.py:59
  157.7 11.6 %convolution_convert_fusion.1 = bf16[1024,64]{0,1:T(8,128)(2,1)} fusion(bf16[1024,8192]{1,0:T(8,128)(2,1)} %all-gather.3.cloned.1.call-done, bf16[8192,64]{0,1:T(8,128)(2,1)S(1)} %bitcast.85), kind=kOutput, calls=%fused_computation.29 | convolution fusion | flops 1073807360 | bytes 17956864 | tf_op jit(solution)/shard_map/dot_general | solution.py:63
  169.7 1.9 multiply_cosine_fusion
  171.6 1.5 fusion.9
  173.1 9.5 %fusion.55 = f32[1024,256]{0,1:T(8,128)S(1)} fusion(bf16[1024,8192]{1,0:T(8,128)(2,1)} %all-gather.3.cloned.1.call-done, bf16[8192,256]{1,0:T(8,128)(2,1)} %param.9), kind=kOutput, calls=%fused_computation.73 | convolution fusion | flops 4294967296 | bytes 22020096 | tf_op jit(solution)/shard_map/dot_general | solution.py:62
  182.6 0.9 fusion.49
  183.8 1.4 copy.46
  185.2 1.2 subtract_convert_fusion.1
  186.4 29.5 %all-gather.5.cloned.1.call-done = bf16[1024,2,1024]{0,2,1:T(8,128)(2,1)} async-done(((bf16[1024,2,32]{0,2,1:T(8,128)(2,1)}), bf16[1024,2,1024]{0,2,1:T(8,128)(2,1)}) %all-gather.5.cloned.1.call-update) | async-done | bytes 4194320 | tf_op jit(solution)/shard_map/all_gather | solution.py:76
  215.9 4.5 %slice_bitcast_fusion = (bf16[128,8,8,128]{3,1,2,0:T(8,128)(2,1)S(1)}, bf16[1024,1,1024]{0,2,1:T(8,128)(2,1)S(1)}, bf16[1024,1,1024]{0,2,1:T(8,128)(2,1)}) fusion(bf16[1024,2,1024]{0,2,1:T(8,128)(2,1)} %all-gather.5.cloned.1.call-done), kind=kLoop, calls=%fused_computation.69 | loop fusion | bytes 10485760
  220.4 2.5 fusion.48
  222.9 3.8 copy.44
  226.6 3.8 copy.45
  230.4 6.6 %add_convert_fusion = (bf16[1024,8,64]{2,0,1:T(8,128)(2,1)}, bf16[1024,8,64]{2,0,1:T(8,128)(2,1)}) fusion(f32[1024,8,64]{2,0,1:T(8,128)} %copy.44, f32[1024,8,64]{2,0,1:T(8,128)} %copy.45, f32[1024,64]{1,0:T(8,128)S(1)} %get-tuple-element.20, f32[1024,64]{1,0:T(8,128)S(1)} %get-tuple-element.19), kind=kLoop, calls=%fused_computation.14 | loop fusion | flops 4194304 | bytes 6815744 | tf_op jit(solution)/shard_map/convert.10
  237.0 8.5 %fusion.50 = (f32[2,1024]{1,0:T(2,128)S(1)}, f32[2,1024,1024]{1,2,0:T(8,128)}) fusion(pred[1024,1024]{0,1:T(8,128)(4,1)} %fusion.9, bf16[1024,2,64]{2,0,1:T(8,128)(2,1)} %get-tuple-element.14, bf16[1024,2,64]{2,0,1:T(8,128)(2,1)} %get-tuple-element.13, s32[]{:T(128)S(6)} %select_n.18, bf16[1024,8,64]{2,0,1:T(8,128)(2,1)} %get-tuple-element.9, ...), kind=kOutput, calls=%fused_computation.72 | convolution fusion | flops 546833408 | bytes 12066820 | tf_op jit(solution)/shard_map/sub | solution.py:94
  245.5 4.2 %fusion.12 = bf16[128,2,1024]{2,0,1:T(8,128)(2,1)S(1)} fusion(f32[2,1024,1024]{1,2,0:T(8,128)} %get-tuple-element.24, f32[2,1024]{1,0:T(2,128)S(1)} %get-tuple-element.23, bf16[1024,8,128]{0,2,1:T(8,128)(2,1)} %bitcast.90, s32[]{:T(128)S(6)} %select_n.18), kind=kOutput, calls=%fused_computation.26 | convolution fusion | flops 541327360 | bytes 9183236 | tf_op jit(solution)/shard_map/hqk,kd->qhd/dot_general | solution.py:96
  249.7 10.5 %convolution_convert_fusion = bf16[1024,8192]{1,0:T(8,128)(2,1)} fusion(bf16[1024,256]{0,1:T(8,128)(2,1)S(1)} %bitcast.93, bf16[256,8192]{1,0:T(8,128)(2,1)} %param.11), kind=kOutput, calls=%fused_computation.1 | convolution fusion | flops 4303355904 | bytes 21495808 | tf_op jit(solution)/shard_map/dot_general | solution.py:100
  260.3 0.6 copy-done.6
  261.3 2.0 copy.48
  263.3 6.9 %copy.37 = bf16[8,128,1,8,128]{4,3,0,1,2:T(8,128)(2,1)} copy(bf16[8,128,1,8,128]{1,0,4,3,2:T(8,128)(2,1)} %bitcast.87) | data formatting | bytes 4194304 | tf_op jit(solution)/shard_map/stack | solution.py:106
  270.1 3.2 copy.35
  273.4 1.4 copy.36
  274.8 1.6 fusion.14
  276.4 0.4 copy.39
  276.9 14.0 %all_to_all.5 = bf16[4,2,2,128,128]{4,1,3,2,0:T(2,128)(2,1)S(1)} all-to-all(bf16[4,2,2,128,128]{4,1,3,2,0:T(2,128)(2,1)S(1)} %copy.39), channel_id=1, replica_groups=mesh['grp'=4,'tp'=32] {'grp'}, dimensions={0} | all-to-all | bytes 1048576 | tf_op jit(solution)/shard_map/all_to_all | solution.py:128
  290.9 0.9 copy.40
  291.8 83.2 %reduce-scatter.2.cloned.1.call-done = bf16[1024,256]{1,0:T(8,128)(2,1)} async-done(((bf16[1024,8192]{1,0:T(8,128)(2,1)}), bf16[1024,256]{1,0:T(8,128)(2,1)}) %reduce-scatter.2.cloned.1.call-update) | async-done | bytes 524304 | tf_op jit(solution)/shard_map/reduce_scatter | solution.py:101
  375.0 2.0 fusion.18
  (31 shorter events, 1.2 us)
Async XLA Ops:
  7.2 150.5 %copy-start = (bf16[8192,2,32]{0,2,1:T(8,128)(2,1)S(1)}, bf16[8192,2,32]{0,2,1:T(8,128)(2,1)}, u32[]{:S(2)}) copy-start(bf16[8192,2,32]{0,2,1:T(8,128)(2,1)} %param.10) | copy-start | bytes 3145732
  7.2 150.5 %all-gather.3.cloned.1.call-start = ((), (), s32[]{:S(2)}) async-start(), calls=%async_computation.2 | async-start | bytes 17301504 | tf_op jit(solution)/shard_map/all_gather | solution.py:59
  80.0 135.9 %all-gather.5.cloned.1.call-start = ((), (), s32[]{:S(2)}) async-start(), calls=%async_computation.3 | async-start | bytes 4325376 | tf_op jit(solution)/shard_map/all_gather | solution.py:76
  157.7 11.7 %copy-start.5 = (s32[1,4]{1,0:T(1,128)S(1)}, s32[1,4]{1,0:T(1,128)}, u32[]{:S(2)}) copy-start(s32[1,4]{1,0:T(1,128)} %param.12) | copy-start | bytes 52
  169.3 205.7 %reduce-scatter.2.cloned.1.call-start = ((), (), s32[]{:S(2)}) async-start(), calls=%async_computation.4 | async-start | bytes 17301504 | tf_op jit(solution)/shard_map/reduce_scatter | solution.py:101
  260.2 0.7 copy-start.6
  263.3 10.1 %copy-start.2 = (bf16[1024,8,64]{2,0,1:T(8,128)(2,1)S(1)}, bf16[1024,8,64]{2,0,1:T(8,128)(2,1)}, u32[]{:S(2)}) copy-start(bf16[1024,8,64]{2,0,1:T(8,128)(2,1)} %get-tuple-element.8) | copy-start | bytes 3145732
  270.1 4.6 %copy-start.4 = (bf16[8,128,1,8,128]{4,3,0,1,2:T(8,128)(2,1)S(1)}, bf16[8,128,1,8,128]{4,3,0,1,2:T(8,128)(2,1)}, u32[]{:S(2)}) copy-start(bf16[8,128,1,8,128]{4,3,0,1,2:T(8,128)(2,1)} %copy.37) | copy-start | bytes 6291460
  274.8 100.2 %copy-start.3 = (bf16[1024,256]{1,0:T(8,128)(2,1)S(1)}, bf16[1024,256]{1,0:T(8,128)(2,1)}, u32[]{:S(2)}) copy-start(bf16[1024,256]{1,0:T(8,128)(2,1)} %param.7) | copy-start | bytes 1572868
  274.8 102.2 %copy-start.1 = (bf16[8192,2,32]{0,2,1:T(8,128)(2,1)S(1)}, bf16[8192,2,32]{0,2,1:T(8,128)(2,1)}, u32[]{:S(2)}) copy-start(bf16[8192,2,32]{0,2,1:T(8,128)(2,1)} %param.10) | copy-start | bytes 3145732
Sparse Core Ops, SparseCore 0:
  80.1 77.5 all-gather.2
  169.4 46.4 all-gather.4
  260.4 114.5 reduce-scatter.1
where the time goes:
time: 384 us
  waiting for transfers between devices  190 us (49%)
  blocking collectives  82.7 us (22%)
  matrix products  46 us (12%)
  local copies, waits for them, and re-layouts  32.7 us (9%)
  other arithmetic  17.7 us (5%)
  between operations  13.9 us (4%)
    reduce_scatter x1, waiting for transfers between devices, local(): lax.psum_scatter(term.astype(jnp.bfloat16), 'tp', scatter_dimension=1, ti...  83.2 us
    all_gather x1, waiting for transfers between devices, local(): piece = lax.all_gather(normalized_input, 'tp', axis=1, tiled=True)  77.6 us
    psum x1, blocking collectives, local(): total_squares = lax.psum(local_squares, 'tp')  68.7 us
    all_gather x1, waiting for transfers between devices, local(): key_value_rows = lax.all_gather(keyval_part, 'tp', axis=2, tiled=True)  29.5 us
    unnamed x21, local copies, waits for them, and re-layouts  17.3 us
    all_to_all x1, blocking collectives, local(): lax.all_to_all(payload, 'grp', split_axis=0, concat_axis=0, tiled=True)  14 us
    dot_general x1, matrix products, local(): jnp.dot(piece, flat_keyval, preferred_element_type=jnp.float32)  11.6 us
    dot_general x1, matrix products, local(): term = jnp.dot(attention_output, w_out, preferred_element_type=jnp.float32)  10.5 us
  transfers between devices with their start and end apart: 3, of which 3 were waited for; matrix products, arithmetic and copies ran while one was open for 9% of the time, Pallas kernels for 0%

commit v1 on v0

v1 whole, which is shorter than its diff:
```python
import functools
import math

import jax
import jax.numpy as jnp
from jax import lax
from jax.experimental import pallas as pl
from jax.experimental.pallas import tpu as pltpu
from jax.sharding import Mesh
from jax.sharding import PartitionSpec as P

WIDTH = 8192
HEAD = 128
BLOCK = 128
SEQ = 1024
COLS = 256
CHUNK = 512
ROPE_BASE = 500000.0
EPS = 1e-05
FILL = -1e30
SCORE_SCALE = math.log2(math.e) / math.sqrt(HEAD)
bf16 = jnp.bfloat16
f32 = jnp.float32

SHIFT = {d: [(i, (i + d) % 4) for i in range(4)] for d in (1, 2, 3)}
SWAP = [(0, 1), (1, 0)]
PAIR = [(0, 1), (1, 0), (2, 3), (3, 2)]


def shift(value, axis, distance):
    return lax.ppermute(value, axis, SHIFT[distance])


def swap(value):
    return lax.ppermute(value, "c", SWAP)


def rotate(vectors, cosine, sine):
    return vectors * cosine + pltpu.roll(vectors, HEAD // 2, 1) * sine


def scale_kernel(tokens, gain, sent):
    tok = tokens[...].astype(f32)
    sent[0:SEQ, :] = (tok * gain[...].astype(f32)).astype(bf16)
    diagonal = lax.broadcasted_iota(jnp.int32, (COLS, COLS), 0) == lax.broadcasted_iota(
        jnp.int32, (COLS, COLS), 1
    )
    rows = []
    for part in range(SEQ // COLS):
        here = tok[part * COLS : (part + 1) * COLS, :]
        column = jnp.sum(here * here, axis=1, keepdims=True)
        rows.append(jnp.sum(jnp.where(diagonal, column, 0.0), axis=0, keepdims=True))
    total = jnp.concatenate(rows + [jnp.zeros((4, COLS), f32)], axis=0)
    high = total.astype(bf16).astype(f32)
    sent[SEQ : SEQ + 16, :] = jnp.concatenate([high, total - high], axis=0).astype(bf16)


def scale_tokens(tokens, gain):
    return pl.pallas_call(
        scale_kernel,
        out_shape=jax.ShapeDtypeStruct((SEQ + 16, COLS), bf16),
        compiler_params=pltpu.CompilerParams(vmem_limit_bytes=56 << 20),
        name="scale_tokens",
    )(tokens, gain.reshape(1, COLS))


def attention_kernel(chunk, steps, per_step, lengths, x, squares, w_q, w_kv, cosine, sine, *rest):
    if chunk == 0:
        attended, keys, values, acc_q, acc_kv, acc_s, all_k, all_v = rest
    else:
        old_k, old_v, attended, keys, values, acc_q, acc_kv, acc_s, all_k, all_v = rest
    step = pl.program_id(0)

    @pl.when(step == 0)
    def _():
        acc_q[...] = jnp.zeros_like(acc_q)
        acc_kv[...] = jnp.zeros_like(acc_kv)
        acc_s[...] = jnp.zeros_like(acc_s)

    rows = jnp.concatenate([x[i] for i in range(per_step)], axis=1)
    acc_q[...] += jnp.dot(rows, w_q[...], preferred_element_type=f32)
    acc_kv[...] += jnp.dot(rows, w_kv[...], preferred_element_type=f32)
    for i in range(per_step):
        acc_s[...] += squares[i].astype(f32)

    @pl.when(step == steps - 1)
    def _():
        base = chunk * CHUNK
        diagonal = lax.broadcasted_iota(jnp.int32, (256, 256), 0) == lax.broadcasted_iota(
            jnp.int32, (256, 256), 1
        )
        for part in range(CHUNK // 256):
            row = (base + part * 256) // 256
            total = acc_s[row : row + 1, :] + acc_s[row + 8 : row + 9, :]
            factor = lax.rsqrt(total * (1.0 / WIDTH) + EPS)
            column = jnp.sum(jnp.where(diagonal, factor, 0.0), axis=1, keepdims=True)
            here = pl.ds(part * 256, 256)
            c, s = cosine[here, :], sine[here, :]
            q = acc_q[here, :] * column
            acc_q[here, :] = jnp.concatenate(
                [rotate(q[:, :HEAD], c, s), rotate(q[:, HEAD:], c, s)], axis=1
            )
            kv = (acc_kv[here, :] * column).astype(bf16)
            k = rotate(kv[:, :HEAD].astype(f32), c, s).astype(bf16)
            keys[here, :] = k
            values[here, :] = kv[:, HEAD:]
            there = pl.ds(base + part * 256, 256)
            all_k[there, :] = k
            all_v[there, :] = kv[:, HEAD:]
        if chunk > 0:
            all_k[0:base, :] = old_k[...]
            all_v[0:base, :] = old_v[...]
        for part in range(CHUNK // 256):
            first = base + part * 256
            low = max(0, first - 512)
            high = first + 256
            here = pl.ds(part * 256, 256)
            i = lax.broadcasted_iota(jnp.int32, (256, 1), 0) + first
            starts = jnp.zeros((256, 1), jnp.int32)
            end = jnp.int32(0)
            for doc in range(4):
                end = end + lengths[doc]
                starts = starts + jnp.where(i >= end, lengths[doc], 0)
            j = lax.broadcasted_iota(jnp.int32, (256, high - low), 1) + low
            allowed = (j <= i) & (j >= starts)
            k = all_k[low:high, :]
            v = all_v[low:high, :]
            outs = []
            for head in range(2):
                q = acc_q[here, head * HEAD : (head + 1) * HEAD].astype(bf16)
                scores = lax.dot_general(q, k, (((1,), (1,)), ((), ())), preferred_element_type=f32)
                scores = jnp.where(allowed, scores * SCORE_SCALE, FILL)
                peak = jnp.max(scores, axis=1, keepdims=True)
                weights = jnp.exp2(scores - peak)
                norm = jnp.sum(weights, axis=1, keepdims=True)
                out = jnp.dot(weights.astype(bf16), v, preferred_element_type=f32)
                outs.append(out / norm)
            attended[here, :] = jnp.concatenate(outs, axis=1).astype(bf16)


def attend_chunk(chunk, gathered, w_q, w_kv, cosine, sine, lengths, old):
    per_step = 4
    steps = 32 // per_step
    in_specs = [
        pl.BlockSpec((per_step, CHUNK, COLS), lambda k, n: (k, chunk, 0)),
        pl.BlockSpec((per_step, 16, COLS), lambda k, n: (k, SEQ // 16, 0)),
        pl.BlockSpec((per_step * COLS, COLS), lambda k, n: (k, 0)),
        pl.BlockSpec((per_step * COLS, COLS), lambda k, n: (k, 0)),
        pl.BlockSpec((CHUNK, HEAD), lambda k, n: (chunk, 0)),
        pl.BlockSpec((CHUNK, HEAD), lambda k, n: (chunk, 0)),
    ]
    args = [gathered, gathered, w_q, w_kv, cosine, sine]
    for part in old:
        in_specs.append(pl.BlockSpec((CHUNK, HEAD), lambda k, n: (0, 0)))
        args.append(part)
    return pl.pallas_call(
        functools.partial(attention_kernel, chunk, steps, per_step),
        grid_spec=pltpu.PrefetchScalarGridSpec(
            num_scalar_prefetch=1,
            grid=(steps,),
            in_specs=in_specs,
            out_specs=[
                pl.BlockSpec((CHUNK, COLS), lambda k, n: (0, 0)),
                pl.BlockSpec((CHUNK, HEAD), lambda k, n: (0, 0)),
                pl.BlockSpec((CHUNK, HEAD), lambda k, n: (0, 0)),
            ],
            scratch_shapes=[
                pltpu.VMEM((CHUNK, COLS), f32),
                pltpu.VMEM((CHUNK, COLS), f32),
                pltpu.VMEM((16, COLS), f32),
                pltpu.VMEM((SEQ, HEAD), bf16),
                pltpu.VMEM((SEQ, HEAD), bf16),
            ],
        ),
        out_shape=[
            jax.ShapeDtypeStruct((CHUNK, COLS), bf16),
            jax.ShapeDtypeStruct((CHUNK, HEAD), bf16),
            jax.ShapeDtypeStruct((CHUNK, HEAD), bf16),
        ],
        compiler_params=pltpu.CompilerParams(vmem_limit_bytes=56 << 20),
        cost_estimate=pl.CostEstimate(
            flops=2 * CHUNK * WIDTH * 512, bytes_accessed=24 << 20, transcendentals=1 << 20
        ),
        name="project_attend",
    )(lengths, *args)


def out_kernel(order, *refs):
    blocks, weights, outs = refs[:8], refs[8], refs[9:]
    step = pl.program_id(0)
    rows = jnp.concatenate([b[...] for b in blocks], axis=1)
    part = jnp.dot(rows, weights[0], preferred_element_type=f32).astype(bf16)
    for i in range(4):

        @pl.when(step == i)
        def _():
            outs[i][...] = part


def project_out(order, blocks, weights):
    whole = pl.BlockSpec((CHUNK, COLS), lambda i, n: (0, 0))
    return pl.pallas_call(
        out_kernel,
        grid_spec=pltpu.PrefetchScalarGridSpec(
            num_scalar_prefetch=1,
            grid=(4,),
            in_specs=[whole] * 8 + [pl.BlockSpec((1, 8 * COLS, COLS), lambda i, n: (n[i], 0, 0))],
            out_specs=[whole] * 4,
        ),
        out_shape=[jax.ShapeDtypeStruct((CHUNK, COLS), bf16)] * 4,
        compiler_params=pltpu.CompilerParams(vmem_limit_bytes=56 << 20),
        cost_estimate=pl.CostEstimate(
            flops=2 * CHUNK * 2048 * 1024, bytes_accessed=8 << 20, transcendentals=0
        ),
        name="project_out",
    )(order, *blocks, weights)


def pick_kernel(index, valid, blocks, *rest):
    outs, sems = rest[:4], rest[4]

    def copy(i):
        return pltpu.make_async_copy(blocks.at[index[i]], outs[i // 2].at[i % 2], sems.at[i])

    for i in range(8):

        @pl.when(valid[i] > 0)
        def _():
            copy(i).start()

        @pl.when(valid[i] <= 0)
        def _():
            outs[i // 2][i % 2] = jnp.zeros((2, BLOCK, HEAD), bf16)

    for i in range(8):

        @pl.when(valid[i] > 0)
        def _():
            copy(i).wait()


def pick_blocks(index, valid, blocks):
    shape = (2, 2, BLOCK, HEAD)
    return pl.pallas_call(
        pick_kernel,
        grid_spec=pltpu.PrefetchScalarGridSpec(
            num_scalar_prefetch=2,
            grid=(1,),
            in_specs=[pl.BlockSpec(memory_space=pl.ANY)],
            out_specs=[pl.BlockSpec(shape, lambda i, n, m: (0, 0, 0, 0))] * 4,
            scratch_shapes=[pltpu.SemaphoreType.DMA((8,))],
        ),
        out_shape=[jax.ShapeDtypeStruct(shape, bf16)] * 4,
        compiler_params=pltpu.CompilerParams(vmem_limit_bytes=56 << 20),
        cost_estimate=pl.CostEstimate(flops=0, bytes_accessed=2 << 20, transcendentals=0),
        name="pick_blocks",
    )(index, valid, blocks)


def spread_out_weights(w_out, g, y, c):
    def piece(d):
        column = (g * 8 + ((y + d) % 4) * 2) * COLS
        return lax.dynamic_slice(w_out, (0, column), (COLS, 2 * COLS))

    parts = [piece(0)] + [shift(piece(d), "y", d) for d in (1, 2, 3)]
    mine = jnp.stack([lax.dynamic_slice(p, (0, c * COLS), (COLS, COLS)) for p in parts])
    send = jnp.stack([lax.dynamic_slice(p, (0, (1 - c) * COLS), (COLS, COLS)) for p in parts])
    theirs = swap(send)
    local = jnp.stack([mine, theirs], axis=1).reshape(8 * COLS, COLS)
    return jnp.stack([local] + [shift(local, "g", d) for d in (1, 2, 3)])


def head_weights(kv_weight, y, c):
    own = kv_weight.transpose(1, 2, 0)
    near = lax.ppermute(own, "y", PAIR)
    both = jnp.where(y % 2 == 0, jnp.stack([own, near]), jnp.stack([near, own]))
    other = swap(both)
    cores = jnp.where(c == 0, jnp.stack([both, other], 1), jnp.stack([other, both], 1))
    return cores.transpose(4, 2, 0, 1, 3).reshape(WIDTH, 2 * HEAD)


def rope_tables(lengths):
    ends = jnp.cumsum(lengths)
    i = jnp.arange(SEQ, dtype=jnp.int32)
    passed = (i[:, None] >= ends[None, :]).astype(jnp.int32)
    positions = (i - jnp.sum(passed * lengths[None, :], axis=1)).astype(f32)
    frequency = jnp.exp(jnp.arange(HEAD // 2, dtype=f32) * (-2.0 * math.log(ROPE_BASE) / HEAD))
    angles = positions[:, None] * frequency[None, :]
    cosine, sine = jnp.cos(angles), jnp.sin(angles)
    return jnp.concatenate([cosine, cosine], 1), jnp.concatenate([-sine, sine], 1)


def store_plan(holder, g, z, y, c):
    owners = lax.dynamic_slice(holder[:, 0], (g * 64,), (64,))
    same = owners[:, None] == owners[None, :]
    before = jnp.arange(64)[None, :] < jnp.arange(64)[:, None]
    rank = jnp.sum((same & before).astype(jnp.int32), axis=1)
    slots = jnp.arange(64, dtype=jnp.int32)
    z_of, y_of, rest = slots // 16, (slots // 4) % 4, slots % 4
    block = ((y_of % 2) * 4 + rest) * 8 + z_of * 2 + y_of // 2
    owner, slot = owners[block], rank[block]
    target = (((g + jnp.arange(4)) % 4) * 32 + z * 8 + y * 2 + c).astype(jnp.int32)
    hit = (owner[None, None, :] == target[:, None, None]) & (
        slot[None, None, :] == jnp.arange(2)[None, :, None]
    )
    hit = hit.reshape(8, 64).astype(jnp.int32)
    return jnp.sum(hit * slots[None, :], axis=1), jnp.sum(hit, axis=1)


def local(tokens, norm_gain, w_query, kv_weight, w_out, doc_lengths, holder):
    g, z, y, c = (lax.axis_index(a) for a in ("g", "z", "y", "c"))
    sent = scale_tokens(tokens, norm_gain)
    gathered = lax.all_gather(sent, ("z", "y", "c"))

    lengths = doc_lengths[0]
    cosine, sine = rope_tables(lengths)
    w_kv = head_weights(kv_weight, y, c)
    w_o = spread_out_weights(w_out, g, y, c)
    order = jnp.stack([(g - z - d) % 4 for d in range(4)]).astype(jnp.int32)
    index, valid = store_plan(holder, g, z, y, c)

    gathered, w_kv, w_o, index, valid, cosine, sine = lax.optimization_barrier(
        (gathered, w_kv, w_o, index, valid, cosine, sine)
    )
    old = ()
    sums, keys, values = [], [], []
    for chunk in range(SEQ // CHUNK):
        attended, k, v = attend_chunk(chunk, gathered, w_query, w_kv, cosine, sine, lengths, old)
        old = (k, v)
        keys.append(k)
        values.append(v)
        blocks = []
        for d in range(4):
            a = attended if d == 0 else shift(attended, "y", d)
            blocks += [a, swap(a)]
        parts = project_out(order, blocks, w_o)
        total = parts[0].astype(f32)
        for d in (1, 2, 3):
            total = total + shift(parts[d], "z", d).astype(f32)
        sums.append(total)
    mixed = (tokens.astype(f32) + jnp.concatenate(sums, axis=0)).astype(bf16)

    place = (y % 2) * 2 + c
    pair = jnp.stack(
        [
            lax.dynamic_slice(jnp.concatenate(part, axis=0), (place * 256, 0), (256, HEAD))
            for part in (keys, values)
        ]
    )
    pair = pair.reshape(2, 2, BLOCK, HEAD).transpose(1, 0, 2, 3)
    everyone = lax.all_gather(pair, ("z", "y", "c")).reshape(64, 2, BLOCK, HEAD)
    picked = pick_blocks(index, valid, everyone)
    arrived = jnp.stack([picked[0]] + [shift(picked[d], "g", d) for d in (1, 2, 3)])
    stored = jnp.stack(
        [lax.dynamic_index_in_dim(arrived, (g - s) % 4, 0, keepdims=False) for s in range(4)]
    )
    return mixed, stored[None]


def solution(mesh):
    grid = Mesh(mesh.devices.reshape(4, 4, 4, 2), ("g", "z", "y", "c"))
    tp = ("z", "y", "c")
    return jax.shard_map(
        local,
        mesh=grid,
        in_specs=(
            P("g", tp),
            P(tp),
            P(None, tp),
            P(None, None, tp),
            P(tp, None),
            P("g", None),
            P(),
        ),
        out_specs=(P("g", tp), P(("g",) + tp, None, None, None, None, None)),
        check_vma=False,
    )
```

time: 384 us -> 227 us (0.59)
  waiting for transfers between devices: 190 us -> 87.3 us
  blocking collectives: 82.7 us -> 0 us
  Pallas kernels: 0 us -> 47 us
  matrix products: 46 us -> 0 us
  starting transfers between devices: 0.12 us -> 45.2 us
  local copies, waits for them, and re-layouts: 32.7 us -> 17.1 us
    all_gather x2, waiting for transfers between devices: 107 us -> 3.92 us  [the longest x1 3.9 us: local(): gathered = lax.all_gather(sent, ('z', 'y', 'c'))]
    ppermute x0 -> x32, waiting for transfers between devices: none -> 83.3 us  [the longest x21 61 us: shift(): return lax.ppermute(value, axis, SHIFT[distance])]
    reduce_scatter x1 -> x0, waiting for transfers between devices: 83.2 us -> none  [local(): lax.psum_scatter(term.astype(jnp.bfloat16), 'tp', scatter_dimension=1, ti...]
    psum x1 -> x0, blocking collectives: 68.7 us -> none  [local(): total_squares = lax.psum(local_squares, 'tp')]
    pallas_call x0 -> x6, Pallas kernels: none -> 47 us  [the longest x2 28.1 us: attend_chunk(): pl.pallas_call(functools.partial(attention_kernel, chunk, steps, per_step...]
    ppermute x0 -> x32, starting transfers between devices: none -> 45.2 us  [the longest x21 42.5 us: shift(): return lax.ppermute(value, axis, SHIFT[distance])]
    dot_general x5 -> x0, matrix products: 37.5 us -> none  [the longest x1 11.6 us: local(): jnp.dot(piece, flat_keyval, preferred_element_type=jnp.float32)]
    unnamed x21 -> x46, local copies, waits for them, and re-layouts: 17.3 us -> 1.78 us
  transfers between devices with their start and end apart: 3 -> 34, of which waited for: 3 -> 12; matrix products, arithmetic and copies ran while one was open for 9% -> 9% of each run, Pallas kernels for 0% -> 6%
where the time goes in v1:
time: 227 us; the launch traced here: 225 us
  waiting for transfers between devices  87.3 us (38%)
  Pallas kernels  47 us (21%)
  starting transfers between devices  45.2 us (20%)
  local copies, waits for them, and re-layouts  17.1 us (8%)
  between operations  14.5 us (6%)
  other arithmetic  14.4 us (6%)
    ppermute x21, waiting for transfers between devices, shift(): return lax.ppermute(value, axis, SHIFT[distance])  61 us
    ppermute x21, starting transfers between devices, shift(): return lax.ppermute(value, axis, SHIFT[distance])  42.5 us
    pallas_call x2, Pallas kernels, attend_chunk(): pl.pallas_call(functools.partial(attention_kernel, chunk, steps, per_step...  28.1 us
    ppermute x1, waiting for transfers between devices, head_weights(): near = lax.ppermute(own, 'y', PAIR)  22.3 us
    pallas_call x2, Pallas kernels, project_out(): pl.pallas_call(out_kernel, grid_spec=pltpu.PrefetchScalarGridSpec(num_sca...  14.2 us
    optimization_barrier x1, local copies, waits for them, and re-layouts, local(): lax.optimization_barrier((gathered, w_kv, w_o, index, valid, cosine, sine))  6.41 us
  transfers between devices with their start and end apart: 34, of which 12 were waited for; matrix products, arithmetic and copies ran while one was open for 9% of the time, Pallas kernels for 6%

profile of v1, /device:TPU:0, one launch (start us, length us, event | category | flops | bytes accessed | tf_op | source)
XLA Modules:
  0.0 225.5 jit_solution(4596988670752261090)
XLA Ops:
  8.5 2.1 scale_tokens.1
  12.0 1.7 collective-permute-start.2
  13.7 2.9 %collective-permute-start.3 = (bf16[256,512]{1,0:T(8,128)(2,1)S(1)}, bf16[256,512]{1,0:T(8,128)(2,1)}, u32[]{:S(2)}, u32[]{:S(2)}) collective-permute-start(bf16[256,512]{1,0:T(8,128)(2,1)S(1)} %get-tuple-element.57), channel_id=1, source_target_pairs={{0,4},{2,6},{4,0},{6,2},{1,5},{3,7},{5,1},{7,3},{8,12},{10,14},{12... | collective-permute-start | bytes 786440 | tf_op jit(solution)/shard_map/ppermute | solution.py:31
  24.8 6.4 %collective-permute-done.3 = bf16[256,512]{1,0:T(8,128)(2,1)} collective-permute-done((bf16[256,512]{1,0:T(8,128)(2,1)S(1)}, bf16[256,512]{1,0:T(8,128)(2,1)}, u32[]{:S(2)}, u32[]{:S(2)}) %collective-permute-start.3) | collective-permute-done | bytes 262176 | tf_op jit(solution)/shard_map/ppermute | solution.py:31
  32.4 1.9 fusion.1
  35.8 1.6 collective-permute-start.6
  37.4 2.8 %collective-permute-start.7 = (bf16[2048,256]{1,0:T(8,128)(2,1)S(1)}, bf16[2048,256]{1,0:T(8,128)(2,1)S(1)}, u32[]{:S(2)}, u32[]{:S(2)}) collective-permute-start(bf16[2048,256]{1,0:T(8,128)(2,1)S(1)} %bitcast.68), channel_id=1, source_target_pairs={{0,64},{32,96},{64,0},{96,32},{1,65},{33,97},{65,1},{97,33},{2,66}... | collective-permute-start | bytes 3145736 | tf_op jit(solution)/shard_map/ppermute | solution.py:31
  41.6 22.3 %collective-permute-done = bf16[2,32,8192]{2,1,0:T(8,128)(2,1)S(1)} collective-permute-done((bf16[2,32,8192]{2,1,0:T(8,128)(2,1)S(1)}, bf16[2,32,8192]{2,1,0:T(8,128)(2,1)S(1)}, u32[]{:S(2)}, u32[]{:S(2)}) %collective-permute-start) | collective-permute-done | bytes 1048608 | tf_op jit(solution)/shard_map/ppermute | solution.py:275
  65.1 21.0 %collective-permute-done.7 = bf16[2048,256]{1,0:T(8,128)(2,1)S(1)} collective-permute-done((bf16[2048,256]{1,0:T(8,128)(2,1)S(1)}, bf16[2048,256]{1,0:T(8,128)(2,1)S(1)}, u32[]{:S(2)}, u32[]{:S(2)}) %collective-permute-start.7) | collective-permute-done | bytes 1048608 | tf_op jit(solution)/shard_map/ppermute | solution.py:31
  86.2 2.3 %pad_maximum_fusion.refs_8_ = bf16[4,2048,256]{2,1,0:T(8,128)(2,1)} fusion(bf16[1,2048,256]{2,1,0:T(8,128)(2,1)S(1)} %bitcast.74, bf16[1,2048,256]{2,1,0:T(8,128)(2,1)S(1)} %bitcast.73, bf16[1,2048,256]{2,1,0:T(8,128)(2,1)S(1)} %bitcast.72, bf16[1,2048,256]{2,1,0:T(8,128)(2,1)S(1)} %bitcast.70), kind=kLoop, calls=%fused_computation.3 | loop fusion | flops 6291456 | bytes 8388608 | tf_op jit(solution)/shard_map/stack | solution.py:270
  88.4 2.4 %maximum_select_fusion = bf16[2,2,2,32,8192]{4,3,1,0,2:T(8,128)(2,1)} fusion(bf16[2,1,2,32,8192]{4,3,1,0,2:T(8,128)(2,1)S(1)} %bitcast.71, bf16[2,1,2,32,8192]{4,3,1,0,2:T(8,128)(2,1)S(1)} %copy_select_fusion, pred[]{:T(512)S(6)} %eq.76), kind=kLoop, calls=%fused_computation.2 | loop fusion | flops 6291456 | bytes 8388609 | tf_op jit(solution)/shard_map/jit(_where)/select_n | solution.py:278
  90.8 3.9 %all-gather.5.cloned.1.call-done = bf16[33280,256]{1,0:T(8,128)(2,1)} async-done(((bf16[1040,256]{1,0:T(8,128)(2,1)}), bf16[33280,256]{1,0:T(8,128)(2,1)}) %all-gather.5.cloned.1.call-update) | async-done | bytes 17039376 | tf_op jit(solution)/shard_map/all_gather | solution.py:313
  94.7 6.4 %copy.22.w_kv = bf16[8192,256]{1,0:T(8,128)(2,1)} copy(bf16[8192,256]{0,1:T(8,128)(2,1)} %bitcast.61) | data formatting | bytes 8388608 | tf_op jit(solution)/shard_map/optimization_barrier | solution.py:322
  101.2 13.6 %project_attend.2 = (bf16[512,256]{1,0:T(8,128)(2,1)}, bf16[512,128]{1,0:T(8,128)(2,1)}, bf16[512,128]{1,0:T(8,128)(2,1)}) custom-call(s32[4]{0:T(128)} %bitcast.82, bf16[32,1040,256]{2,1,0:T(8,128)(2,1)} %bitcast.57, bf16[32,1040,256]{2,1,0:T(8,128)(2,1)} %bitcast.58, bf16[8192,256]{1,0:T(8,128)(2,1)} %w_q.3, bf16[8192,256]{1,0:T(8,128)(2,1)} %copy.22.w_kv, ...), custom_call_target="tpu_custom_call" | custom-call | flops 4294967296 | bytes 25165824 | tf_op jit(solution)/shard_map/project_attend/pallas_call | solution.py:156
  114.8 14.5 %project_attend.3 = (bf16[512,256]{1,0:T(8,128)(2,1)}, bf16[512,128]{1,0:T(8,128)(2,1)}, bf16[512,128]{1,0:T(8,128)(2,1)}) custom-call(s32[4]{0:T(128)} %bitcast.83, bf16[32,1040,256]{2,1,0:T(8,128)(2,1)} %bitcast.59, bf16[32,1040,256]{2,1,0:T(8,128)(2,1)} %bitcast.60, bf16[8192,256]{1,0:T(8,128)(2,1)} %w_q.3, bf16[8192,256]{1,0:T(8,128)(2,1)} %copy.22.w_kv, ...), custom_call_target="tpu_custom_call" | custom-call | flops 4294967296 | bytes 25165824 | tf_op jit(solution)/shard_map/project_attend/pallas_call | solution.py:156
  131.9 2.8 %collective-permute-start.12 = (bf16[512,256]{1,0:T(8,128)(2,1)S(1)}, bf16[512,256]{1,0:T(8,128)(2,1)S(1)}, u32[]{:S(2)}, u32[]{:S(2)}) collective-permute-start(bf16[512,256]{1,0:T(8,128)(2,1)S(1)} %copy-done.12), channel_id=1, source_target_pairs={{0,4},{2,6},{4,0},{6,2},{1,5},{3,7},{5,1},{7,3},{8,12},{10,14},{12... | collective-permute-start | bytes 786440 | tf_op jit(solution)/shard_map/ppermute | solution.py:31
  136.8 3.3 %collective-permute-done.10.refs_2_ = bf16[512,256]{1,0:T(8,128)(2,1)S(1)} collective-permute-done((bf16[512,256]{1,0:T(8,128)(2,1)S(1)}, bf16[512,256]{1,0:T(8,128)(2,1)S(1)}, u32[]{:S(2)}, u32[]{:S(2)}) %collective-permute-start.10) | collective-permute-done | bytes 262176 | tf_op jit(solution)/shard_map/ppermute | solution.py:31
  140.1 8.2 %collective-permute-start.22 = (bf16[512,256]{1,0:T(8,128)(2,1)}, bf16[512,256]{1,0:T(8,128)(2,1)S(1)}, u32[]{:S(2)}, u32[]{:S(2)}) collective-permute-start(bf16[512,256]{1,0:T(8,128)(2,1)} %get-tuple-element.39.refs_0_), channel_id=1, source_target_pairs={{0,4},{2,6},{4,0},{6,2},{1,5},{3,7},{5,1},{7,3},{8,12},{10,14},{12... | collective-permute-start | bytes 786440 | tf_op jit(solution)/shard_map/ppermute | solution.py:31
  148.9 4.5 %collective-permute-done.20.refs_2_ = bf16[512,256]{1,0:T(8,128)(2,1)S(1)} collective-permute-done((bf16[512,256]{1,0:T(8,128)(2,1)}, bf16[512,256]{1,0:T(8,128)(2,1)S(1)}, u32[]{:S(2)}, u32[]{:S(2)}) %collective-permute-start.20) | collective-permute-done | bytes 262176 | tf_op jit(solution)/shard_map/ppermute | solution.py:31
  153.4 6.9 %collective-permute-done.22.refs_4_ = bf16[512,256]{1,0:T(8,128)(2,1)S(1)} collective-permute-done((bf16[512,256]{1,0:T(8,128)(2,1)}, bf16[512,256]{1,0:T(8,128)(2,1)S(1)}, u32[]{:S(2)}, u32[]{:S(2)}) %collective-permute-start.22) | collective-permute-done | bytes 262176 | tf_op jit(solution)/shard_map/ppermute | solution.py:31
  162.2 7.1 %project_out.2 = (bf16[512,256]{1,0:T(8,128)(2,1)}, bf16[512,256]{1,0:T(8,128)(2,1)}, bf16[512,256]{1,0:T(8,128)(2,1)}, bf16[512,256]{1,0:T(8,128)(2,1)}) custom-call(s32[4]{0:T(128)} %pad_add_fusion.order, bf16[512,256]{1,0:T(8,128)(2,1)} %get-tuple-element.31.refs_0_, bf16[512,256]{1,0:T(8,128)(2,1)} %copy-done.19, bf16[512,256]{1,0:T(8,128)(2,1)} %copy-done.15, ...), custom_call_target="tpu_custom_call" | custom-call | flops 2147483648 | bytes 8388608 | tf_op jit(solution)/shard_map/project_out/pallas_call | solution.py:202
  169.3 2.1 collective-permute-start.16
  171.4 3.6 %collective-permute-start.17 = (bf16[512,256]{1,0:T(8,128)(2,1)}, bf16[512,256]{1,0:T(8,128)(2,1)S(1)}, u32[]{:S(2)}, u32[]{:S(2)}) collective-permute-start(bf16[512,256]{1,0:T(8,128)(2,1)} %get-tuple-element.35), channel_id=1, source_target_pairs={{0,16},{8,24},{16,0},{24,8},{1,17},{9,25},{17,1},{25,9},{2,18},{10... | collective-permute-start | bytes 786440 | tf_op jit(solution)/shard_map/ppermute | solution.py:31
  177.4 7.1 %project_out.3 = (bf16[512,256]{1,0:T(8,128)(2,1)}, bf16[512,256]{1,0:T(8,128)(2,1)}, bf16[512,256]{1,0:T(8,128)(2,1)}, bf16[512,256]{1,0:T(8,128)(2,1)}) custom-call(s32[4]{0:T(128)} %pad_add_fusion.order, bf16[512,256]{1,0:T(8,128)(2,1)} %get-tuple-element.39.refs_0_, bf16[512,256]{1,0:T(8,128)(2,1)} %copy-done.13, bf16[512,256]{1,0:T(8,128)(2,1)} %copy-done.9, ...), custom_call_target="tpu_custom_call" | custom-call | flops 2147483648 | bytes 8388608 | tf_op jit(solution)/shard_map/project_out/pallas_call | solution.py:202
  186.2 2.1 collective-permute-start.28
  188.3 4.5 %collective-permute-done.17 = bf16[512,256]{1,0:T(8,128)(2,1)S(1)} collective-permute-done((bf16[512,256]{1,0:T(8,128)(2,1)}, bf16[512,256]{1,0:T(8,128)(2,1)S(1)}, u32[]{:S(2)}, u32[]{:S(2)}) %collective-permute-start.17) | collective-permute-done | bytes 262176 | tf_op jit(solution)/shard_map/ppermute | solution.py:31
  192.9 5.4 %collective-permute-done.26 = bf16[512,256]{1,0:T(8,128)(2,1)S(1)} collective-permute-done((bf16[512,256]{1,0:T(8,128)(2,1)}, bf16[512,256]{1,0:T(8,128)(2,1)S(1)}, u32[]{:S(2)}, u32[]{:S(2)}) %collective-permute-start.26) | collective-permute-done | bytes 262176 | tf_op jit(solution)/shard_map/ppermute | solution.py:31
  198.3 5.2 %collective-permute-done.27 = bf16[512,256]{1,0:T(8,128)(2,1)S(1)} collective-permute-done((bf16[512,256]{1,0:T(8,128)(2,1)}, bf16[512,256]{1,0:T(8,128)(2,1)S(1)}, u32[]{:S(2)}, u32[]{:S(2)}) %collective-permute-start.27) | collective-permute-done | bytes 262176 | tf_op jit(solution)/shard_map/ppermute | solution.py:31
  204.6 2.5 %pick_blocks.1 = (bf16[2,2,128,128]{3,2,1,0:T(8,128)(2,1)}, bf16[2,2,128,128]{3,2,1,0:T(8,128)(2,1)}, bf16[2,2,128,128]{3,2,1,0:T(8,128)(2,1)}, bf16[2,2,128,128]{3,2,1,0:T(8,128)(2,1)}) custom-call(s32[8]{0:T(128)} %reduce_sum.42.index, s32[8]{0:T(128)} %reduce_sum.44.valid, bf16[64,2,128,128]{3,2,1,0:T(8,128)(2,1)} %all-gather.7.cloned.1.call-done.blocks), custom_call_target="tpu_custom_call" | custom-call | bytes 2097152 | tf_op jit(solution)/shard_map/pick_blocks/pallas_call | solution.py:244
  207.2 1.6 collective-permute-start.29
  208.7 2.8 %collective-permute-start.30 = (bf16[2,2,128,128]{3,2,1,0:T(8,128)(2,1)}, bf16[2,2,128,128]{3,2,1,0:T(8,128)(2,1)S(1)}, u32[]{:S(2)}, u32[]{:S(2)}) collective-permute-start(bf16[2,2,128,128]{3,2,1,0:T(8,128)(2,1)} %get-tuple-element.50), channel_id=1, source_target_pairs={{0,64},{32,96},{64,0},{96,32},{1,65},{33,97},{65,1},{97,33},{2,66}... | collective-permute-start | bytes 393224 | tf_op jit(solution)/shard_map/ppermute | solution.py:31
  214.1 3.6 %collective-permute-done.30 = bf16[2,2,128,128]{3,2,1,0:T(8,128)(2,1)S(1)} collective-permute-done((bf16[2,2,128,128]{3,2,1,0:T(8,128)(2,1)}, bf16[2,2,128,128]{3,2,1,0:T(8,128)(2,1)S(1)}, u32[]{:S(2)}, u32[]{:S(2)}) %collective-permute-start.30) | collective-permute-done | bytes 131104 | tf_op jit(solution)/shard_map/ppermute | solution.py:31
  (135 shorter events, 31.9 us)
Async XLA Ops:
  7.2 87.6 %all-gather.5.cloned.1.call-start = ((), (), s32[]{:S(2)}) async-start(), calls=%async_computation | async-start | bytes 17571840 | tf_op jit(solution)/shard_map/all_gather | solution.py:313
  10.7 193.9 %all-gather.7.cloned.1.call-start = ((), (), s32[]{:S(2)}) async-start(), calls=%async_computation.1 | async-start | bytes 4325376 | tf_op jit(solution)/shard_map/all_gather | solution.py:351
  12.0 11.8 %collective-permute-start.2 = (bf16[256,512]{1,0:T(8,128)(2,1)S(1)}, bf16[256,512]{1,0:T(8,128)(2,1)}, u32[]{:S(2)}, u32[]{:S(2)}) collective-permute-start(bf16[256,512]{1,0:T(8,128)(2,1)S(1)} %get-tuple-element.56), channel_id=1, source_target_pairs={{0,2},{2,4},{4,6},{6,0},{1,3},{3,5},{5,7},{7,1},{8,10},{10,12},{12... | collective-permute-start | bytes 786440 | tf_op jit(solution)/shard_map/ppermute | solution.py:31
  13.7 17.5 %collective-permute-start.3 = (bf16[256,512]{1,0:T(8,128)(2,1)S(1)}, bf16[256,512]{1,0:T(8,128)(2,1)}, u32[]{:S(2)}, u32[]{:S(2)}) collective-permute-start(bf16[256,512]{1,0:T(8,128)(2,1)S(1)} %get-tuple-element.57), channel_id=1, source_target_pairs={{0,4},{2,6},{4,0},{6,2},{1,5},{3,7},{5,1},{7,3},{8,12},{10,14},{12... | collective-permute-start | bytes 786440 | tf_op jit(solution)/shard_map/ppermute | solution.py:31
  16.6 15.6 %collective-permute-start.4 = (bf16[256,512]{1,0:T(8,128)(2,1)S(1)}, bf16[256,512]{1,0:T(8,128)(2,1)S(1)}, u32[]{:S(2)}, u32[]{:S(2)}) collective-permute-start(bf16[256,512]{1,0:T(8,128)(2,1)S(1)} %get-tuple-element.58), channel_id=1, source_target_pairs={{0,6},{2,0},{4,2},{6,4},{1,7},{3,1},{5,3},{7,5},{8,14},{10,8},{12,... | collective-permute-start | bytes 786440 | tf_op jit(solution)/shard_map/ppermute | solution.py:31
  18.0 45.9 %collective-permute-start = (bf16[2,32,8192]{2,1,0:T(8,128)(2,1)S(1)}, bf16[2,32,8192]{2,1,0:T(8,128)(2,1)S(1)}, u32[]{:S(2)}, u32[]{:S(2)}) collective-permute-start(bf16[2,32,8192]{2,1,0:T(8,128)(2,1)S(1)} %bitcast.62), channel_id=1, source_target_pairs={{0,2},{2,0},{4,6},{6,4},{1,3},{3,1},{5,7},{7,5},{8,10},{10,8},{12,... | collective-permute-start | bytes 3145736 | tf_op jit(solution)/shard_map/ppermute | solution.py:275
  35.8 29.3 %collective-permute-start.6 = (bf16[2048,256]{1,0:T(8,128)(2,1)S(1)}, bf16[2048,256]{1,0:T(8,128)(2,1)S(1)}, u32[]{:S(2)}, u32[]{:S(2)}) collective-permute-start(bf16[2048,256]{1,0:T(8,128)(2,1)S(1)} %bitcast.67), channel_id=1, source_target_pairs={{0,32},{32,64},{64,96},{96,0},{1,33},{33,65},{65,97},{97,1},{2,34}... | collective-permute-start | bytes 3145736 | tf_op jit(solution)/shard_map/ppermute | solution.py:31
  37.4 48.8 %collective-permute-start.7 = (bf16[2048,256]{1,0:T(8,128)(2,1)S(1)}, bf16[2048,256]{1,0:T(8,128)(2,1)S(1)}, u32[]{:S(2)}, u32[]{:S(2)}) collective-permute-start(bf16[2048,256]{1,0:T(8,128)(2,1)S(1)} %bitcast.68), channel_id=1, source_target_pairs={{0,64},{32,96},{64,0},{96,32},{1,65},{33,97},{65,1},{97,33},{2,66}... | collective-permute-start | bytes 3145736 | tf_op jit(solution)/shard_map/ppermute | solution.py:31
  40.2 46.0 %collective-permute-start.8 = (bf16[2048,256]{1,0:T(8,128)(2,1)S(1)}, bf16[2048,256]{1,0:T(8,128)(2,1)S(1)}, u32[]{:S(2)}, u32[]{:S(2)}) collective-permute-start(bf16[2048,256]{1,0:T(8,128)(2,1)S(1)} %bitcast.69), channel_id=1, source_target_pairs={{0,96},{32,0},{64,32},{96,64},{1,97},{33,1},{65,33},{97,65},{2,98}... | collective-permute-start | bytes 3145736 | tf_op jit(solution)/shard_map/ppermute | solution.py:31
  64.2 24.2 %collective-permute-start.1 = (bf16[2,2,32,8192]{3,2,0,1:T(8,128)(2,1)S(1)}, bf16[2,2,32,8192]{3,2,0,1:T(8,128)(2,1)S(1)}, u32[]{:S(2)}, u32[]{:S(2)}) collective-permute-start(bf16[2,2,32,8192]{3,2,0,1:T(8,128)(2,1)S(1)} %maximum_select_fusion.1), channel_id=1, source_target_pairs={{0,1},{1,0},{2,3},{3,2},{4,5},{5,4},{6,7},{7,6},{8,9},{9,8},{10,11... | collective-permute-start | bytes 6291464 | tf_op jit(solution)/shard_map/ppermute | solution.py:35
  130.3 9.7 %collective-permute-start.10 = (bf16[512,256]{1,0:T(8,128)(2,1)S(1)}, bf16[512,256]{1,0:T(8,128)(2,1)S(1)}, u32[]{:S(2)}, u32[]{:S(2)}) collective-permute-start(bf16[512,256]{1,0:T(8,128)(2,1)S(1)} %copy-done.12), channel_id=1, source_target_pairs={{0,2},{2,4},{4,6},{6,0},{1,3},{3,5},{5,7},{7,1},{8,10},{10,12},{12... | collective-permute-start | bytes 786440 | tf_op jit(solution)/shard_map/ppermute | solution.py:31
  131.9 16.4 %collective-permute-start.12 = (bf16[512,256]{1,0:T(8,128)(2,1)S(1)}, bf16[512,256]{1,0:T(8,128)(2,1)S(1)}, u32[]{:S(2)}, u32[]{:S(2)}) collective-permute-start(bf16[512,256]{1,0:T(8,128)(2,1)S(1)} %copy-done.12), channel_id=1, source_target_pairs={{0,4},{2,6},{4,0},{6,2},{1,5},{3,7},{5,1},{7,3},{8,12},{10,14},{12... | collective-permute-start | bytes 786440 | tf_op jit(solution)/shard_map/ppermute | solution.py:31
  134.7 13.5 %collective-permute-start.14 = (bf16[512,256]{1,0:T(8,128)(2,1)S(1)}, bf16[512,256]{1,0:T(8,128)(2,1)S(1)}, u32[]{:S(2)}, u32[]{:S(2)}) collective-permute-start(bf16[512,256]{1,0:T(8,128)(2,1)S(1)} %copy-done.12), channel_id=1, source_target_pairs={{0,6},{2,0},{4,2},{6,4},{1,7},{3,1},{5,3},{7,5},{8,14},{10,8},{12,... | collective-permute-start | bytes 786440 | tf_op jit(solution)/shard_map/ppermute | solution.py:31
  136.1 12.3 %collective-permute-start.9 = (bf16[512,256]{1,0:T(8,128)(2,1)S(1)}, bf16[512,256]{1,0:T(8,128)(2,1)S(1)}, u32[]{:S(2)}, u32[]{:S(2)}) collective-permute-start(bf16[512,256]{1,0:T(8,128)(2,1)S(1)} %copy-done.12), channel_id=1, source_target_pairs={{0,1},{1,0},{2,3},{3,2},{4,5},{5,4},{6,7},{7,6},{8,9},{9,8},{10,11... | collective-permute-start | bytes 786440 | tf_op jit(solution)/shard_map/ppermute | solution.py:35
  136.1 17.3 %collective-permute-start.20 = (bf16[512,256]{1,0:T(8,128)(2,1)}, bf16[512,256]{1,0:T(8,128)(2,1)S(1)}, u32[]{:S(2)}, u32[]{:S(2)}) collective-permute-start(bf16[512,256]{1,0:T(8,128)(2,1)} %get-tuple-element.39.refs_0_), channel_id=1, source_target_pairs={{0,2},{2,4},{4,6},{6,0},{1,3},{3,5},{5,7},{7,1},{8,10},{10,12},{12... | collective-permute-start | bytes 786440 | tf_op jit(solution)/shard_map/ppermute | solution.py:31
  140.1 20.2 %collective-permute-start.22 = (bf16[512,256]{1,0:T(8,128)(2,1)}, bf16[512,256]{1,0:T(8,128)(2,1)S(1)}, u32[]{:S(2)}, u32[]{:S(2)}) collective-permute-start(bf16[512,256]{1,0:T(8,128)(2,1)} %get-tuple-element.39.refs_0_), channel_id=1, source_target_pairs={{0,4},{2,6},{4,0},{6,2},{1,5},{3,7},{5,1},{7,3},{8,12},{10,14},{12... | collective-permute-start | bytes 786440 | tf_op jit(solution)/shard_map/ppermute | solution.py:31
  148.2 12.0 %collective-permute-start.24 = (bf16[512,256]{1,0:T(8,128)(2,1)}, bf16[512,256]{1,0:T(8,128)(2,1)S(1)}, u32[]{:S(2)}, u32[]{:S(2)}) collective-permute-start(bf16[512,256]{1,0:T(8,128)(2,1)} %get-tuple-element.39.refs_0_), channel_id=1, source_target_pairs={{0,6},{2,0},{4,2},{6,4},{1,7},{3,1},{5,3},{7,5},{8,14},{10,8},{12,... | collective-permute-start | bytes 786440 | tf_op jit(solution)/shard_map/ppermute | solution.py:31
  148.3 13.1 %collective-permute-start.11 = (bf16[512,256]{1,0:T(8,128)(2,1)S(1)}, bf16[512,256]{1,0:T(8,128)(2,1)S(1)}, u32[]{:S(2)}, u32[]{:S(2)}) collective-permute-start(bf16[512,256]{1,0:T(8,128)(2,1)S(1)} %collective-permute-done.10.refs_2_), channel_id=1, source_target_pairs={{0,1},{1,0},{2,3},{3,2},{4,5},{5,4},{6,7},{7,6},{8,9},{9,8},{10,11... | collective-permute-start | bytes 786440 | tf_op jit(solution)/shard_map/ppermute | solution.py:35
  148.4 13.1 %collective-permute-start.13 = (bf16[512,256]{1,0:T(8,128)(2,1)S(1)}, bf16[512,256]{1,0:T(8,128)(2,1)S(1)}, u32[]{:S(2)}, u32[]{:S(2)}) collective-permute-start(bf16[512,256]{1,0:T(8,128)(2,1)S(1)} %collective-permute-done.12.refs_4_), channel_id=1, source_target_pairs={{0,1},{1,0},{2,3},{3,2},{4,5},{5,4},{6,7},{7,6},{8,9},{9,8},{10,11... | collective-permute-start | bytes 786440 | tf_op jit(solution)/shard_map/ppermute | solution.py:35
  153.4 8.5 %collective-permute-start.15 = (bf16[512,256]{1,0:T(8,128)(2,1)S(1)}, bf16[512,256]{1,0:T(8,128)(2,1)}, u32[]{:S(2)}, u32[]{:S(2)}) collective-permute-start(bf16[512,256]{1,0:T(8,128)(2,1)S(1)} %collective-permute-done.14.refs_6_), channel_id=1, source_target_pairs={{0,1},{1,0},{2,3},{3,2},{4,5},{5,4},{6,7},{7,6},{8,9},{9,8},{10,11... | collective-permute-start | bytes 786440 | tf_op jit(solution)/shard_map/ppermute | solution.py:35
  160.2 11.1 %collective-permute-start.19 = (bf16[512,256]{1,0:T(8,128)(2,1)}, bf16[512,256]{1,0:T(8,128)(2,1)S(1)}, u32[]{:S(2)}, u32[]{:S(2)}) collective-permute-start(bf16[512,256]{1,0:T(8,128)(2,1)} %get-tuple-element.39.refs_0_), channel_id=1, source_target_pairs={{0,1},{1,0},{2,3},{3,2},{4,5},{5,4},{6,7},{7,6},{8,9},{9,8},{10,11... | collective-permute-start | bytes 786440 | tf_op jit(solution)/shard_map/ppermute | solution.py:35
  160.3 14.7 %collective-permute-start.21 = (bf16[512,256]{1,0:T(8,128)(2,1)S(1)}, bf16[512,256]{1,0:T(8,128)(2,1)S(1)}, u32[]{:S(2)}, u32[]{:S(2)}) collective-permute-start(bf16[512,256]{1,0:T(8,128)(2,1)S(1)} %collective-permute-done.20.refs_2_), channel_id=1, source_target_pairs={{0,1},{1,0},{2,3},{3,2},{4,5},{5,4},{6,7},{7,6},{8,9},{9,8},{10,11... | collective-permute-start | bytes 786440 | tf_op jit(solution)/shard_map/ppermute | solution.py:35
  161.4 14.6 %collective-permute-start.23 = (bf16[512,256]{1,0:T(8,128)(2,1)S(1)}, bf16[512,256]{1,0:T(8,128)(2,1)S(1)}, u32[]{:S(2)}, u32[]{:S(2)}) collective-permute-start(bf16[512,256]{1,0:T(8,128)(2,1)S(1)} %collective-permute-done.22.refs_4_), channel_id=1, source_target_pairs={{0,1},{1,0},{2,3},{3,2},{4,5},{5,4},{6,7},{7,6},{8,9},{9,8},{10,11... | collective-permute-start | bytes 786440 | tf_op jit(solution)/shard_map/ppermute | solution.py:35
  161.5 14.5 %collective-permute-start.25 = (bf16[512,256]{1,0:T(8,128)(2,1)S(1)}, bf16[512,256]{1,0:T(8,128)(2,1)S(1)}, u32[]{:S(2)}, u32[]{:S(2)}) collective-permute-start(bf16[512,256]{1,0:T(8,128)(2,1)S(1)} %collective-permute-done.24.refs_6_), channel_id=1, source_target_pairs={{0,1},{1,0},{2,3},{3,2},{4,5},{5,4},{6,7},{7,6},{8,9},{9,8},{10,11... | collective-permute-start | bytes 786440 | tf_op jit(solution)/shard_map/ppermute | solution.py:35
  169.3 16.9 %collective-permute-start.16 = (bf16[512,256]{1,0:T(8,128)(2,1)}, bf16[512,256]{1,0:T(8,128)(2,1)S(1)}, u32[]{:S(2)}, u32[]{:S(2)}) collective-permute-start(bf16[512,256]{1,0:T(8,128)(2,1)} %get-tuple-element.34), channel_id=1, source_target_pairs={{0,8},{8,16},{16,24},{24,0},{1,9},{9,17},{17,25},{25,1},{2,10},{10... | collective-permute-start | bytes 786440 | tf_op jit(solution)/shard_map/ppermute | solution.py:31
  171.4 21.4 %collective-permute-start.17 = (bf16[512,256]{1,0:T(8,128)(2,1)}, bf16[512,256]{1,0:T(8,128)(2,1)S(1)}, u32[]{:S(2)}, u32[]{:S(2)}) collective-permute-start(bf16[512,256]{1,0:T(8,128)(2,1)} %get-tuple-element.35), channel_id=1, source_target_pairs={{0,16},{8,24},{16,0},{24,8},{1,17},{9,25},{17,1},{25,9},{2,18},{10... | collective-permute-start | bytes 786440 | tf_op jit(solution)/shard_map/ppermute | solution.py:31
  175.0 17.8 %collective-permute-start.18 = (bf16[512,256]{1,0:T(8,128)(2,1)}, bf16[512,256]{1,0:T(8,128)(2,1)S(1)}, u32[]{:S(2)}, u32[]{:S(2)}) collective-permute-start(bf16[512,256]{1,0:T(8,128)(2,1)} %get-tuple-element.36), channel_id=1, source_target_pairs={{0,24},{8,0},{16,8},{24,16},{1,25},{9,1},{17,9},{25,17},{2,26},{10... | collective-permute-start | bytes 786440 | tf_op jit(solution)/shard_map/ppermute | solution.py:31
  184.5 13.8 %collective-permute-start.26 = (bf16[512,256]{1,0:T(8,128)(2,1)}, bf16[512,256]{1,0:T(8,128)(2,1)S(1)}, u32[]{:S(2)}, u32[]{:S(2)}) collective-permute-start(bf16[512,256]{1,0:T(8,128)(2,1)} %get-tuple-element.41), channel_id=1, source_target_pairs={{0,8},{8,16},{16,24},{24,0},{1,9},{9,17},{17,25},{25,1},{2,10},{10... | collective-permute-start | bytes 786440 | tf_op jit(solution)/shard_map/ppermute | solution.py:31
  185.5 18.0 %collective-permute-start.27 = (bf16[512,256]{1,0:T(8,128)(2,1)}, bf16[512,256]{1,0:T(8,128)(2,1)S(1)}, u32[]{:S(2)}, u32[]{:S(2)}) collective-permute-start(bf16[512,256]{1,0:T(8,128)(2,1)} %get-tuple-element.42), channel_id=1, source_target_pairs={{0,16},{8,24},{16,0},{24,8},{1,17},{9,25},{17,1},{25,9},{2,18},{10... | collective-permute-start | bytes 786440 | tf_op jit(solution)/shard_map/ppermute | solution.py:31
  186.2 17.3 %collective-permute-start.28 = (bf16[512,256]{1,0:T(8,128)(2,1)}, bf16[512,256]{1,0:T(8,128)(2,1)S(1)}, u32[]{:S(2)}, u32[]{:S(2)}) collective-permute-start(bf16[512,256]{1,0:T(8,128)(2,1)} %get-tuple-element.43), channel_id=1, source_target_pairs={{0,24},{8,0},{16,8},{24,16},{1,25},{9,1},{17,9},{25,17},{2,26},{10... | collective-permute-start | bytes 786440 | tf_op jit(solution)/shard_map/ppermute | solution.py:31
  207.2 6.9 %collective-permute-start.29 = (bf16[2,2,128,128]{3,2,1,0:T(8,128)(2,1)}, bf16[2,2,128,128]{3,2,1,0:T(8,128)(2,1)S(1)}, u32[]{:S(2)}, u32[]{:S(2)}) collective-permute-start(bf16[2,2,128,128]{3,2,1,0:T(8,128)(2,1)} %get-tuple-element.49), channel_id=1, source_target_pairs={{0,32},{32,64},{64,96},{96,0},{1,33},{33,65},{65,97},{97,1},{2,34}... | collective-permute-start | bytes 393224 | tf_op jit(solution)/shard_map/ppermute | solution.py:31
  208.7 8.9 %collective-permute-start.30 = (bf16[2,2,128,128]{3,2,1,0:T(8,128)(2,1)}, bf16[2,2,128,128]{3,2,1,0:T(8,128)(2,1)S(1)}, u32[]{:S(2)}, u32[]{:S(2)}) collective-permute-start(bf16[2,2,128,128]{3,2,1,0:T(8,128)(2,1)} %get-tuple-element.50), channel_id=1, source_target_pairs={{0,64},{32,96},{64,0},{96,32},{1,65},{33,97},{65,1},{97,33},{2,66}... | collective-permute-start | bytes 393224 | tf_op jit(solution)/shard_map/ppermute | solution.py:31
  (25 other events, 235.0 us)
Sparse Core Ops, SparseCore 0:
  10.8 83.8 all-gather.4
  130.4 61.4 all-gather.6

commit v2 on v1

v2 whole, which is shorter than its diff:
```python
import functools
import math

import jax
import jax.numpy as jnp
from jax import lax
from jax.experimental import pallas as pl
from jax.experimental.pallas import tpu as pltpu
from jax.sharding import Mesh
from jax.sharding import PartitionSpec as P

WIDTH = 8192
HEAD = 128
BLOCK = 128
SEQ = 1024
COLS = 256
CHUNK = 512
ROPE_BASE = 500000.0
EPS = 1e-05
FILL = -1e30
SCORE_SCALE = math.log2(math.e) / math.sqrt(HEAD)
bf16 = jnp.bfloat16
f32 = jnp.float32

SHIFT = {d: [(i, (i + d) % 4) for i in range(4)] for d in (1, 2, 3)}
SWAP = [(0, 1), (1, 0)]
PAIR = [(0, 1), (1, 0), (2, 3), (3, 2)]


def shift(value, axis, distance):
    return lax.ppermute(value, axis, SHIFT[distance])


def swap(value):
    return lax.ppermute(value, "c", SWAP)


def rotate(vectors, cosine, sine):
    return vectors * cosine + pltpu.roll(vectors, HEAD // 2, 1) * sine


def scale_kernel(tokens, gain, sent):
    tok = tokens[...].astype(f32)
    sent[0:SEQ, :] = (tok * gain[...].astype(f32).reshape(1, COLS)).astype(bf16)
    diagonal = lax.broadcasted_iota(jnp.int32, (COLS, COLS), 0) == lax.broadcasted_iota(
        jnp.int32, (COLS, COLS), 1
    )
    rows = []
    for part in range(SEQ // COLS):
        here = tok[part * COLS : (part + 1) * COLS, :]
        column = jnp.sum(here * here, axis=1, keepdims=True)
        rows.append(jnp.sum(jnp.where(diagonal, column, 0.0), axis=0, keepdims=True))
    total = jnp.concatenate(rows + [jnp.zeros((4, COLS), f32)], axis=0)
    high = total.astype(bf16).astype(f32)
    sent[SEQ : SEQ + 16, :] = jnp.concatenate([high, total - high], axis=0).astype(bf16)


def scale_tokens(tokens, gain):
    return pl.pallas_call(
        scale_kernel,
        out_shape=jax.ShapeDtypeStruct((SEQ + 16, COLS), bf16),
        compiler_params=pltpu.CompilerParams(vmem_limit_bytes=56 << 20),
        name="scale_tokens",
    )(tokens, gain)


def row_factors(squares, part):
    diagonal = lax.broadcasted_iota(jnp.int32, (COLS, COLS), 0) == lax.broadcasted_iota(
        jnp.int32, (COLS, COLS), 1
    )
    every = jnp.sum(squares[...].astype(f32), axis=0)
    every = every[:8, :] + every[8:, :]
    mine = lax.broadcasted_iota(jnp.int32, (8, COLS), 0) == part
    total = jnp.sum(jnp.where(mine, every, 0.0), axis=0, keepdims=True)
    factor = lax.rsqrt(total * (1.0 / WIDTH) + EPS)
    return jnp.sum(jnp.where(diagonal, factor, 0.0), axis=1, keepdims=True)


def key_value_kernel(steps, per_step, place, x, squares, weights, cosine, sine, out, acc):
    step = pl.program_id(0)

    @pl.when(step == 0)
    def _():
        acc[...] = jnp.zeros_like(acc)

    rows = jnp.concatenate([x[i] for i in range(per_step)], axis=1)
    acc[...] += lax.dot_general(
        rows, weights[...], (((1,), (1,)), ((), ())), preferred_element_type=f32
    )

    @pl.when(step == steps - 1)
    def _():
        kv = (acc[...] * row_factors(squares, place[0])).astype(bf16)
        keys = rotate(kv[:, :HEAD].astype(f32), cosine[...], sine[...]).astype(bf16)
        for i in range(2):
            out[i, 0] = keys[i * BLOCK : (i + 1) * BLOCK, :]
            out[i, 1] = kv[i * BLOCK : (i + 1) * BLOCK, HEAD:]


def project_key_value(place, gathered, weights, cosine, sine):
    per_step = 8
    steps = 32 // per_step
    return pl.pallas_call(
        functools.partial(key_value_kernel, steps, per_step),
        grid_spec=pltpu.PrefetchScalarGridSpec(
            num_scalar_prefetch=1,
            grid=(steps,),
            in_specs=[
                pl.BlockSpec((per_step, COLS, COLS), lambda k, n: (k, n[0], 0)),
                pl.BlockSpec((32, 16, COLS), lambda k, n: (0, SEQ // 16, 0)),
                pl.BlockSpec((2 * HEAD, per_step * COLS), lambda k, n: (0, k)),
                pl.BlockSpec((COLS, HEAD), lambda k, n: (n[0], 0)),
                pl.BlockSpec((COLS, HEAD), lambda k, n: (n[0], 0)),
            ],
            out_specs=pl.BlockSpec((2, 2, BLOCK, HEAD), lambda k, n: (0, 0, 0, 0)),
            scratch_shapes=[pltpu.VMEM((COLS, 2 * HEAD), f32)],
        ),
        out_shape=jax.ShapeDtypeStruct((2, 2, BLOCK, HEAD), bf16),
        compiler_params=pltpu.CompilerParams(vmem_limit_bytes=56 << 20),
        cost_estimate=pl.CostEstimate(
            flops=2 * COLS * WIDTH * 256, bytes_accessed=8 << 20, transcendentals=0
        ),
        name="project_key_value",
    )(place, gathered, gathered, weights, cosine, sine)


def query_kernel(steps, per_step, x, squares, weights, cosine, sine, first, second, acc):
    step = pl.program_id(0)

    @pl.when(step == 0)
    def _():
        acc[...] = jnp.zeros_like(acc)

    rows = jnp.concatenate([x[i] for i in range(per_step)], axis=1)
    acc[...] += jnp.dot(rows, weights[...], preferred_element_type=f32)

    @pl.when(step == steps - 1)
    def _():
        for part in range(SEQ // COLS):
            here = pl.ds(part * COLS, COLS)
            q = acc[here, :] * row_factors(squares, part)
            c, s = cosine[here, :], sine[here, :]
            out = first if part < 2 else second
            out[pl.ds((part % 2) * COLS, COLS), :] = jnp.concatenate(
                [rotate(q[:, :HEAD], c, s), rotate(q[:, HEAD:], c, s)], axis=1
            ).astype(bf16)


def project_query(gathered, weights, cosine, sine):
    per_step = 8
    steps = 32 // per_step
    return pl.pallas_call(
        functools.partial(query_kernel, steps, per_step),
        grid=(steps,),
        in_specs=[
            pl.BlockSpec((per_step, SEQ, COLS), lambda k: (k, 0, 0)),
            pl.BlockSpec((32, 16, COLS), lambda k: (0, SEQ // 16, 0)),
            pl.BlockSpec((per_step * COLS, COLS), lambda k: (k, 0)),
            pl.BlockSpec((SEQ, HEAD), lambda k: (0, 0)),
            pl.BlockSpec((SEQ, HEAD), lambda k: (0, 0)),
        ],
        out_specs=[pl.BlockSpec((CHUNK, COLS), lambda k: (0, 0))] * 2,
        out_shape=[jax.ShapeDtypeStruct((CHUNK, COLS), bf16)] * 2,
        scratch_shapes=[pltpu.VMEM((SEQ, COLS), f32)],
        compiler_params=pltpu.CompilerParams(vmem_limit_bytes=56 << 20),
        cost_estimate=pl.CostEstimate(
            flops=2 * SEQ * WIDTH * 256, bytes_accessed=20 << 20, transcendentals=0
        ),
        name="project_query",
    )(gathered, gathered, weights, cosine, sine)


def attention_kernel(chunk, scalars, queries, kv0, kv1, kv2, kv3, attended, all_k, all_v):
    for source, kv in enumerate((kv0, kv1, kv2, kv3)):
        start = pl.multiple_of(scalars[4 + source] * 256, 256)
        for i in range(2):
            there = pl.ds(start + i * BLOCK, BLOCK)
            all_k[there, :] = kv[i, 0]
            all_v[there, :] = kv[i, 1]
    base = chunk * CHUNK
    for part in range(CHUNK // 256):
        first = base + part * 256
        low = max(0, first - 512)
        high = first + 256
        here = pl.ds(part * 256, 256)
        i = lax.broadcasted_iota(jnp.int32, (256, 1), 0) + first
        starts = jnp.zeros((256, 1), jnp.int32)
        end = jnp.int32(0)
        for doc in range(4):
            end = end + scalars[doc]
            starts = starts + jnp.where(i >= end, scalars[doc], 0)
        j = lax.broadcasted_iota(jnp.int32, (256, high - low), 1) + low
        allowed = (j <= i) & (j >= starts)
        k = all_k[low:high, :]
        v = all_v[low:high, :]
        outs = []
        for head in range(2):
            q = queries[here, head * HEAD : (head + 1) * HEAD]
            scores = lax.dot_general(q, k, (((1,), (1,)), ((), ())), preferred_element_type=f32)
            scores = jnp.where(allowed, scores * SCORE_SCALE, FILL)
            peak = jnp.max(scores, axis=1, keepdims=True)
            weights = jnp.exp2(scores - peak)
            norm = jnp.sum(weights, axis=1, keepdims=True)
            out = jnp.dot(weights.astype(bf16), v, preferred_element_type=f32)
            outs.append(out / norm)
        attended[here, :] = jnp.concatenate(outs, axis=1).astype(bf16)


def attend(chunk, scalars, queries, kvs):
    kv_spec = pl.BlockSpec((2, 2, BLOCK, HEAD), lambda k, n: (0, 0, 0, 0))
    return pl.pallas_call(
        functools.partial(attention_kernel, chunk),
        grid_spec=pltpu.PrefetchScalarGridSpec(
            num_scalar_prefetch=1,
            grid=(1,),
            in_specs=[pl.BlockSpec((CHUNK, COLS), lambda k, n: (0, 0))] + [kv_spec] * 4,
            out_specs=pl.BlockSpec((CHUNK, COLS), lambda k, n: (0, 0)),
            scratch_shapes=[pltpu.VMEM((SEQ, HEAD), bf16), pltpu.VMEM((SEQ, HEAD), bf16)],
        ),
        out_shape=jax.ShapeDtypeStruct((CHUNK, COLS), bf16),
        compiler_params=pltpu.CompilerParams(vmem_limit_bytes=56 << 20),
        cost_estimate=pl.CostEstimate(flops=1024, bytes_accessed=1024, transcendentals=0),
        name="attend",
    )(scalars, queries, *kvs)


def out_kernel(scalars, *refs):
    local, (up, far_up, far_down, down), blocks = refs[:4], refs[4:8], refs[8:12]
    keep, send = refs[12:14]
    rows = jnp.concatenate([b[...] for b in blocks], axis=1)
    half = 2 * COLS
    sources = (
        [(i * COLS, (i + 1) * COLS, w) for i, w in enumerate(local)],
        [(0, 4 * COLS, up)],
        [(0, half, far_up), (half, 4 * COLS, far_down)],
        [(0, 4 * COLS, down)],
    )
    for i, source in enumerate(sources):
        parts = [
            jnp.dot(rows[:, low:high], w[...], preferred_element_type=f32) for low, high, w in source
        ]
        part = functools.reduce(jnp.add, parts).astype(bf16)
        distance = scalars[i]
        mine, theirs = part[:, :COLS], part[:, COLS:]

        @pl.when(scalars[4] == 0)
        def _():
            keep[distance] = mine
            send[distance] = theirs

        @pl.when(scalars[4] == 1)
        def _():
            keep[distance] = theirs
            send[distance] = mine


def project_out(scalars, blocks, local, others):
    arrays = (*local, *others, *blocks)
    return pl.pallas_call(
        out_kernel,
        grid_spec=pltpu.PrefetchScalarGridSpec(
            num_scalar_prefetch=1,
            grid=(1,),
            in_specs=[pl.BlockSpec(a.shape, lambda i, n: (0, 0)) for a in arrays],
            out_specs=[pl.BlockSpec((4, CHUNK, COLS), lambda i, n: (0, 0, 0))] * 2,
        ),
        out_shape=[jax.ShapeDtypeStruct((4, CHUNK, COLS), bf16)] * 2,
        compiler_params=pltpu.CompilerParams(vmem_limit_bytes=56 << 20),
        cost_estimate=pl.CostEstimate(flops=1024, bytes_accessed=1024, transcendentals=0),
        name="project_out",
    )(scalars, *arrays)


def add_kernel(keep, got, *outs):
    for d in range(4):
        outs[d][...] = (keep[d].astype(f32) + got[d].astype(f32)).astype(bf16)


def add_cores(keep, got):
    return pl.pallas_call(
        add_kernel,
        out_shape=[jax.ShapeDtypeStruct((CHUNK, COLS), bf16)] * 4,
        compiler_params=pltpu.CompilerParams(vmem_limit_bytes=56 << 20),
        cost_estimate=pl.CostEstimate(flops=1024, bytes_accessed=1024, transcendentals=0),
        name="add_cores",
    )(keep, got)


def pick_kernel(index, valid, blocks, *rest):
    outs, sems = rest[:4], rest[4]

    def copy(i):
        return pltpu.make_async_copy(blocks.at[index[i]], outs[i // 2].at[i % 2], sems.at[i])

    for i in range(8):

        @pl.when(valid[i] > 0)
        def _():
            copy(i).start()

        @pl.when(valid[i] <= 0)
        def _():
            outs[i // 2][i % 2] = jnp.zeros((2, BLOCK, HEAD), bf16)

    for i in range(8):

        @pl.when(valid[i] > 0)
        def _():
            copy(i).wait()


def pick_blocks(index, valid, blocks):
    shape = (2, 2, BLOCK, HEAD)
    return pl.pallas_call(
        pick_kernel,
        grid_spec=pltpu.PrefetchScalarGridSpec(
            num_scalar_prefetch=2,
            grid=(1,),
            in_specs=[pl.BlockSpec(memory_space=pl.ANY)],
            out_specs=[pl.BlockSpec(shape, lambda i, n, m: (0, 0, 0, 0))] * 4,
            scratch_shapes=[pltpu.SemaphoreType.DMA((8,))],
        ),
        out_shape=[jax.ShapeDtypeStruct(shape, bf16)] * 4,
        compiler_params=pltpu.CompilerParams(vmem_limit_bytes=56 << 20),
        cost_estimate=pl.CostEstimate(flops=1024, bytes_accessed=1024, transcendentals=0),
        name="pick_blocks",
    )(index, valid, blocks)


def out_weights_along_y(w_out, g, y):
    def piece(d):
        column = (g * 8 + ((y + d) % 4) * 2) * COLS
        return lax.dynamic_slice(w_out, (0, column), (COLS, 2 * COLS))

    return [piece(0)] + [shift(piece(d), "y", d) for d in (1, 2, 3)]


def near_quarter(kv_weight, g):
    own = kv_weight.transpose(1, 2, 0)
    quarter = lax.dynamic_slice(own, (0, 0, g * 2048), (2, 32, 2048))
    return own, lax.ppermute(quarter, "y", PAIR)


def whole_near(near, g):
    relative = [near] + [shift(near, "g", d) for d in (3, 2, 1)]
    return lax.dynamic_slice(
        jnp.concatenate(relative + relative[:3], axis=2), (0, 0, ((4 - g) % 4) * 2048), (2, 32, WIDTH)
    )


def head_weights(own, near, y, c):
    pairs = []
    for value in (own, near):
        other = swap(value)
        pairs.append((jnp.where(c == 0, value, other), jnp.where(c == 0, other, value)))
    parts = [jnp.where(y % 2 == 0, pairs[0][i], pairs[1][i]) for i in range(2)]
    parts += [jnp.where(y % 2 == 0, pairs[1][i], pairs[0][i]) for i in range(2)]
    return jnp.stack(parts, axis=1).reshape(2 * HEAD, WIDTH)


def rope_tables(lengths):
    ends = jnp.cumsum(lengths)
    i = jnp.arange(SEQ, dtype=jnp.int32)
    passed = (i[:, None] >= ends[None, :]).astype(jnp.int32)
    positions = (i - jnp.sum(passed * lengths[None, :], axis=1)).astype(f32)
    frequency = jnp.exp(jnp.arange(HEAD // 2, dtype=f32) * (-2.0 * math.log(ROPE_BASE) / HEAD))
    angles = positions[:, None] * frequency[None, :]
    cosine, sine = jnp.cos(angles), jnp.sin(angles)
    return jnp.concatenate([cosine, cosine], 1), jnp.concatenate([-sine, sine], 1)


def store_plan(holder, g, z, y, c):
    owners = lax.dynamic_slice(holder[:, 0], (g * 64,), (64,))
    same = owners[:, None] == owners[None, :]
    before = jnp.arange(64)[None, :] < jnp.arange(64)[:, None]
    rank = jnp.sum((same & before).astype(jnp.int32), axis=1)
    slots = jnp.arange(64, dtype=jnp.int32)
    z_of, y_of, rest = slots // 16, (slots // 4) % 4, slots % 4
    block = ((y_of % 2) * 4 + rest) * 8 + z_of * 2 + y_of // 2
    owner, slot = owners[block], rank[block]
    target = (((g + jnp.arange(4)) % 4) * 32 + z * 8 + y * 2 + c).astype(jnp.int32)
    hit = (owner[None, None, :] == target[:, None, None]) & (
        slot[None, None, :] == jnp.arange(2)[None, :, None]
    )
    hit = hit.reshape(8, 64).astype(jnp.int32)
    return jnp.sum(hit * slots[None, :], axis=1), jnp.sum(hit, axis=1)


def local(tokens, norm_gain, w_query, kv_weight, w_out, doc_lengths, holder):
    g, z, y, c = (lax.axis_index(a) for a in ("g", "z", "y", "c"))
    sent = scale_tokens(tokens, norm_gain)
    gathered = lax.all_gather(sent, ("z", "y", "c"))

    own, near = near_quarter(kv_weight, g)
    local = out_weights_along_y(w_out, g, y)
    row = jnp.concatenate(local, axis=0)
    near, doc_lengths, holder, row = lax.optimization_barrier((near, doc_lengths, holder, row))
    up, down = shift(row, "g", 1), shift(row, "g", 3)
    far_up, far_down = shift(up[: 2 * COLS], "g", 1), shift(down[2 * COLS :], "g", 3)
    near = whole_near(near, g)
    w_kv = head_weights(own, near, y, c)
    order = jnp.stack([(g - z - d) % 4 for d in range(4)] + [c]).astype(jnp.int32)
    lengths = doc_lengths[0]
    cosine, sine = rope_tables(lengths)
    index, valid = store_plan(holder, g, z, y, c)
    low = y % 2
    place = low * 2 + c
    places = [place, low * 2 + 1 - c, (1 - low) * 2 + c, (1 - low) * 2 + 1 - c]
    scalars = jnp.concatenate([lengths, jnp.stack(places).astype(jnp.int32)])
    place = place.astype(jnp.int32).reshape(1)
    w_o = (local, (up, far_up, far_down, down))
    gathered, w_kv, w_o, order, index, valid, cosine, sine, scalars, place = (
        lax.optimization_barrier(
            (gathered, w_kv, w_o, order, index, valid, cosine, sine, scalars, place)
        )
    )

    own = project_key_value(place, gathered, w_kv, cosine, sine)
    everyone = lax.all_gather(own, ("z", "y", "c")).reshape(64, 2, BLOCK, HEAD)
    near = lax.ppermute(own, "y", PAIR)
    gathered, own = lax.optimization_barrier((gathered, own))
    queries = project_query(gathered, w_query, cosine, sine)
    near, queries = lax.optimization_barrier((near, queries))
    kvs = (own, swap(own), near, swap(near))

    attended = [attend(0, scalars, queries[0], kvs)]
    queries, attended[0] = lax.optimization_barrier((queries, attended[0]))
    attended.append(attend(1, scalars, queries[1], kvs))
    landed = [[shift(a, "y", d) for d in (1, 2, 3)] for a in attended]
    landed[0], attended[1] = lax.optimization_barrier((landed[0], attended[1]))
    sums = []
    for chunk in range(SEQ // CHUNK):
        keep, send = project_out(order, (attended[chunk], *landed[chunk]), *w_o)
        got = swap(send)
        if chunk == 0:
            keep, landed[1] = lax.optimization_barrier((keep, landed[1]))
        parts = add_cores(keep, got)
        sums.append([parts[0]] + [shift(parts[d], "z", d) for d in (1, 2, 3)])

    picked = pick_blocks(index, valid, everyone)
    arrived = [picked[0]] + [shift(picked[d], "g", d) for d in (1, 2, 3)]
    sums, arrived = lax.optimization_barrier((sums, arrived))
    sums = [sum(part.astype(f32) for part in moved) for moved in sums]
    mixed = (tokens.astype(f32) + jnp.concatenate(sums, axis=0)).astype(bf16)

    arrived = jnp.stack(arrived)
    stored = jnp.stack(
        [lax.dynamic_index_in_dim(arrived, (g - s) % 4, 0, keepdims=False) for s in range(4)]
    )
    return mixed, stored[None]


def solution(mesh):
    grid = Mesh(mesh.devices.reshape(4, 4, 4, 2), ("g", "z", "y", "c"))
    tp = ("z", "y", "c")
    return jax.shard_map(
        local,
        mesh=grid,
        in_specs=(
            P("g", tp),
            P(tp),
            P(None, tp),
            P(None, None, tp),
            P(tp, None),
            P("g", None),
            P(),
        ),
        out_specs=(P("g", tp), P(("g",) + tp, None, None, None, None, None)),
        check_vma=False,
    )
```

time: 227 us -> 207 us (0.912)
  waiting for transfers between devices: 87.3 us -> 55.6 us
  local copies, waits for them, and re-layouts: 17.1 us -> 23.9 us
  starting transfers between devices: 45.2 us -> 51.1 us
  Pallas kernels: 47 us -> 50.5 us
  other arithmetic: 14.4 us -> 10.9 us
    ppermute x21 -> x25, waiting for transfers between devices: 61 us -> 41.2 us  [shift(): return lax.ppermute(value, axis, SHIFT[distance])]
    ppermute x1 -> x2, waiting for transfers between devices: 22.3 us -> 8.96 us  [the longest x1 8.96 us: near_quarter(): return (own, lax.ppermute(quarter, 'y', PAIR))]
    unnamed x46 -> x62, local copies, waits for them, and re-layouts: 1.78 us -> 10.9 us
    optimization_barrier x1 -> x0, local copies, waits for them, and re-layouts: 6.41 us -> none  [local(): lax.optimization_barrier((gathered, w_kv, w_o, index, valid, cosine, sine))]
    ppermute x21 -> x25, starting transfers between devices: 42.5 us -> 47.6 us  [shift(): return lax.ppermute(value, axis, SHIFT[distance])]
    ppermute x10 -> x6, waiting for transfers between devices: 0.03 us -> 3.97 us  [swap(): return lax.ppermute(value, 'c', SWAP)]
    dynamic_slice x0 -> x2, local copies, waits for them, and re-layouts: none -> 3.36 us  [the longest x1 2.39 us: whole_near(): lax.dynamic_slice(jnp.concatenate(relative + relative[:3], axis=2), (0, 0...]
    select_n x3 -> x0, other arithmetic: 2.98 us -> none  [the longest x1 2.42 us: head_weights(): jnp.where(c == 0, jnp.stack([both, other], 1), jnp.stack([other, both], 1))]
  transfers between devices with their start and end apart: 34 -> 35, of which waited for: 12 -> 18; matrix products, arithmetic and copies ran while one was open for 9% -> 14% of each run, Pallas kernels for 6% -> 21%
where the time goes in v2:
time: 207 us; the launch traced here: 206 us
  waiting for transfers between devices  55.6 us (27%)
  starting transfers between devices  51.1 us (25%)
  Pallas kernels  50.5 us (24%)
  local copies, waits for them, and re-layouts  23.9 us (12%)
  between operations  14.5 us (7%)
  other arithmetic  10.9 us (5%)
    ppermute x25, starting transfers between devices, shift(): return lax.ppermute(value, axis, SHIFT[distance])  47.6 us
    ppermute x25, waiting for transfers between devices, shift(): return lax.ppermute(value, axis, SHIFT[distance])  41.2 us
    pallas_call x2, Pallas kernels, project_out(): pl.pallas_call(out_kernel, grid_spec=pltpu.PrefetchScalarGridSpec(num_sca...  15.3 us
    pallas_call x1, Pallas kernels, project_query(): pl.pallas_call(functools.partial(query_kernel, steps, per_step), grid=(st...  11.2 us
    unnamed x62, local copies, waits for them, and re-layouts  10.9 us
    ppermute x1, waiting for transfers between devices, near_quarter(): return (own, lax.ppermute(quarter, 'y', PAIR))  8.96 us
    pallas_call x2, Pallas kernels, attend(): pl.pallas_call(functools.partial(attention_kernel, chunk), grid_spec=pltp...  8.32 us
    pallas_call x1, Pallas kernels, project_key_value(): pl.pallas_call(functools.partial(key_value_kernel, steps, per_step), grid...  5.92 us
  transfers between devices with their start and end apart: 35, of which 18 were waited for; matrix products, arithmetic and copies ran while one was open for 14% of the time, Pallas kernels for 21%

profile of v2, /device:TPU:0, one launch (start us, length us, event | category | flops | bytes accessed | tf_op | source)
XLA Modules:
  0.0 206.4 jit_solution(5202658812980165042)
XLA Ops:
  7.2 2.1 %scale_tokens.1 = bf16[1040,256]{1,0:T(8,128)(2,1)} custom-call(bf16[1024,256]{1,0:T(8,128)(2,1)} %tokens.1, bf16[256]{0:T(256)(128)(2,1)} %gain.1), custom_call_target="tpu_custom_call" | custom-call | tf_op jit(solution)/shard_map/scale_tokens/pallas_call | solution.py:59
  12.5 2.9 %collective-permute-start.3 = (bf16[256,512]{1,0:T(8,128)(2,1)S(1)}, bf16[256,512]{1,0:T(8,128)(2,1)S(1)}, u32[]{:S(2)}, u32[]{:S(2)}) collective-permute-start(bf16[256,512]{1,0:T(8,128)(2,1)S(1)} %get-tuple-element.143), channel_id=1, source_target_pairs={{0,4},{2,6},{4,0},{6,2},{1,5},{3,7},{5,1},{7,3},{8,12},{10,14},{12... | collective-permute-start | bytes 786440 | tf_op jit(solution)/shard_map/ppermute | solution.py:31
  20.2 9.0 %collective-permute-done.3.refs_2_ = bf16[256,512]{1,0:T(8,128)(2,1)S(1)} collective-permute-done((bf16[256,512]{1,0:T(8,128)(2,1)S(1)}, bf16[256,512]{1,0:T(8,128)(2,1)S(1)}, u32[]{:S(2)}, u32[]{:S(2)}) %collective-permute-start.3) | collective-permute-done | bytes 262176 | tf_op jit(solution)/shard_map/ppermute | solution.py:31
  30.9 9.0 %collective-permute-done.1 = bf16[2,32,2048]{2,1,0:T(8,128)(2,1)S(1)} collective-permute-done((bf16[2,32,2048]{2,1,0:T(8,128)(2,1)S(1)}, bf16[2,32,2048]{2,1,0:T(8,128)(2,1)S(1)}, u32[]{:S(2)}, u32[]{:S(2)}) %collective-permute-start.1) | collective-permute-done | bytes 262176 | tf_op jit(solution)/shard_map/ppermute | solution.py:341
  39.8 2.9 %collective-permute-start.5 = (bf16[2,32,2048]{2,1,0:T(8,128)(2,1)S(1)}, bf16[2,32,2048]{2,1,0:T(8,128)(2,1)S(1)}, u32[]{:S(2)}, u32[]{:S(2)}) collective-permute-start(bf16[2,32,2048]{2,1,0:T(8,128)(2,1)S(1)} %collective-permute-done.1), channel_id=1, source_target_pairs={{0,96},{32,0},{64,32},{96,64},{1,97},{33,1},{65,33},{97,65},{2,98}... | collective-permute-start | bytes 786440 | tf_op jit(solution)/shard_map/ppermute | solution.py:31
  49.1 3.8 %collective-permute-start.11 = (bf16[1024,512]{1,0:T(8,128)(2,1)}, bf16[1024,512]{1,0:T(8,128)(2,1)S(1)}, u32[]{:S(2)}, u32[]{:S(2)}) collective-permute-start(bf16[1024,512]{1,0:T(8,128)(2,1)} %pad_maximum_fusion.1), channel_id=1, source_target_pairs={{0,96},{32,0},{64,32},{96,64},{1,97},{33,1},{65,33},{97,65},{2,98}... | collective-permute-start | bytes 3145736 | tf_op jit(solution)/shard_map/ppermute | solution.py:31
  61.6 2.4 %constant_dynamic-slice_fusion.5 = bf16[2,32,8192]{2,1,0:T(8,128)(2,1)} fusion(bf16[2,32,14336]{2,1,0:T(8,128)(2,1)} %constant_dynamic-update-slice_fusion, s32[]{:T(128)S(6)} %select_n.255), kind=kLoop, calls=%fused_computation.48 | loop fusion | bytes 2097156 | tf_op jit(solution)/shard_map/dynamic_slice | solution.py:346
  69.4 7.1 %collective-permute-done.9.refs_4_ = bf16[1024,512]{1,0:T(8,128)(2,1)S(1)} collective-permute-done((bf16[1024,512]{1,0:T(8,128)(2,1)}, bf16[1024,512]{1,0:T(8,128)(2,1)S(1)}, u32[]{:S(2)}, u32[]{:S(2)}) %collective-permute-start.9) | collective-permute-done | bytes 1048608 | tf_op jit(solution)/shard_map/ppermute | solution.py:31
  76.8 3.3 %collective-permute-start.12 = (bf16[512,512]{1,0:T(8,128)(2,1)S(1)}, bf16[512,512]{1,0:T(8,128)(2,1)S(1)}, u32[]{:S(2)}, u32[]{:S(2)}) collective-permute-start(bf16[512,512]{1,0:T(8,128)(2,1)S(1)} %slice.13), channel_id=1, source_target_pairs={{0,96},{32,0},{64,32},{96,64},{1,97},{33,1},{65,33},{97,65},{2,98}... | collective-permute-start | bytes 1572872 | tf_op jit(solution)/shard_map/ppermute | solution.py:31
  80.1 3.2 %select_bitcast_fusion.3 = (bf16[2,1,32,8192]{3,2,0,1:T(8,128)(2,1)S(1)}, bf16[2,1,32,8192]{3,2,0,1:T(8,128)(2,1)S(1)}, bf16[2,1,32,8192]{3,2,0,1:T(8,128)(2,1)S(1)}, bf16[2,1,32,8192]{3,2,0,1:T(8,128)(2,1)S(1)}) fusion(pred[]{:T(512)S(6)} %eq.86, bf16[2,32,8192]{2,1,0:T(8,128)(2,1)} %collective-permute-done, pred[]{:T(512)S(6)} %eq.87, ...), kind=kLoop, calls=%fused_computation.9 | loop fusion | flops 4194304 | bytes 8388614 | tf_op jit(solution)/shard_map/stack | solution.py:358
  83.8 2.3 %copy.12 = bf16[2,4,32,8192]{3,2,1,0:T(8,128)(2,1)} copy(bf16[2,4,32,8192]{3,2,0,1:T(8,128)(2,1)S(1)} %pad_maximum_fusion) | data formatting | bytes 8388608 | tf_op jit(solution)/shard_map/stack | solution.py:358
  86.1 3.4 %collective-permute-done.10.refs_5_ = bf16[512,512]{1,0:T(8,128)(2,1)S(1)} collective-permute-done((bf16[512,512]{1,0:T(8,128)(2,1)S(1)}, bf16[512,512]{1,0:T(8,128)(2,1)S(1)}, u32[]{:S(2)}, u32[]{:S(2)}) %collective-permute-start.10) | collective-permute-done | bytes 524320 | tf_op jit(solution)/shard_map/ppermute | solution.py:31
  90.9 5.9 %project_key_value.1.kv0 = bf16[2,2,128,128]{3,2,1,0:T(8,128)(2,1)} custom-call(s32[1]{0:T(128)} %bitcast.18.place, bf16[32,1040,256]{2,1,0:T(8,128)(2,1)} %bitcast.39, bf16[32,1040,256]{2,1,0:T(8,128)(2,1)} %bitcast.40, bf16[256,8192]{1,0:T(8,128)(2,1)} %bitcast.43, f32[1024,128]{1,0:T(8,128)} %get-tuple-element.84.cosine, f32[1024,128]{1,0:T(8,128)} %get-tuple-element.85.sine), custom_call_target="tpu_custom_call" | custom-call | flops 1073741824 | bytes 8388608 | tf_op jit(solution)/shard_map/project_key_value/pallas_call | solution.py:103
  98.5 11.2 %project_query.1 = (bf16[512,256]{1,0:T(8,128)(2,1)}, bf16[512,256]{1,0:T(8,128)(2,1)}) custom-call(bf16[32,1040,256]{2,1,0:T(8,128)(2,1)} %bitcast.41, bf16[32,1040,256]{2,1,0:T(8,128)(2,1)} %bitcast.42, bf16[8192,256]{1,0:T(8,128)(2,1)} %weights.1, f32[1024,128]{1,0:T(8,128)} %get-tuple-element.84.cosine, f32[1024,128]{1,0:T(8,128)} %get-tuple-element.85.sine), custom_call_target="tpu_custom_call" | custom-call | flops 4294967296 | bytes 20971520 | tf_op jit(solution)/shard_map/project_query/pallas_call | solution.py:152
  111.9 3.9 %attend.2.refs_8_ = bf16[512,256]{1,0:T(8,128)(2,1)} custom-call(s32[8]{0:T(128)} %concatenate.22.scalars, bf16[512,256]{1,0:T(8,128)(2,1)} %get-tuple-element.89.queries, bf16[2,2,128,128]{3,2,1,0:T(8,128)(2,1)} %project_key_value.1.kv0, bf16[2,2,128,128]{3,2,1,0:T(8,128)(2,1)} %copy-done.15, bf16[2,2,128,128]{3,2,1,0:T(8,128)(2,1)} %copy-done.14, ...), custom_call_target="tpu_custom_call" | custom-call | flops 1024 | bytes 1024 | tf_op jit(solution)/shard_map/attend/pallas_call | solution.py:211
  116.4 3.0 %collective-permute-start.17 = (bf16[512,256]{1,0:T(8,128)(2,1)}, bf16[512,256]{1,0:T(8,128)(2,1)S(1)}, u32[]{:S(2)}, u32[]{:S(2)}) collective-permute-start(bf16[512,256]{1,0:T(8,128)(2,1)} %attend.2.refs_8_), channel_id=1, source_target_pairs={{0,4},{2,6},{4,0},{6,2},{1,5},{3,7},{5,1},{7,3},{8,12},{10,14},{12... | collective-permute-start | bytes 786440 | tf_op jit(solution)/shard_map/ppermute | solution.py:31
  121.2 4.4 %attend.3.refs_8_ = bf16[512,256]{1,0:T(8,128)(2,1)} custom-call(s32[8]{0:T(128)} %concatenate.22.scalars, bf16[512,256]{1,0:T(8,128)(2,1)} %get-tuple-element.95.queries, bf16[2,2,128,128]{3,2,1,0:T(8,128)(2,1)} %project_key_value.1.kv0, bf16[2,2,128,128]{3,2,1,0:T(8,128)(2,1)} %copy-done.15, bf16[2,2,128,128]{3,2,1,0:T(8,128)(2,1)} %copy-done.14, ...), custom_call_target="tpu_custom_call" | custom-call | flops 1024 | bytes 1024 | tf_op jit(solution)/shard_map/attend/pallas_call | solution.py:211
  127.1 2.0 collective-permute-start.21
  129.1 3.6 %collective-permute-done.17.refs_10_ = bf16[512,256]{1,0:T(8,128)(2,1)S(1)} collective-permute-done((bf16[512,256]{1,0:T(8,128)(2,1)}, bf16[512,256]{1,0:T(8,128)(2,1)S(1)}, u32[]{:S(2)}, u32[]{:S(2)}) %collective-permute-start.17) | collective-permute-done | bytes 262176 | tf_op jit(solution)/shard_map/ppermute | solution.py:31
  134.1 7.5 %project_out.2 = (bf16[4,512,256]{2,1,0:T(8,128)(2,1)}, bf16[4,512,256]{2,1,0:T(8,128)(2,1)}) custom-call(s32[5]{0:T(128)} %stack.77.scalars, bf16[256,512]{1,0:T(8,128)(2,1)} %copy-done.4, bf16[256,512]{1,0:T(8,128)(2,1)} %copy-done.6, bf16[256,512]{1,0:T(8,128)(2,1)} %copy-done.7, bf16[256,512]{1,0:T(8,128)(2,1)} %copy-done.8, ...), custom_call_target="tpu_custom_call" | custom-call | flops 1024 | bytes 1024 | tf_op jit(solution)/shard_map/project_out/pallas_call | solution.py:259
  141.7 8.2 %collective-permute-done.20.refs_10_ = bf16[512,256]{1,0:T(8,128)(2,1)S(1)} collective-permute-done((bf16[512,256]{1,0:T(8,128)(2,1)}, bf16[512,256]{1,0:T(8,128)(2,1)S(1)}, u32[]{:S(2)}, u32[]{:S(2)}) %collective-permute-start.20) | collective-permute-done | bytes 262176 | tf_op jit(solution)/shard_map/ppermute | solution.py:31
  150.8 7.7 %project_out.3 = (bf16[4,512,256]{2,1,0:T(8,128)(2,1)}, bf16[4,512,256]{2,1,0:T(8,128)(2,1)}) custom-call(s32[5]{0:T(128)} %stack.77.scalars, bf16[256,512]{1,0:T(8,128)(2,1)} %copy-done.4, bf16[256,512]{1,0:T(8,128)(2,1)} %copy-done.6, bf16[256,512]{1,0:T(8,128)(2,1)} %copy-done.7, bf16[256,512]{1,0:T(8,128)(2,1)} %copy-done.8, ...), custom_call_target="tpu_custom_call" | custom-call | flops 1024 | bytes 1024 | tf_op jit(solution)/shard_map/project_out/pallas_call | solution.py:259
  159.0 3.0 %collective-permute-done.26.got = bf16[4,512,256]{2,1,0:T(8,128)(2,1)S(1)} collective-permute-done((bf16[4,512,256]{2,1,0:T(8,128)(2,1)}, bf16[4,512,256]{2,1,0:T(8,128)(2,1)S(1)}, u32[]{:S(2)}, u32[]{:S(2)}) %collective-permute-start.26) | collective-permute-done | bytes 1048608 | tf_op jit(solution)/shard_map/ppermute | solution.py:35
  163.0 2.6 %add_cores.3 = (bf16[512,256]{1,0:T(8,128)(2,1)}, bf16[512,256]{1,0:T(8,128)(2,1)}, bf16[512,256]{1,0:T(8,128)(2,1)}, bf16[512,256]{1,0:T(8,128)(2,1)}) custom-call(bf16[4,512,256]{2,1,0:T(8,128)(2,1)} %get-tuple-element.110.keep, bf16[4,512,256]{2,1,0:T(8,128)(2,1)} %copy-done.13), custom_call_target="tpu_custom_call" | custom-call | flops 1024 | bytes 1024 | tf_op jit(solution)/shard_map/add_cores/pallas_call | solution.py:280
  165.7 6.7 %collective-permute-start.28 = (bf16[512,256]{1,0:T(8,128)(2,1)}, bf16[512,256]{1,0:T(8,128)(2,1)S(1)}, u32[]{:S(2)}, u32[]{:S(2)}) collective-permute-start(bf16[512,256]{1,0:T(8,128)(2,1)} %get-tuple-element.114), channel_id=1, source_target_pairs={{0,16},{8,24},{16,0},{24,8},{1,17},{9,25},{17,1},{25,9},{2,18},{10... | collective-permute-start | bytes 786440 | tf_op jit(solution)/shard_map/ppermute | solution.py:31
  173.5 2.6 %add_cores.2 = (bf16[512,256]{1,0:T(8,128)(2,1)}, bf16[512,256]{1,0:T(8,128)(2,1)}, bf16[512,256]{1,0:T(8,128)(2,1)}, bf16[512,256]{1,0:T(8,128)(2,1)}) custom-call(bf16[4,512,256]{2,1,0:T(8,128)(2,1)} %get-tuple-element.100.keep, bf16[4,512,256]{2,1,0:T(8,128)(2,1)} %copy-done.12), custom_call_target="tpu_custom_call" | custom-call | flops 1024 | bytes 1024 | tf_op jit(solution)/shard_map/add_cores/pallas_call | solution.py:280
  176.1 2.0 collective-permute-start.23
  178.1 2.7 %collective-permute-start.25 = (bf16[512,256]{1,0:T(8,128)(2,1)}, bf16[512,256]{1,0:T(8,128)(2,1)S(1)}, u32[]{:S(2)}, u32[]{:S(2)}) collective-permute-start(bf16[512,256]{1,0:T(8,128)(2,1)} %get-tuple-element.105), channel_id=1, source_target_pairs={{0,24},{8,0},{16,8},{24,16},{1,25},{9,1},{17,9},{25,17},{2,26},{10... | collective-permute-start | bytes 786440 | tf_op jit(solution)/shard_map/ppermute | solution.py:31
  180.8 2.5 %pick_blocks.1 = (bf16[2,2,128,128]{3,2,1,0:T(8,128)(2,1)}, bf16[2,2,128,128]{3,2,1,0:T(8,128)(2,1)}, bf16[2,2,128,128]{3,2,1,0:T(8,128)(2,1)}, bf16[2,2,128,128]{3,2,1,0:T(8,128)(2,1)}) custom-call(s32[8]{0:T(128)} %reduce_sum.42.index, s32[8]{0:T(128)} %reduce_sum.44.valid, bf16[64,2,128,128]{3,2,1,0:T(8,128)(2,1)} %all-gather.7.cloned.1.call-done.blocks), custom_call_target="tpu_custom_call" | custom-call | flops 1024 | bytes 1024 | tf_op jit(solution)/shard_map/pick_blocks/pallas_call | solution.py:314
  183.3 2.2 %collective-permute-done.28 = bf16[512,256]{1,0:T(8,128)(2,1)S(1)} collective-permute-done((bf16[512,256]{1,0:T(8,128)(2,1)}, bf16[512,256]{1,0:T(8,128)(2,1)S(1)}, u32[]{:S(2)}, u32[]{:S(2)}) %collective-permute-start.28) | collective-permute-done | bytes 262176 | tf_op jit(solution)/shard_map/ppermute | solution.py:31
  185.5 4.5 %collective-permute-start.31 = (bf16[2,2,128,128]{3,2,1,0:T(8,128)(2,1)}, bf16[2,2,128,128]{3,2,1,0:T(8,128)(2,1)S(1)}, u32[]{:S(2)}, u32[]{:S(2)}) collective-permute-start(bf16[2,2,128,128]{3,2,1,0:T(8,128)(2,1)} %get-tuple-element.120), channel_id=1, source_target_pairs={{0,64},{32,96},{64,0},{96,32},{1,65},{33,97},{65,1},{97,33},{2,66}... | collective-permute-start | bytes 393224 | tf_op jit(solution)/shard_map/ppermute | solution.py:31
  190.9 3.1 %collective-permute-start.32 = (bf16[2,2,128,128]{3,2,1,0:T(8,128)(2,1)}, bf16[2,2,128,128]{3,2,1,0:T(8,128)(2,1)S(1)}, u32[]{:S(2)}, u32[]{:S(2)}) collective-permute-start(bf16[2,2,128,128]{3,2,1,0:T(8,128)(2,1)} %get-tuple-element.121), channel_id=1, source_target_pairs={{0,96},{32,0},{64,32},{96,64},{1,97},{33,1},{65,33},{97,65},{2,98}... | collective-permute-start | bytes 393224 | tf_op jit(solution)/shard_map/ppermute | solution.py:31
  (150 shorter events, 51.2 us)
Async XLA Ops:
  7.2 83.8 %all-gather.5.cloned.1.call-start = ((), (), s32[]{:S(2)}) async-start(), calls=%async_computation | async-start | bytes 17571840 | tf_op jit(solution)/shard_map/all_gather | solution.py:392
  9.4 171.4 %all-gather.7.cloned.1.call-start = ((), (), s32[]{:S(2)}) async-start(), calls=%async_computation.1 | async-start | bytes 4325376 | tf_op jit(solution)/shard_map/all_gather | solution.py:419
  10.8 9.5 %collective-permute-start.2 = (bf16[256,512]{1,0:T(8,128)(2,1)S(1)}, bf16[256,512]{1,0:T(8,128)(2,1)S(1)}, u32[]{:S(2)}, u32[]{:S(2)}) collective-permute-start(bf16[256,512]{1,0:T(8,128)(2,1)S(1)} %get-tuple-element.141), channel_id=1, source_target_pairs={{0,2},{2,4},{4,6},{6,0},{1,3},{3,5},{5,7},{7,1},{8,10},{10,12},{12... | collective-permute-start | bytes 786440 | tf_op jit(solution)/shard_map/ppermute | solution.py:31
  12.5 16.7 %collective-permute-start.3 = (bf16[256,512]{1,0:T(8,128)(2,1)S(1)}, bf16[256,512]{1,0:T(8,128)(2,1)S(1)}, u32[]{:S(2)}, u32[]{:S(2)}) collective-permute-start(bf16[256,512]{1,0:T(8,128)(2,1)S(1)} %get-tuple-element.143), channel_id=1, source_target_pairs={{0,4},{2,6},{4,0},{6,2},{1,5},{3,7},{5,1},{7,3},{8,12},{10,14},{12... | collective-permute-start | bytes 786440 | tf_op jit(solution)/shard_map/ppermute | solution.py:31
  15.4 14.4 %collective-permute-start.4 = (bf16[256,512]{1,0:T(8,128)(2,1)S(1)}, bf16[256,512]{1,0:T(8,128)(2,1)S(1)}, u32[]{:S(2)}, u32[]{:S(2)}) collective-permute-start(bf16[256,512]{1,0:T(8,128)(2,1)S(1)} %get-tuple-element.142), channel_id=1, source_target_pairs={{0,6},{2,0},{4,2},{6,4},{1,7},{3,1},{5,3},{7,5},{8,14},{10,8},{12,... | collective-permute-start | bytes 786440 | tf_op jit(solution)/shard_map/ppermute | solution.py:31
  17.7 22.1 %collective-permute-start.1 = (bf16[2,32,2048]{2,1,0:T(8,128)(2,1)S(1)}, bf16[2,32,2048]{2,1,0:T(8,128)(2,1)S(1)}, u32[]{:S(2)}, u32[]{:S(2)}) collective-permute-start(bf16[2,32,2048]{2,1,0:T(8,128)(2,1)S(1)} %dynamic-slice_bitcast_fusion), channel_id=1, source_target_pairs={{0,2},{2,0},{4,6},{6,4},{1,3},{3,1},{5,7},{7,5},{8,10},{10,8},{12,... | collective-permute-start | bytes 786440 | tf_op jit(solution)/shard_map/ppermute | solution.py:341
  18.5 61.6 %collective-permute-start = (bf16[2,32,8192]{2,1,0:T(8,128)(2,1)}, bf16[2,32,8192]{2,1,0:T(8,128)(2,1)}, u32[]{:S(2)}, u32[]{:S(2)}) collective-permute-start(bf16[2,32,8192]{2,1,0:T(8,128)(2,1)} %bitcast.1), channel_id=1, source_target_pairs={{0,1},{1,0},{2,3},{3,2},{4,5},{5,4},{6,7},{7,6},{8,9},{9,8},{10,11... | collective-permute-start | bytes 3145736 | tf_op jit(solution)/shard_map/ppermute | solution.py:35
  39.8 9.3 %collective-permute-start.5 = (bf16[2,32,2048]{2,1,0:T(8,128)(2,1)S(1)}, bf16[2,32,2048]{2,1,0:T(8,128)(2,1)S(1)}, u32[]{:S(2)}, u32[]{:S(2)}) collective-permute-start(bf16[2,32,2048]{2,1,0:T(8,128)(2,1)S(1)} %collective-permute-done.1), channel_id=1, source_target_pairs={{0,96},{32,0},{64,32},{96,64},{1,97},{33,1},{65,33},{97,65},{2,98}... | collective-permute-start | bytes 786440 | tf_op jit(solution)/shard_map/ppermute | solution.py:31
  42.7 10.9 %collective-permute-start.6 = (bf16[2,32,2048]{2,1,0:T(8,128)(2,1)S(1)}, bf16[2,32,2048]{2,1,0:T(8,128)(2,1)}, u32[]{:S(2)}, u32[]{:S(2)}) collective-permute-start(bf16[2,32,2048]{2,1,0:T(8,128)(2,1)S(1)} %collective-permute-done.1), channel_id=1, source_target_pairs={{0,64},{32,96},{64,0},{96,32},{1,65},{33,97},{65,1},{97,33},{2,66}... | collective-permute-start | bytes 786440 | tf_op jit(solution)/shard_map/ppermute | solution.py:31
  43.5 13.2 %collective-permute-start.7 = (bf16[2,32,2048]{2,1,0:T(8,128)(2,1)S(1)}, bf16[2,32,2048]{2,1,0:T(8,128)(2,1)}, u32[]{:S(2)}, u32[]{:S(2)}) collective-permute-start(bf16[2,32,2048]{2,1,0:T(8,128)(2,1)S(1)} %collective-permute-done.1), channel_id=1, source_target_pairs={{0,32},{32,64},{64,96},{96,0},{1,33},{33,65},{65,97},{97,1},{2,34}... | collective-permute-start | bytes 786440 | tf_op jit(solution)/shard_map/ppermute | solution.py:31
  47.2 29.4 %collective-permute-start.9 = (bf16[1024,512]{1,0:T(8,128)(2,1)}, bf16[1024,512]{1,0:T(8,128)(2,1)S(1)}, u32[]{:S(2)}, u32[]{:S(2)}) collective-permute-start(bf16[1024,512]{1,0:T(8,128)(2,1)} %pad_maximum_fusion.1), channel_id=1, source_target_pairs={{0,32},{32,64},{64,96},{96,0},{1,33},{33,65},{65,97},{97,1},{2,34}... | collective-permute-start | bytes 3145736 | tf_op jit(solution)/shard_map/ppermute | solution.py:31
  49.1 27.6 %collective-permute-start.11 = (bf16[1024,512]{1,0:T(8,128)(2,1)}, bf16[1024,512]{1,0:T(8,128)(2,1)S(1)}, u32[]{:S(2)}, u32[]{:S(2)}) collective-permute-start(bf16[1024,512]{1,0:T(8,128)(2,1)} %pad_maximum_fusion.1), channel_id=1, source_target_pairs={{0,96},{32,0},{64,32},{96,64},{1,97},{33,1},{65,33},{97,65},{2,98}... | collective-permute-start | bytes 3145736 | tf_op jit(solution)/shard_map/ppermute | solution.py:31
  64.0 16.1 %collective-permute-start.8 = (bf16[2,32,8192]{2,1,0:T(8,128)(2,1)}, bf16[2,32,8192]{2,1,0:T(8,128)(2,1)}, u32[]{:S(2)}, u32[]{:S(2)}) collective-permute-start(bf16[2,32,8192]{2,1,0:T(8,128)(2,1)} %constant_dynamic-slice_fusion.5), channel_id=1, source_target_pairs={{0,1},{1,0},{2,3},{3,2},{4,5},{5,4},{6,7},{7,6},{8,9},{9,8},{10,11... | collective-permute-start | bytes 3145736 | tf_op jit(solution)/shard_map/ppermute | solution.py:35
  76.6 12.9 %collective-permute-start.10 = (bf16[512,512]{1,0:T(8,128)(2,1)S(1)}, bf16[512,512]{1,0:T(8,128)(2,1)S(1)}, u32[]{:S(2)}, u32[]{:S(2)}) collective-permute-start(bf16[512,512]{1,0:T(8,128)(2,1)S(1)} %slice.12), channel_id=1, source_target_pairs={{0,32},{32,64},{64,96},{96,0},{1,33},{33,65},{65,97},{97,1},{2,34}... | collective-permute-start | bytes 1572872 | tf_op jit(solution)/shard_map/ppermute | solution.py:31
  76.8 12.7 %collective-permute-start.12 = (bf16[512,512]{1,0:T(8,128)(2,1)S(1)}, bf16[512,512]{1,0:T(8,128)(2,1)S(1)}, u32[]{:S(2)}, u32[]{:S(2)}) collective-permute-start(bf16[512,512]{1,0:T(8,128)(2,1)S(1)} %slice.13), channel_id=1, source_target_pairs={{0,96},{32,0},{64,32},{96,64},{1,97},{33,1},{65,33},{97,65},{2,98}... | collective-permute-start | bytes 1572872 | tf_op jit(solution)/shard_map/ppermute | solution.py:31
  96.9 12.8 %collective-permute-start.13 = (bf16[2,2,128,128]{3,2,1,0:T(8,128)(2,1)}, bf16[2,2,128,128]{3,2,1,0:T(8,128)(2,1)S(1)}, u32[]{:S(2)}, u32[]{:S(2)}) collective-permute-start(bf16[2,2,128,128]{3,2,1,0:T(8,128)(2,1)} %project_key_value.1.kv0), channel_id=1, source_target_pairs={{0,2},{2,0},{4,6},{6,4},{1,3},{3,1},{5,7},{7,5},{8,10},{10,8},{12,... | collective-permute-start | bytes 393224 | tf_op jit(solution)/shard_map/ppermute | solution.py:420
  98.5 11.8 %collective-permute-start.14 = (bf16[2,2,128,128]{3,2,1,0:T(8,128)(2,1)}, bf16[2,2,128,128]{3,2,1,0:T(8,128)(2,1)S(1)}, u32[]{:S(2)}, u32[]{:S(2)}) collective-permute-start(bf16[2,2,128,128]{3,2,1,0:T(8,128)(2,1)} %project_key_value.1.kv0), channel_id=1, source_target_pairs={{0,1},{1,0},{2,3},{3,2},{4,5},{5,4},{6,7},{7,6},{8,9},{9,8},{10,11... | collective-permute-start | bytes 393224 | tf_op jit(solution)/shard_map/ppermute | solution.py:35
  115.9 11.2 %collective-permute-start.16 = (bf16[512,256]{1,0:T(8,128)(2,1)}, bf16[512,256]{1,0:T(8,128)(2,1)S(1)}, u32[]{:S(2)}, u32[]{:S(2)}) collective-permute-start(bf16[512,256]{1,0:T(8,128)(2,1)} %attend.2.refs_8_), channel_id=1, source_target_pairs={{0,2},{2,4},{4,6},{6,0},{1,3},{3,5},{5,7},{7,1},{8,10},{10,12},{12... | collective-permute-start | bytes 786440 | tf_op jit(solution)/shard_map/ppermute | solution.py:31
  116.4 16.2 %collective-permute-start.17 = (bf16[512,256]{1,0:T(8,128)(2,1)}, bf16[512,256]{1,0:T(8,128)(2,1)S(1)}, u32[]{:S(2)}, u32[]{:S(2)}) collective-permute-start(bf16[512,256]{1,0:T(8,128)(2,1)} %attend.2.refs_8_), channel_id=1, source_target_pairs={{0,4},{2,6},{4,0},{6,2},{1,5},{3,7},{5,1},{7,3},{8,12},{10,14},{12... | collective-permute-start | bytes 786440 | tf_op jit(solution)/shard_map/ppermute | solution.py:31
  119.4 13.5 %collective-permute-start.18 = (bf16[512,256]{1,0:T(8,128)(2,1)}, bf16[512,256]{1,0:T(8,128)(2,1)S(1)}, u32[]{:S(2)}, u32[]{:S(2)}) collective-permute-start(bf16[512,256]{1,0:T(8,128)(2,1)} %attend.2.refs_8_), channel_id=1, source_target_pairs={{0,6},{2,0},{4,2},{6,4},{1,7},{3,1},{5,3},{7,5},{8,14},{10,8},{12,... | collective-permute-start | bytes 786440 | tf_op jit(solution)/shard_map/ppermute | solution.py:31
  125.6 16.0 %collective-permute-start.19 = (bf16[512,256]{1,0:T(8,128)(2,1)}, bf16[512,256]{1,0:T(8,128)(2,1)S(1)}, u32[]{:S(2)}, u32[]{:S(2)}) collective-permute-start(bf16[512,256]{1,0:T(8,128)(2,1)} %attend.3.refs_8_), channel_id=1, source_target_pairs={{0,2},{2,4},{4,6},{6,0},{1,3},{3,5},{5,7},{7,1},{8,10},{10,12},{12... | collective-permute-start | bytes 786440 | tf_op jit(solution)/shard_map/ppermute | solution.py:31
  125.8 24.1 %collective-permute-start.20 = (bf16[512,256]{1,0:T(8,128)(2,1)}, bf16[512,256]{1,0:T(8,128)(2,1)S(1)}, u32[]{:S(2)}, u32[]{:S(2)}) collective-permute-start(bf16[512,256]{1,0:T(8,128)(2,1)} %attend.3.refs_8_), channel_id=1, source_target_pairs={{0,4},{2,6},{4,0},{6,2},{1,5},{3,7},{5,1},{7,3},{8,12},{10,14},{12... | collective-permute-start | bytes 786440 | tf_op jit(solution)/shard_map/ppermute | solution.py:31
  127.1 22.9 %collective-permute-start.21 = (bf16[512,256]{1,0:T(8,128)(2,1)}, bf16[512,256]{1,0:T(8,128)(2,1)S(1)}, u32[]{:S(2)}, u32[]{:S(2)}) collective-permute-start(bf16[512,256]{1,0:T(8,128)(2,1)} %attend.3.refs_8_), channel_id=1, source_target_pairs={{0,6},{2,0},{4,2},{6,4},{1,7},{3,1},{5,3},{7,5},{8,14},{10,8},{12,... | collective-permute-start | bytes 786440 | tf_op jit(solution)/shard_map/ppermute | solution.py:31
  158.5 14.0 %collective-permute-start.22 = (bf16[4,512,256]{2,1,0:T(8,128)(2,1)S(1)}, bf16[4,512,256]{2,1,0:T(8,128)(2,1)S(1)}, u32[]{:S(2)}, u32[]{:S(2)}) collective-permute-start(bf16[4,512,256]{2,1,0:T(8,128)(2,1)S(1)} %copy-done.27), channel_id=1, source_target_pairs={{0,1},{1,0},{2,3},{3,2},{4,5},{5,4},{6,7},{7,6},{8,9},{9,8},{10,11... | collective-permute-start | bytes 3145736 | tf_op jit(solution)/shard_map/ppermute | solution.py:35
  165.5 12.6 %collective-permute-start.27 = (bf16[512,256]{1,0:T(8,128)(2,1)}, bf16[512,256]{1,0:T(8,128)(2,1)S(1)}, u32[]{:S(2)}, u32[]{:S(2)}) collective-permute-start(bf16[512,256]{1,0:T(8,128)(2,1)} %get-tuple-element.113), channel_id=1, source_target_pairs={{0,8},{8,16},{16,24},{24,0},{1,9},{9,17},{17,25},{25,1},{2,10},{10... | collective-permute-start | bytes 786440 | tf_op jit(solution)/shard_map/ppermute | solution.py:31
  165.7 19.7 %collective-permute-start.28 = (bf16[512,256]{1,0:T(8,128)(2,1)}, bf16[512,256]{1,0:T(8,128)(2,1)S(1)}, u32[]{:S(2)}, u32[]{:S(2)}) collective-permute-start(bf16[512,256]{1,0:T(8,128)(2,1)} %get-tuple-element.114), channel_id=1, source_target_pairs={{0,16},{8,24},{16,0},{24,8},{1,17},{9,25},{17,1},{25,9},{2,18},{10... | collective-permute-start | bytes 786440 | tf_op jit(solution)/shard_map/ppermute | solution.py:31
  172.5 13.0 %collective-permute-start.29 = (bf16[512,256]{1,0:T(8,128)(2,1)}, bf16[512,256]{1,0:T(8,128)(2,1)S(1)}, u32[]{:S(2)}, u32[]{:S(2)}) collective-permute-start(bf16[512,256]{1,0:T(8,128)(2,1)} %get-tuple-element.115), channel_id=1, source_target_pairs={{0,24},{8,0},{16,8},{24,16},{1,25},{9,1},{17,9},{25,17},{2,26},{10... | collective-permute-start | bytes 786440 | tf_op jit(solution)/shard_map/ppermute | solution.py:31
  176.1 14.8 %collective-permute-start.23 = (bf16[512,256]{1,0:T(8,128)(2,1)}, bf16[512,256]{1,0:T(8,128)(2,1)S(1)}, u32[]{:S(2)}, u32[]{:S(2)}) collective-permute-start(bf16[512,256]{1,0:T(8,128)(2,1)} %get-tuple-element.103), channel_id=1, source_target_pairs={{0,8},{8,16},{16,24},{24,0},{1,9},{9,17},{17,25},{25,1},{2,10},{10... | collective-permute-start | bytes 786440 | tf_op jit(solution)/shard_map/ppermute | solution.py:31
  178.1 17.8 %collective-permute-start.24 = (bf16[512,256]{1,0:T(8,128)(2,1)}, bf16[512,256]{1,0:T(8,128)(2,1)S(1)}, u32[]{:S(2)}, u32[]{:S(2)}) collective-permute-start(bf16[512,256]{1,0:T(8,128)(2,1)} %get-tuple-element.104), channel_id=1, source_target_pairs={{0,16},{8,24},{16,0},{24,8},{1,17},{9,25},{17,1},{25,9},{2,18},{10... | collective-permute-start | bytes 786440 | tf_op jit(solution)/shard_map/ppermute | solution.py:31
  178.1 17.8 %collective-permute-start.25 = (bf16[512,256]{1,0:T(8,128)(2,1)}, bf16[512,256]{1,0:T(8,128)(2,1)S(1)}, u32[]{:S(2)}, u32[]{:S(2)}) collective-permute-start(bf16[512,256]{1,0:T(8,128)(2,1)} %get-tuple-element.105), channel_id=1, source_target_pairs={{0,24},{8,0},{16,8},{24,16},{1,25},{9,1},{17,9},{25,17},{2,26},{10... | collective-permute-start | bytes 786440 | tf_op jit(solution)/shard_map/ppermute | solution.py:31
  185.5 10.4 %collective-permute-start.30 = (bf16[2,2,128,128]{3,2,1,0:T(8,128)(2,1)}, bf16[2,2,128,128]{3,2,1,0:T(8,128)(2,1)S(1)}, u32[]{:S(2)}, u32[]{:S(2)}) collective-permute-start(bf16[2,2,128,128]{3,2,1,0:T(8,128)(2,1)} %get-tuple-element.119), channel_id=1, source_target_pairs={{0,32},{32,64},{64,96},{96,0},{1,33},{33,65},{65,97},{97,1},{2,34}... | collective-permute-start | bytes 393224 | tf_op jit(solution)/shard_map/ppermute | solution.py:31
  185.5 10.4 %collective-permute-start.31 = (bf16[2,2,128,128]{3,2,1,0:T(8,128)(2,1)}, bf16[2,2,128,128]{3,2,1,0:T(8,128)(2,1)S(1)}, u32[]{:S(2)}, u32[]{:S(2)}) collective-permute-start(bf16[2,2,128,128]{3,2,1,0:T(8,128)(2,1)} %get-tuple-element.120), channel_id=1, source_target_pairs={{0,64},{32,96},{64,0},{96,32},{1,65},{33,97},{65,1},{97,33},{2,66}... | collective-permute-start | bytes 393224 | tf_op jit(solution)/shard_map/ppermute | solution.py:31
  (31 other events, 301.9 us)
Sparse Core Ops, SparseCore 0:
  10.3 80.6 all-gather.4
  97.0 57.6 all-gather.6

commit v3 on v2

--- a/solution.py
+++ b/solution.py
@@ -124,7 +124,7 @@
     )(place, gathered, gathered, weights, cosine, sine)
 
 
-def query_kernel(steps, per_step, x, squares, weights, cosine, sine, first, second, acc):
+def query_kernel(chunk, steps, per_step, x, squares, weights, cosine, sine, out, acc):
     step = pl.program_id(0)
 
     @pl.when(step == 0)
@@ -136,35 +136,34 @@
 
     @pl.when(step == steps - 1)
     def _():
-        for part in range(SEQ // COLS):
+        for part in range(CHUNK // COLS):
             here = pl.ds(part * COLS, COLS)
-            q = acc[here, :] * row_factors(squares, part)
+            q = acc[here, :] * row_factors(squares, chunk * (CHUNK // COLS) + part)
             c, s = cosine[here, :], sine[here, :]
-            out = first if part < 2 else second
-            out[pl.ds((part % 2) * COLS, COLS), :] = jnp.concatenate(
+            out[here, :] = jnp.concatenate(
                 [rotate(q[:, :HEAD], c, s), rotate(q[:, HEAD:], c, s)], axis=1
             ).astype(bf16)
 
 
-def project_query(gathered, weights, cosine, sine):
+def project_query(chunk, gathered, weights, cosine, sine):
     per_step = 8
     steps = 32 // per_step
     return pl.pallas_call(
-        functools.partial(query_kernel, steps, per_step),
+        functools.partial(query_kernel, chunk, steps, per_step),
         grid=(steps,),
         in_specs=[
-            pl.BlockSpec((per_step, SEQ, COLS), lambda k: (k, 0, 0)),
+            pl.BlockSpec((per_step, CHUNK, COLS), lambda k: (k, chunk, 0)),
             pl.BlockSpec((32, 16, COLS), lambda k: (0, SEQ // 16, 0)),
             pl.BlockSpec((per_step * COLS, COLS), lambda k: (k, 0)),
-            pl.BlockSpec((SEQ, HEAD), lambda k: (0, 0)),
-            pl.BlockSpec((SEQ, HEAD), lambda k: (0, 0)),
+            pl.BlockSpec((CHUNK, HEAD), lambda k: (chunk, 0)),
+            pl.BlockSpec((CHUNK, HEAD), lambda k: (chunk, 0)),
         ],
-        out_specs=[pl.BlockSpec((CHUNK, COLS), lambda k: (0, 0))] * 2,
-        out_shape=[jax.ShapeDtypeStruct((CHUNK, COLS), bf16)] * 2,
-        scratch_shapes=[pltpu.VMEM((SEQ, COLS), f32)],
+        out_specs=pl.BlockSpec((CHUNK, COLS), lambda k: (0, 0)),
+        out_shape=jax.ShapeDtypeStruct((CHUNK, COLS), bf16),
+        scratch_shapes=[pltpu.VMEM((CHUNK, COLS), f32)],
         compiler_params=pltpu.CompilerParams(vmem_limit_bytes=56 << 20),
         cost_estimate=pl.CostEstimate(
-            flops=2 * SEQ * WIDTH * 256, bytes_accessed=20 << 20, transcendentals=0
+            flops=2 * CHUNK * WIDTH * 256, bytes_accessed=12 << 20, transcendentals=0
         ),
         name="project_query",
     )(gathered, gathered, weights, cosine, sine)
@@ -226,9 +225,18 @@
 
 def out_kernel(scalars, *refs):
     local, (up, far_up, far_down, down), blocks = refs[:4], refs[4:8], refs[8:12]
-    keep, send = refs[12:14]
+    keep, sends = refs[12], refs[13:]
+    size = 4 // len(sends)
     rows = jnp.concatenate([b[...] for b in blocks], axis=1)
     half = 2 * COLS
+
+    def put(distance, value):
+        for j, send in enumerate(sends):
+
+            @pl.when(distance // size == j)
+            def _():
+                send[distance % size] = value
+
     sources = (
         [(i * COLS, (i + 1) * COLS, w) for i, w in enumerate(local)],
         [(0, 4 * COLS, up)],
@@ -246,12 +254,12 @@
         @pl.when(scalars[4] == 0)
         def _():
             keep[distance] = mine
-            send[distance] = theirs
+            put(distance, theirs)
 
         @pl.when(scalars[4] == 1)
         def _():
             keep[distance] = theirs
-            send[distance] = mine
+            put(distance, mine)
 
 
 def project_out(scalars, blocks, local, others):
@@ -262,18 +270,22 @@
             num_scalar_prefetch=1,
             grid=(1,),
             in_specs=[pl.BlockSpec(a.shape, lambda i, n: (0, 0)) for a in arrays],
-            out_specs=[pl.BlockSpec((4, CHUNK, COLS), lambda i, n: (0, 0, 0))] * 2,
-        ),
-        out_shape=[jax.ShapeDtypeStruct((4, CHUNK, COLS), bf16)] * 2,
+            out_specs=[pl.BlockSpec((4, CHUNK, COLS), lambda i, n: (0, 0, 0))]
+            + [pl.BlockSpec((1, CHUNK, COLS), lambda i, n: (0, 0, 0))] * 4,
+        ),
+        out_shape=[jax.ShapeDtypeStruct((4, CHUNK, COLS), bf16)]
+        + [jax.ShapeDtypeStruct((1, CHUNK, COLS), bf16)] * 4,
         compiler_params=pltpu.CompilerParams(vmem_limit_bytes=56 << 20),
         cost_estimate=pl.CostEstimate(flops=1024, bytes_accessed=1024, transcendentals=0),
         name="project_out",
     )(scalars, *arrays)
 
 
-def add_kernel(keep, got, *outs):
+def add_kernel(keep, *refs):
+    gots, outs = refs[:4], refs[4:]
     for d in range(4):
-        outs[d][...] = (keep[d].astype(f32) + got[d].astype(f32)).astype(bf16)
+        got = gots[d // 1][d % 1]
+        outs[d][...] = (keep[d].astype(f32) + got.astype(f32)).astype(bf16)
 
 
 def add_cores(keep, got):
@@ -283,7 +295,7 @@
         compiler_params=pltpu.CompilerParams(vmem_limit_bytes=56 << 20),
         cost_estimate=pl.CostEstimate(flops=1024, bytes_accessed=1024, transcendentals=0),
         name="add_cores",
-    )(keep, got)
+    )(keep, *got)
 
 
 def pick_kernel(index, valid, blocks, *rest):
@@ -327,12 +339,12 @@
     )(index, valid, blocks)
 
 
-def out_weights_along_y(w_out, g, y):
+def out_weights_along(w_out, axis, place, stride, base):
     def piece(d):
-        column = (g * 8 + ((y + d) % 4) * 2) * COLS
+        column = (base + ((place + d) % 4) * stride) * COLS
         return lax.dynamic_slice(w_out, (0, column), (COLS, 2 * COLS))
 
-    return [piece(0)] + [shift(piece(d), "y", d) for d in (1, 2, 3)]
+    return [piece(0)] + [shift(piece(d), axis, d) for d in (1, 2, 3)]
 
 
 def near_quarter(kv_weight, g):
@@ -392,14 +404,14 @@
     gathered = lax.all_gather(sent, ("z", "y", "c"))
 
     own, near = near_quarter(kv_weight, g)
-    local = out_weights_along_y(w_out, g, y)
+    local = out_weights_along(w_out, "z", z, 8, g * 2)
     row = jnp.concatenate(local, axis=0)
     near, doc_lengths, holder, row = lax.optimization_barrier((near, doc_lengths, holder, row))
     up, down = shift(row, "g", 1), shift(row, "g", 3)
     far_up, far_down = shift(up[: 2 * COLS], "g", 1), shift(down[2 * COLS :], "g", 3)
     near = whole_near(near, g)
     w_kv = head_weights(own, near, y, c)
-    order = jnp.stack([(g - z - d) % 4 for d in range(4)] + [c]).astype(jnp.int32)
+    order = jnp.stack([(g - y - d) % 4 for d in range(4)] + [c]).astype(jnp.int32)
     lengths = doc_lengths[0]
     cosine, sine = rope_tables(lengths)
     index, valid = store_plan(holder, g, z, y, c)
@@ -419,25 +431,27 @@
     everyone = lax.all_gather(own, ("z", "y", "c")).reshape(64, 2, BLOCK, HEAD)
     near = lax.ppermute(own, "y", PAIR)
     gathered, own = lax.optimization_barrier((gathered, own))
-    queries = project_query(gathered, w_query, cosine, sine)
+    queries = project_query(0, gathered, w_query, cosine, sine)
     near, queries = lax.optimization_barrier((near, queries))
     kvs = (own, swap(own), near, swap(near))
-
-    attended = [attend(0, scalars, queries[0], kvs)]
-    queries, attended[0] = lax.optimization_barrier((queries, attended[0]))
-    attended.append(attend(1, scalars, queries[1], kvs))
-    landed = [[shift(a, "y", d) for d in (1, 2, 3)] for a in attended]
+    attended = [attend(0, scalars, queries, kvs)]
+    gathered, attended[0] = lax.optimization_barrier((gathered, attended[0]))
+    queries = project_query(1, gathered, w_query, cosine, sine)
+    attended.append(attend(1, scalars, queries, kvs))
+    landed = [[shift(a, "z", d) for d in (1, 2, 3)] for a in attended]
     landed[0], attended[1] = lax.optimization_barrier((landed[0], attended[1]))
+    picked = pick_blocks(index, valid, everyone)
     sums = []
     for chunk in range(SEQ // CHUNK):
-        keep, send = project_out(order, (attended[chunk], *landed[chunk]), *w_o)
-        got = swap(send)
+        keep, *send = project_out(order, (attended[chunk], *landed[chunk]), *w_o)
+        got = [swap(part) for part in send]
         if chunk == 0:
-            keep, landed[1] = lax.optimization_barrier((keep, landed[1]))
+            got, landed[1] = lax.optimization_barrier((got, landed[1]))
+        else:
+            got, picked = lax.optimization_barrier((got, picked))
         parts = add_cores(keep, got)
-        sums.append([parts[0]] + [shift(parts[d], "z", d) for d in (1, 2, 3)])
-
-    picked = pick_blocks(index, valid, everyone)
+        sums.append([parts[0]] + [shift(parts[d], "y", d) for d in (1, 2, 3)])
+
     arrived = [picked[0]] + [shift(picked[d], "g", d) for d in (1, 2, 3)]
     sums, arrived = lax.optimization_barrier((sums, arrived))
     sums = [sum(part.astype(f32) for part in moved) for moved in sums]

time: 207 us -> 197 us (0.952)
  waiting for transfers between devices: 55.6 us -> 45.5 us
  Pallas kernels: 50.5 us -> 54.9 us
  starting transfers between devices: 51.1 us -> 48 us
    ppermute x1, waiting for transfers between devices: 8.96 us -> 0.01 us  [near_quarter(): return (own, lax.ppermute(quarter, 'y', PAIR))]
    ppermute x25, starting transfers between devices: 47.6 us -> 42.5 us  [shift(): return lax.ppermute(value, axis, SHIFT[distance])]
    pallas_call x1 -> x2, Pallas kernels: 11.2 us -> 15.4 us  [project_query(): pl.pallas_call(functools.partial(query_kernel, chunk, steps, per_step), g...]
    ppermute x6 -> x12, waiting for transfers between devices: 3.97 us -> 1.01 us  [swap(): return lax.ppermute(value, 'c', SWAP)]
    unnamed x62 -> x78, local copies, waits for them, and re-layouts: 10.9 us -> 9.8 us
  transfers between devices with their start and end apart: 35 -> 41, of which waited for: 18 -> 16; matrix products, arithmetic and copies ran while one was open for 14% -> 14% of each run, Pallas kernels for 21% -> 24%
where the time goes in v3:
time: 197 us
  Pallas kernels  54.9 us (28%)
  starting transfers between devices  48 us (24%)
  waiting for transfers between devices  45.5 us (23%)
  local copies, waits for them, and re-layouts  22.7 us (12%)
  between operations  14.7 us (7%)
  other arithmetic  11 us (6%)
    ppermute x25, waiting for transfers between devices, shift(): return lax.ppermute(value, axis, SHIFT[distance])  42.9 us
    ppermute x25, starting transfers between devices, shift(): return lax.ppermute(value, axis, SHIFT[distance])  42.5 us
    pallas_call x2, Pallas kernels, project_out(): pl.pallas_call(out_kernel, grid_spec=pltpu.PrefetchScalarGridSpec(num_sca...  15.5 us
    pallas_call x2, Pallas kernels, project_query(): pl.pallas_call(functools.partial(query_kernel, chunk, steps, per_step), g...  15.4 us
    unnamed x78, local copies, waits for them, and re-layouts  9.8 us
    pallas_call x2, Pallas kernels, attend(): pl.pallas_call(functools.partial(attention_kernel, chunk), grid_spec=pltp...  8.34 us
    pallas_call x1, Pallas kernels, project_key_value(): pl.pallas_call(functools.partial(key_value_kernel, steps, per_step), grid...  5.92 us
    pallas_call x2, Pallas kernels, add_cores(): pl.pallas_call(add_kernel, out_shape=[jax.ShapeDtypeStruct((CHUNK, COLS),...  5.09 us
  transfers between devices with their start and end apart: 41, of which 16 were waited for; matrix products, arithmetic and copies ran while one was open for 14% of the time, Pallas kernels for 24%

profile of v3, /device:TPU:0, one launch (start us, length us, event | category | flops | bytes accessed | tf_op | source)
XLA Modules:
  0.0 196.7 jit_solution(2177416858380652813)
XLA Ops:
  7.2 2.1 %scale_tokens.1 = bf16[1040,256]{1,0:T(8,128)(2,1)} custom-call(bf16[1024,256]{1,0:T(8,128)(2,1)} %tokens.1, bf16[256]{0:T(256)(128)(2,1)} %gain.1), custom_call_target="tpu_custom_call" | custom-call | tf_op jit(solution)/shard_map/scale_tokens/pallas_call | solution.py:59
  10.8 2.1 %collective-permute-start.2 = (bf16[256,512]{1,0:T(8,128)(2,1)S(1)}, bf16[256,512]{1,0:T(8,128)(2,1)S(1)}, u32[]{:S(2)}, u32[]{:S(2)}) collective-permute-start(bf16[256,512]{1,0:T(8,128)(2,1)S(1)} %get-tuple-element.169), channel_id=1, source_target_pairs={{0,8},{8,16},{16,24},{24,0},{1,9},{9,17},{17,25},{25,1},{2,10},{10... | collective-permute-start | bytes 786440 | tf_op jit(solution)/shard_map/ppermute | solution.py:31
  12.8 3.6 %collective-permute-start.3 = (bf16[256,512]{1,0:T(8,128)(2,1)S(1)}, bf16[256,512]{1,0:T(8,128)(2,1)S(1)}, u32[]{:S(2)}, u32[]{:S(2)}) collective-permute-start(bf16[256,512]{1,0:T(8,128)(2,1)S(1)} %get-tuple-element.171), channel_id=1, source_target_pairs={{0,16},{8,24},{16,0},{24,8},{1,17},{9,25},{17,1},{25,9},{2,18},{10... | collective-permute-start | bytes 786440 | tf_op jit(solution)/shard_map/ppermute | solution.py:31
  21.3 7.9 %collective-permute-done.3.refs_2_ = bf16[256,512]{1,0:T(8,128)(2,1)S(1)} collective-permute-done((bf16[256,512]{1,0:T(8,128)(2,1)S(1)}, bf16[256,512]{1,0:T(8,128)(2,1)S(1)}, u32[]{:S(2)}, u32[]{:S(2)}) %collective-permute-start.3) | collective-permute-done | bytes 262176 | tf_op jit(solution)/shard_map/ppermute | solution.py:31
  31.3 2.8 %collective-permute-start.5 = (bf16[2,32,2048]{2,1,0:T(8,128)(2,1)S(1)}, bf16[2,32,2048]{2,1,0:T(8,128)(2,1)S(1)}, u32[]{:S(2)}, u32[]{:S(2)}) collective-permute-start(bf16[2,32,2048]{2,1,0:T(8,128)(2,1)S(1)} %collective-permute-done.1), channel_id=1, source_target_pairs={{0,96},{32,0},{64,32},{96,64},{1,97},{33,1},{65,33},{97,65},{2,98}... | collective-permute-start | bytes 786440 | tf_op jit(solution)/shard_map/ppermute | solution.py:31
  40.5 3.8 %collective-permute-done.5 = bf16[2,32,2048]{2,1,0:T(8,128)(2,1)S(1)} collective-permute-done((bf16[2,32,2048]{2,1,0:T(8,128)(2,1)S(1)}, bf16[2,32,2048]{2,1,0:T(8,128)(2,1)S(1)}, u32[]{:S(2)}, u32[]{:S(2)}) %collective-permute-start.5) | collective-permute-done | bytes 262176 | tf_op jit(solution)/shard_map/ppermute | solution.py:31
  44.2 4.2 %collective-permute-start.11 = (bf16[1024,512]{1,0:T(8,128)(2,1)}, bf16[1024,512]{1,0:T(8,128)(2,1)S(1)}, u32[]{:S(2)}, u32[]{:S(2)}) collective-permute-start(bf16[1024,512]{1,0:T(8,128)(2,1)} %pad_maximum_fusion.1), channel_id=1, source_target_pairs={{0,96},{32,0},{64,32},{96,64},{1,97},{33,1},{65,33},{97,65},{2,98}... | collective-permute-start | bytes 3145736 | tf_op jit(solution)/shard_map/ppermute | solution.py:31
  55.6 2.3 %constant_dynamic-slice_fusion.5 = bf16[2,32,8192]{2,1,0:T(8,128)(2,1)} fusion(bf16[2,32,14336]{2,1,0:T(8,128)(2,1)} %constant_dynamic-update-slice_fusion, s32[]{:T(128)S(6)} %select_n.255), kind=kLoop, calls=%fused_computation.48 | loop fusion | bytes 2097156 | tf_op jit(solution)/shard_map/dynamic_slice | solution.py:358
  63.4 6.9 %collective-permute-done.9.refs_4_ = bf16[1024,512]{1,0:T(8,128)(2,1)S(1)} collective-permute-done((bf16[1024,512]{1,0:T(8,128)(2,1)}, bf16[1024,512]{1,0:T(8,128)(2,1)S(1)}, u32[]{:S(2)}, u32[]{:S(2)}) %collective-permute-start.9) | collective-permute-done | bytes 1048608 | tf_op jit(solution)/shard_map/ppermute | solution.py:31
  70.5 3.3 %collective-permute-start.12 = (bf16[512,512]{1,0:T(8,128)(2,1)S(1)}, bf16[512,512]{1,0:T(8,128)(2,1)S(1)}, u32[]{:S(2)}, u32[]{:S(2)}) collective-permute-start(bf16[512,512]{1,0:T(8,128)(2,1)S(1)} %slice.13), channel_id=1, source_target_pairs={{0,96},{32,0},{64,32},{96,64},{1,97},{33,1},{65,33},{97,65},{2,98}... | collective-permute-start | bytes 1572872 | tf_op jit(solution)/shard_map/ppermute | solution.py:31
  73.7 3.3 %select_bitcast_fusion.3 = (bf16[2,1,32,8192]{3,2,0,1:T(8,128)(2,1)S(1)}, bf16[2,1,32,8192]{3,2,0,1:T(8,128)(2,1)S(1)}, bf16[2,1,32,8192]{3,2,0,1:T(8,128)(2,1)S(1)}, bf16[2,1,32,8192]{3,2,0,1:T(8,128)(2,1)S(1)}) fusion(pred[]{:T(512)S(6)} %eq.86, bf16[2,32,8192]{2,1,0:T(8,128)(2,1)} %collective-permute-done, pred[]{:T(512)S(6)} %eq.87, ...), kind=kLoop, calls=%fused_computation.9 | loop fusion | flops 4194304 | bytes 8388614 | tf_op jit(solution)/shard_map/stack | solution.py:370
  77.6 2.3 %copy.12 = bf16[2,4,32,8192]{3,2,1,0:T(8,128)(2,1)} copy(bf16[2,4,32,8192]{3,2,0,1:T(8,128)(2,1)S(1)} %pad_maximum_fusion) | data formatting | bytes 8388608 | tf_op jit(solution)/shard_map/stack | solution.py:370
  79.9 5.6 %collective-permute-done.10.refs_5_ = bf16[512,512]{1,0:T(8,128)(2,1)S(1)} collective-permute-done((bf16[512,512]{1,0:T(8,128)(2,1)S(1)}, bf16[512,512]{1,0:T(8,128)(2,1)S(1)}, u32[]{:S(2)}, u32[]{:S(2)}) %collective-permute-start.10) | collective-permute-done | bytes 524320 | tf_op jit(solution)/shard_map/ppermute | solution.py:31
  87.0 5.9 %project_key_value.1.kv0 = bf16[2,2,128,128]{3,2,1,0:T(8,128)(2,1)} custom-call(s32[1]{0:T(128)} %bitcast.18.place, bf16[32,1040,256]{2,1,0:T(8,128)(2,1)} %bitcast.39, bf16[32,1040,256]{2,1,0:T(8,128)(2,1)} %bitcast.40, bf16[256,8192]{1,0:T(8,128)(2,1)} %bitcast.45, f32[1024,128]{1,0:T(8,128)} %get-tuple-element.98.cosine, f32[1024,128]{1,0:T(8,128)} %get-tuple-element.99.sine), custom_call_target="tpu_custom_call" | custom-call | flops 1073741824 | bytes 8388608 | tf_op jit(solution)/shard_map/project_key_value/pallas_call | solution.py:103
  94.6 7.7 %project_query.2.queries = bf16[512,256]{1,0:T(8,128)(2,1)} custom-call(bf16[32,1040,256]{2,1,0:T(8,128)(2,1)} %bitcast.41, bf16[32,1040,256]{2,1,0:T(8,128)(2,1)} %bitcast.42, bf16[8192,256]{1,0:T(8,128)(2,1)} %weights.3, f32[1024,128]{1,0:T(8,128)} %get-tuple-element.98.cosine, f32[1024,128]{1,0:T(8,128)} %get-tuple-element.99.sine), custom_call_target="tpu_custom_call" | custom-call | flops 2147483648 | bytes 12582912 | tf_op jit(solution)/shard_map/project_query/pallas_call | solution.py:151
  104.5 3.9 %attend.2.refs_8_ = bf16[512,256]{1,0:T(8,128)(2,1)} custom-call(s32[8]{0:T(128)} %concatenate.22.scalars, bf16[512,256]{1,0:T(8,128)(2,1)} %project_query.2.queries, bf16[2,2,128,128]{3,2,1,0:T(8,128)(2,1)} %project_key_value.1.kv0, bf16[2,2,128,128]{3,2,1,0:T(8,128)(2,1)} %copy-done.13, bf16[2,2,128,128]{3,2,1,0:T(8,128)(2,1)} %copy-done.12, ...), custom_call_target="tpu_custom_call" | custom-call | flops 1024 | bytes 1024 | tf_op jit(solution)/shard_map/attend/pallas_call | solution.py:210
  108.7 4.1 %collective-permute-start.17 = (bf16[512,256]{1,0:T(8,128)(2,1)}, bf16[512,256]{1,0:T(8,128)(2,1)S(1)}, u32[]{:S(2)}, u32[]{:S(2)}) collective-permute-start(bf16[512,256]{1,0:T(8,128)(2,1)} %attend.2.refs_8_), channel_id=1, source_target_pairs={{0,16},{8,24},{16,0},{24,8},{1,17},{9,25},{17,1},{25,9},{2,18},{10... | collective-permute-start | bytes 786440 | tf_op jit(solution)/shard_map/ppermute | solution.py:31
  112.8 7.7 %project_query.3.queries = bf16[512,256]{1,0:T(8,128)(2,1)} custom-call(bf16[32,1040,256]{2,1,0:T(8,128)(2,1)} %bitcast.43, bf16[32,1040,256]{2,1,0:T(8,128)(2,1)} %bitcast.44, bf16[8192,256]{1,0:T(8,128)(2,1)} %weights.3, f32[1024,128]{1,0:T(8,128)} %get-tuple-element.98.cosine, f32[1024,128]{1,0:T(8,128)} %get-tuple-element.99.sine), custom_call_target="tpu_custom_call" | custom-call | flops 2147483648 | bytes 12582912 | tf_op jit(solution)/shard_map/project_query/pallas_call | solution.py:151
  120.5 4.4 %attend.3.refs_8_ = bf16[512,256]{1,0:T(8,128)(2,1)} custom-call(s32[8]{0:T(128)} %concatenate.22.scalars, bf16[512,256]{1,0:T(8,128)(2,1)} %project_query.3.queries, bf16[2,2,128,128]{3,2,1,0:T(8,128)(2,1)} %project_key_value.1.kv0, bf16[2,2,128,128]{3,2,1,0:T(8,128)(2,1)} %copy-done.13, bf16[2,2,128,128]{3,2,1,0:T(8,128)(2,1)} %copy-done.12, ...), custom_call_target="tpu_custom_call" | custom-call | flops 1024 | bytes 1024 | tf_op jit(solution)/shard_map/attend/pallas_call | solution.py:210
  124.9 2.0 %collective-permute-start.23 = (bf16[512,256]{1,0:T(8,128)(2,1)}, bf16[512,256]{1,0:T(8,128)(2,1)S(1)}, u32[]{:S(2)}, u32[]{:S(2)}) collective-permute-start(bf16[512,256]{1,0:T(8,128)(2,1)} %attend.3.refs_8_), channel_id=1, source_target_pairs={{0,8},{8,16},{16,24},{24,0},{1,9},{9,17},{17,25},{25,1},{2,10},{10... | collective-permute-start | bytes 786440 | tf_op jit(solution)/shard_map/ppermute | solution.py:31
  127.0 2.6 %collective-permute-start.25 = (bf16[512,256]{1,0:T(8,128)(2,1)}, bf16[512,256]{1,0:T(8,128)(2,1)S(1)}, u32[]{:S(2)}, u32[]{:S(2)}) collective-permute-start(bf16[512,256]{1,0:T(8,128)(2,1)} %attend.3.refs_8_), channel_id=1, source_target_pairs={{0,24},{8,0},{16,8},{24,16},{1,25},{9,1},{17,9},{25,17},{2,26},{10... | collective-permute-start | bytes 786440 | tf_op jit(solution)/shard_map/ppermute | solution.py:31
  131.0 7.6 %project_out.2 = (bf16[4,512,256]{2,1,0:T(8,128)(2,1)}, bf16[1,512,256]{2,1,0:T(8,128)(2,1)}, bf16[1,512,256]{2,1,0:T(8,128)(2,1)}, bf16[1,512,256]{2,1,0:T(8,128)(2,1)}, bf16[1,512,256]{2,1,0:T(8,128)(2,1)}) custom-call(s32[5]{0:T(128)} %stack.77.scalars, bf16[256,512]{1,0:T(8,128)(2,1)} %copy-done.4, bf16[256,512]{1,0:T(8,128)(2,1)} %copy-done.6, ...), custom_call_target="tpu_custom_call" | custom-call | flops 1024 | bytes 1024 | tf_op jit(solution)/shard_map/project_out/pallas_call | solution.py:267
  139.1 2.4 %collective-permute-done.23.refs_9_ = bf16[512,256]{1,0:T(8,128)(2,1)S(1)} collective-permute-done((bf16[512,256]{1,0:T(8,128)(2,1)}, bf16[512,256]{1,0:T(8,128)(2,1)S(1)}, u32[]{:S(2)}, u32[]{:S(2)}) %collective-permute-start.23) | collective-permute-done | bytes 262176 | tf_op jit(solution)/shard_map/ppermute | solution.py:31
  141.6 4.2 %collective-permute-done.24.refs_10_ = bf16[512,256]{1,0:T(8,128)(2,1)S(1)} collective-permute-done((bf16[512,256]{1,0:T(8,128)(2,1)}, bf16[512,256]{1,0:T(8,128)(2,1)S(1)}, u32[]{:S(2)}, u32[]{:S(2)}) %collective-permute-start.24) | collective-permute-done | bytes 262176 | tf_op jit(solution)/shard_map/ppermute | solution.py:31
  148.3 7.9 %project_out.3 = (bf16[4,512,256]{2,1,0:T(8,128)(2,1)}, bf16[1,512,256]{2,1,0:T(8,128)(2,1)}, bf16[1,512,256]{2,1,0:T(8,128)(2,1)}, bf16[1,512,256]{2,1,0:T(8,128)(2,1)}, bf16[1,512,256]{2,1,0:T(8,128)(2,1)}) custom-call(s32[5]{0:T(128)} %stack.77.scalars, bf16[256,512]{1,0:T(8,128)(2,1)} %copy-done.4, bf16[256,512]{1,0:T(8,128)(2,1)} %copy-done.6, ...), custom_call_target="tpu_custom_call" | custom-call | flops 1024 | bytes 1024 | tf_op jit(solution)/shard_map/project_out/pallas_call | solution.py:267
  157.3 2.6 %add_cores.2 = (bf16[512,256]{1,0:T(8,128)(2,1)}, bf16[512,256]{1,0:T(8,128)(2,1)}, bf16[512,256]{1,0:T(8,128)(2,1)}, bf16[512,256]{1,0:T(8,128)(2,1)}) custom-call(bf16[4,512,256]{2,1,0:T(8,128)(2,1)} %get-tuple-element.110.keep, bf16[1,512,256]{2,1,0:T(8,128)(2,1)} %copy-done.17, bf16[1,512,256]{2,1,0:T(8,128)(2,1)} %copy-done.18, ...), custom_call_target="tpu_custom_call" | custom-call | flops 1024 | bytes 1024 | tf_op jit(solution)/shard_map/add_cores/pallas_call | solution.py:292
  163.6 2.0 %collective-permute-start.28 = (bf16[512,256]{1,0:T(8,128)(2,1)}, bf16[512,256]{1,0:T(8,128)(2,1)S(1)}, u32[]{:S(2)}, u32[]{:S(2)}) collective-permute-start(bf16[512,256]{1,0:T(8,128)(2,1)} %get-tuple-element.122), channel_id=1, source_target_pairs={{0,6},{2,0},{4,2},{6,4},{1,7},{3,1},{5,3},{7,5},{8,14},{10,8},{12,... | collective-permute-start | bytes 786440 | tf_op jit(solution)/shard_map/ppermute | solution.py:31
  165.6 2.5 %pick_blocks.1 = (bf16[2,2,128,128]{3,2,1,0:T(8,128)(2,1)}, bf16[2,2,128,128]{3,2,1,0:T(8,128)(2,1)}, bf16[2,2,128,128]{3,2,1,0:T(8,128)(2,1)}, bf16[2,2,128,128]{3,2,1,0:T(8,128)(2,1)}) custom-call(s32[8]{0:T(128)} %reduce_sum.42.index, s32[8]{0:T(128)} %reduce_sum.44.valid, bf16[64,2,128,128]{3,2,1,0:T(8,128)(2,1)} %all-gather.7.cloned.1.call-done.blocks), custom_call_target="tpu_custom_call" | custom-call | flops 1024 | bytes 1024 | tf_op jit(solution)/shard_map/pick_blocks/pallas_call | solution.py:326
  168.9 2.5 %add_cores.3 = (bf16[512,256]{1,0:T(8,128)(2,1)}, bf16[512,256]{1,0:T(8,128)(2,1)}, bf16[512,256]{1,0:T(8,128)(2,1)}, bf16[512,256]{1,0:T(8,128)(2,1)}) custom-call(bf16[4,512,256]{2,1,0:T(8,128)(2,1)} %get-tuple-element.127.keep, bf16[1,512,256]{2,1,0:T(8,128)(2,1)} %copy-done.19, bf16[1,512,256]{2,1,0:T(8,128)(2,1)} %copy-done.21, ...), custom_call_target="tpu_custom_call" | custom-call | flops 1024 | bytes 1024 | tf_op jit(solution)/shard_map/add_cores/pallas_call | solution.py:292
  172.6 2.7 %collective-permute-start.34 = (bf16[512,256]{1,0:T(8,128)(2,1)}, bf16[512,256]{1,0:T(8,128)(2,1)S(1)}, u32[]{:S(2)}, u32[]{:S(2)}) collective-permute-start(bf16[512,256]{1,0:T(8,128)(2,1)} %get-tuple-element.144), channel_id=1, source_target_pairs={{0,4},{2,6},{4,0},{6,2},{1,5},{3,7},{5,1},{7,3},{8,12},{10,14},{12... | collective-permute-start | bytes 786440 | tf_op jit(solution)/shard_map/ppermute | solution.py:31
  176.6 2.6 %collective-permute-start.37 = (bf16[2,2,128,128]{3,2,1,0:T(8,128)(2,1)S(1)}, bf16[2,2,128,128]{3,2,1,0:T(8,128)(2,1)S(1)}, u32[]{:S(2)}, u32[]{:S(2)}) collective-permute-start(bf16[2,2,128,128]{3,2,1,0:T(8,128)(2,1)S(1)} %copy-done.34), channel_id=1, source_target_pairs={{0,64},{32,96},{64,0},{96,32},{1,65},{33,97},{65,1},{97,33},{2,66}... | collective-permute-start | bytes 393224 | tf_op jit(solution)/shard_map/ppermute | solution.py:31
  180.0 3.1 %collective-permute-done.37 = bf16[2,2,128,128]{3,2,1,0:T(8,128)(2,1)S(1)} collective-permute-done((bf16[2,2,128,128]{3,2,1,0:T(8,128)(2,1)S(1)}, bf16[2,2,128,128]{3,2,1,0:T(8,128)(2,1)S(1)}, u32[]{:S(2)}, u32[]{:S(2)}) %collective-permute-start.37) | collective-permute-done | bytes 131104 | tf_op jit(solution)/shard_map/ppermute | solution.py:31
  (179 shorter events, 53.5 us)
Async XLA Ops:
  7.2 79.9 %all-gather.5.cloned.1.call-start = ((), (), s32[]{:S(2)}) async-start(), calls=%async_computation | async-start | bytes 17571840 | tf_op jit(solution)/shard_map/all_gather | solution.py:404
  9.3 156.2 %all-gather.7.cloned.1.call-start = ((), (), s32[]{:S(2)}) async-start(), calls=%async_computation.1 | async-start | bytes 4325376 | tf_op jit(solution)/shard_map/all_gather | solution.py:431
  10.8 10.5 %collective-permute-start.2 = (bf16[256,512]{1,0:T(8,128)(2,1)S(1)}, bf16[256,512]{1,0:T(8,128)(2,1)S(1)}, u32[]{:S(2)}, u32[]{:S(2)}) collective-permute-start(bf16[256,512]{1,0:T(8,128)(2,1)S(1)} %get-tuple-element.169), channel_id=1, source_target_pairs={{0,8},{8,16},{16,24},{24,0},{1,9},{9,17},{17,25},{25,1},{2,10},{10... | collective-permute-start | bytes 786440 | tf_op jit(solution)/shard_map/ppermute | solution.py:31
  12.8 16.3 %collective-permute-start.3 = (bf16[256,512]{1,0:T(8,128)(2,1)S(1)}, bf16[256,512]{1,0:T(8,128)(2,1)S(1)}, u32[]{:S(2)}, u32[]{:S(2)}) collective-permute-start(bf16[256,512]{1,0:T(8,128)(2,1)S(1)} %get-tuple-element.171), channel_id=1, source_target_pairs={{0,16},{8,24},{16,0},{24,8},{1,17},{9,25},{17,1},{25,9},{2,18},{10... | collective-permute-start | bytes 786440 | tf_op jit(solution)/shard_map/ppermute | solution.py:31
  16.4 13.8 %collective-permute-start.4 = (bf16[256,512]{1,0:T(8,128)(2,1)S(1)}, bf16[256,512]{1,0:T(8,128)(2,1)S(1)}, u32[]{:S(2)}, u32[]{:S(2)}) collective-permute-start(bf16[256,512]{1,0:T(8,128)(2,1)S(1)} %get-tuple-element.170), channel_id=1, source_target_pairs={{0,24},{8,0},{16,8},{24,16},{1,25},{9,1},{17,9},{25,17},{2,26},{10... | collective-permute-start | bytes 786440 | tf_op jit(solution)/shard_map/ppermute | solution.py:31
  18.4 12.9 %collective-permute-start.1 = (bf16[2,32,2048]{2,1,0:T(8,128)(2,1)S(1)}, bf16[2,32,2048]{2,1,0:T(8,128)(2,1)S(1)}, u32[]{:S(2)}, u32[]{:S(2)}) collective-permute-start(bf16[2,32,2048]{2,1,0:T(8,128)(2,1)S(1)} %dynamic-slice_bitcast_fusion), channel_id=1, source_target_pairs={{0,2},{2,0},{4,6},{6,4},{1,3},{3,1},{5,7},{7,5},{8,10},{10,8},{12,... | collective-permute-start | bytes 786440 | tf_op jit(solution)/shard_map/ppermute | solution.py:353
  20.0 53.7 %collective-permute-start = (bf16[2,32,8192]{2,1,0:T(8,128)(2,1)}, bf16[2,32,8192]{2,1,0:T(8,128)(2,1)}, u32[]{:S(2)}, u32[]{:S(2)}) collective-permute-start(bf16[2,32,8192]{2,1,0:T(8,128)(2,1)} %bitcast.1), channel_id=1, source_target_pairs={{0,1},{1,0},{2,3},{3,2},{4,5},{5,4},{6,7},{7,6},{8,9},{9,8},{10,11... | collective-permute-start | bytes 3145736 | tf_op jit(solution)/shard_map/ppermute | solution.py:35
  31.3 13.0 %collective-permute-start.5 = (bf16[2,32,2048]{2,1,0:T(8,128)(2,1)S(1)}, bf16[2,32,2048]{2,1,0:T(8,128)(2,1)S(1)}, u32[]{:S(2)}, u32[]{:S(2)}) collective-permute-start(bf16[2,32,2048]{2,1,0:T(8,128)(2,1)S(1)} %collective-permute-done.1), channel_id=1, source_target_pairs={{0,96},{32,0},{64,32},{96,64},{1,97},{33,1},{65,33},{97,65},{2,98}... | collective-permute-start | bytes 786440 | tf_op jit(solution)/shard_map/ppermute | solution.py:31
  34.1 15.0 %collective-permute-start.6 = (bf16[2,32,2048]{2,1,0:T(8,128)(2,1)S(1)}, bf16[2,32,2048]{2,1,0:T(8,128)(2,1)}, u32[]{:S(2)}, u32[]{:S(2)}) collective-permute-start(bf16[2,32,2048]{2,1,0:T(8,128)(2,1)S(1)} %collective-permute-done.1), channel_id=1, source_target_pairs={{0,64},{32,96},{64,0},{96,32},{1,65},{33,97},{65,1},{97,33},{2,66}... | collective-permute-start | bytes 786440 | tf_op jit(solution)/shard_map/ppermute | solution.py:31
  34.8 16.0 %collective-permute-start.7 = (bf16[2,32,2048]{2,1,0:T(8,128)(2,1)S(1)}, bf16[2,32,2048]{2,1,0:T(8,128)(2,1)}, u32[]{:S(2)}, u32[]{:S(2)}) collective-permute-start(bf16[2,32,2048]{2,1,0:T(8,128)(2,1)S(1)} %collective-permute-done.1), channel_id=1, source_target_pairs={{0,32},{32,64},{64,96},{96,0},{1,33},{33,65},{65,97},{97,1},{2,34}... | collective-permute-start | bytes 786440 | tf_op jit(solution)/shard_map/ppermute | solution.py:31
  38.5 31.8 %collective-permute-start.9 = (bf16[1024,512]{1,0:T(8,128)(2,1)}, bf16[1024,512]{1,0:T(8,128)(2,1)S(1)}, u32[]{:S(2)}, u32[]{:S(2)}) collective-permute-start(bf16[1024,512]{1,0:T(8,128)(2,1)} %pad_maximum_fusion.1), channel_id=1, source_target_pairs={{0,32},{32,64},{64,96},{96,0},{1,33},{33,65},{65,97},{97,1},{2,34}... | collective-permute-start | bytes 3145736 | tf_op jit(solution)/shard_map/ppermute | solution.py:31
  44.2 26.2 %collective-permute-start.11 = (bf16[1024,512]{1,0:T(8,128)(2,1)}, bf16[1024,512]{1,0:T(8,128)(2,1)S(1)}, u32[]{:S(2)}, u32[]{:S(2)}) collective-permute-start(bf16[1024,512]{1,0:T(8,128)(2,1)} %pad_maximum_fusion.1), channel_id=1, source_target_pairs={{0,96},{32,0},{64,32},{96,64},{1,97},{33,1},{65,33},{97,65},{2,98}... | collective-permute-start | bytes 3145736 | tf_op jit(solution)/shard_map/ppermute | solution.py:31
  57.9 15.8 %collective-permute-start.8 = (bf16[2,32,8192]{2,1,0:T(8,128)(2,1)}, bf16[2,32,8192]{2,1,0:T(8,128)(2,1)}, u32[]{:S(2)}, u32[]{:S(2)}) collective-permute-start(bf16[2,32,8192]{2,1,0:T(8,128)(2,1)} %constant_dynamic-slice_fusion.5), channel_id=1, source_target_pairs={{0,1},{1,0},{2,3},{3,2},{4,5},{5,4},{6,7},{7,6},{8,9},{9,8},{10,11... | collective-permute-start | bytes 3145736 | tf_op jit(solution)/shard_map/ppermute | solution.py:35
  70.3 15.2 %collective-permute-start.10 = (bf16[512,512]{1,0:T(8,128)(2,1)S(1)}, bf16[512,512]{1,0:T(8,128)(2,1)S(1)}, u32[]{:S(2)}, u32[]{:S(2)}) collective-permute-start(bf16[512,512]{1,0:T(8,128)(2,1)S(1)} %slice.12), channel_id=1, source_target_pairs={{0,32},{32,64},{64,96},{96,0},{1,33},{33,65},{65,97},{97,1},{2,34}... | collective-permute-start | bytes 1572872 | tf_op jit(solution)/shard_map/ppermute | solution.py:31
  70.5 15.1 %collective-permute-start.12 = (bf16[512,512]{1,0:T(8,128)(2,1)S(1)}, bf16[512,512]{1,0:T(8,128)(2,1)S(1)}, u32[]{:S(2)}, u32[]{:S(2)}) collective-permute-start(bf16[512,512]{1,0:T(8,128)(2,1)S(1)} %slice.13), channel_id=1, source_target_pairs={{0,96},{32,0},{64,32},{96,64},{1,97},{33,1},{65,33},{97,65},{2,98}... | collective-permute-start | bytes 1572872 | tf_op jit(solution)/shard_map/ppermute | solution.py:31
  93.0 9.3 %collective-permute-start.13 = (bf16[2,2,128,128]{3,2,1,0:T(8,128)(2,1)}, bf16[2,2,128,128]{3,2,1,0:T(8,128)(2,1)S(1)}, u32[]{:S(2)}, u32[]{:S(2)}) collective-permute-start(bf16[2,2,128,128]{3,2,1,0:T(8,128)(2,1)} %project_key_value.1.kv0), channel_id=1, source_target_pairs={{0,2},{2,0},{4,6},{6,4},{1,3},{3,1},{5,7},{7,5},{8,10},{10,8},{12,... | collective-permute-start | bytes 393224 | tf_op jit(solution)/shard_map/ppermute | solution.py:432
  108.4 18.5 %collective-permute-start.16 = (bf16[512,256]{1,0:T(8,128)(2,1)}, bf16[512,256]{1,0:T(8,128)(2,1)S(1)}, u32[]{:S(2)}, u32[]{:S(2)}) collective-permute-start(bf16[512,256]{1,0:T(8,128)(2,1)} %attend.2.refs_8_), channel_id=1, source_target_pairs={{0,8},{8,16},{16,24},{24,0},{1,9},{9,17},{17,25},{25,1},{2,10},{10... | collective-permute-start | bytes 786440 | tf_op jit(solution)/shard_map/ppermute | solution.py:31
  108.7 20.9 %collective-permute-start.17 = (bf16[512,256]{1,0:T(8,128)(2,1)}, bf16[512,256]{1,0:T(8,128)(2,1)S(1)}, u32[]{:S(2)}, u32[]{:S(2)}) collective-permute-start(bf16[512,256]{1,0:T(8,128)(2,1)} %attend.2.refs_8_), channel_id=1, source_target_pairs={{0,16},{8,24},{16,0},{24,8},{1,17},{9,25},{17,1},{25,9},{2,18},{10... | collective-permute-start | bytes 786440 | tf_op jit(solution)/shard_map/ppermute | solution.py:31
  112.8 16.8 %collective-permute-start.18 = (bf16[512,256]{1,0:T(8,128)(2,1)}, bf16[512,256]{1,0:T(8,128)(2,1)S(1)}, u32[]{:S(2)}, u32[]{:S(2)}) collective-permute-start(bf16[512,256]{1,0:T(8,128)(2,1)} %attend.2.refs_8_), channel_id=1, source_target_pairs={{0,24},{8,0},{16,8},{24,16},{1,25},{9,1},{17,9},{25,17},{2,26},{10... | collective-permute-start | bytes 786440 | tf_op jit(solution)/shard_map/ppermute | solution.py:31
  124.9 16.6 %collective-permute-start.23 = (bf16[512,256]{1,0:T(8,128)(2,1)}, bf16[512,256]{1,0:T(8,128)(2,1)S(1)}, u32[]{:S(2)}, u32[]{:S(2)}) collective-permute-start(bf16[512,256]{1,0:T(8,128)(2,1)} %attend.3.refs_8_), channel_id=1, source_target_pairs={{0,8},{8,16},{16,24},{24,0},{1,9},{9,17},{17,25},{25,1},{2,10},{10... | collective-permute-start | bytes 786440 | tf_op jit(solution)/shard_map/ppermute | solution.py:31
  126.9 18.9 %collective-permute-start.24 = (bf16[512,256]{1,0:T(8,128)(2,1)}, bf16[512,256]{1,0:T(8,128)(2,1)S(1)}, u32[]{:S(2)}, u32[]{:S(2)}) collective-permute-start(bf16[512,256]{1,0:T(8,128)(2,1)} %attend.3.refs_8_), channel_id=1, source_target_pairs={{0,16},{8,24},{16,0},{24,8},{1,17},{9,25},{17,1},{25,9},{2,18},{10... | collective-permute-start | bytes 786440 | tf_op jit(solution)/shard_map/ppermute | solution.py:31
  127.0 20.6 %collective-permute-start.25 = (bf16[512,256]{1,0:T(8,128)(2,1)}, bf16[512,256]{1,0:T(8,128)(2,1)S(1)}, u32[]{:S(2)}, u32[]{:S(2)}) collective-permute-start(bf16[512,256]{1,0:T(8,128)(2,1)} %attend.3.refs_8_), channel_id=1, source_target_pairs={{0,24},{8,0},{16,8},{24,16},{1,25},{9,1},{17,9},{25,17},{2,26},{10... | collective-permute-start | bytes 786440 | tf_op jit(solution)/shard_map/ppermute | solution.py:31
  138.6 8.9 %collective-permute-start.19 = (bf16[1,512,256]{2,1,0:T(8,128)(2,1)}, bf16[1,512,256]{2,1,0:T(8,128)(2,1)S(1)}, u32[]{:S(2)}, u32[]{:S(2)}) collective-permute-start(bf16[1,512,256]{2,1,0:T(8,128)(2,1)} %get-tuple-element.111), channel_id=1, source_target_pairs={{0,1},{1,0},{2,3},{3,2},{4,5},{5,4},{6,7},{7,6},{8,9},{9,8},{10,11... | collective-permute-start | bytes 786440 | tf_op jit(solution)/shard_map/ppermute | solution.py:35
  138.6 8.9 %collective-permute-start.20 = (bf16[1,512,256]{2,1,0:T(8,128)(2,1)}, bf16[1,512,256]{2,1,0:T(8,128)(2,1)S(1)}, u32[]{:S(2)}, u32[]{:S(2)}) collective-permute-start(bf16[1,512,256]{2,1,0:T(8,128)(2,1)} %get-tuple-element.112), channel_id=1, source_target_pairs={{0,1},{1,0},{2,3},{3,2},{4,5},{5,4},{6,7},{7,6},{8,9},{9,8},{10,11... | collective-permute-start | bytes 786440 | tf_op jit(solution)/shard_map/ppermute | solution.py:35
  156.8 11.3 %collective-permute-start.31 = (bf16[1,512,256]{2,1,0:T(8,128)(2,1)}, bf16[1,512,256]{2,1,0:T(8,128)(2,1)S(1)}, u32[]{:S(2)}, u32[]{:S(2)}) collective-permute-start(bf16[1,512,256]{2,1,0:T(8,128)(2,1)} %get-tuple-element.130), channel_id=1, source_target_pairs={{0,1},{1,0},{2,3},{3,2},{4,5},{5,4},{6,7},{7,6},{8,9},{9,8},{10,11... | collective-permute-start | bytes 786440 | tf_op jit(solution)/shard_map/ppermute | solution.py:35
  156.9 11.3 %collective-permute-start.32 = (bf16[1,512,256]{2,1,0:T(8,128)(2,1)}, bf16[1,512,256]{2,1,0:T(8,128)(2,1)S(1)}, u32[]{:S(2)}, u32[]{:S(2)}) collective-permute-start(bf16[1,512,256]{2,1,0:T(8,128)(2,1)} %get-tuple-element.131), channel_id=1, source_target_pairs={{0,1},{1,0},{2,3},{3,2},{4,5},{5,4},{6,7},{7,6},{8,9},{9,8},{10,11... | collective-permute-start | bytes 786440 | tf_op jit(solution)/shard_map/ppermute | solution.py:35
  159.9 12.8 %collective-permute-start.26 = (bf16[512,256]{1,0:T(8,128)(2,1)}, bf16[512,256]{1,0:T(8,128)(2,1)S(1)}, u32[]{:S(2)}, u32[]{:S(2)}) collective-permute-start(bf16[512,256]{1,0:T(8,128)(2,1)} %get-tuple-element.120), channel_id=1, source_target_pairs={{0,2},{2,4},{4,6},{6,0},{1,3},{3,5},{5,7},{7,1},{8,10},{10,12},{12... | collective-permute-start | bytes 786440 | tf_op jit(solution)/shard_map/ppermute | solution.py:31
  161.8 14.8 %collective-permute-start.27 = (bf16[512,256]{1,0:T(8,128)(2,1)}, bf16[512,256]{1,0:T(8,128)(2,1)S(1)}, u32[]{:S(2)}, u32[]{:S(2)}) collective-permute-start(bf16[512,256]{1,0:T(8,128)(2,1)} %get-tuple-element.121), channel_id=1, source_target_pairs={{0,4},{2,6},{4,0},{6,2},{1,5},{3,7},{5,1},{7,3},{8,12},{10,14},{12... | collective-permute-start | bytes 786440 | tf_op jit(solution)/shard_map/ppermute | solution.py:31
  163.6 13.0 %collective-permute-start.28 = (bf16[512,256]{1,0:T(8,128)(2,1)}, bf16[512,256]{1,0:T(8,128)(2,1)S(1)}, u32[]{:S(2)}, u32[]{:S(2)}) collective-permute-start(bf16[512,256]{1,0:T(8,128)(2,1)} %get-tuple-element.122), channel_id=1, source_target_pairs={{0,6},{2,0},{4,2},{6,4},{1,7},{3,1},{5,3},{7,5},{8,14},{10,8},{12,... | collective-permute-start | bytes 786440 | tf_op jit(solution)/shard_map/ppermute | solution.py:31
  171.5 13.5 %collective-permute-start.33 = (bf16[512,256]{1,0:T(8,128)(2,1)}, bf16[512,256]{1,0:T(8,128)(2,1)S(1)}, u32[]{:S(2)}, u32[]{:S(2)}) collective-permute-start(bf16[512,256]{1,0:T(8,128)(2,1)} %get-tuple-element.143), channel_id=1, source_target_pairs={{0,2},{2,4},{4,6},{6,0},{1,3},{3,5},{5,7},{7,1},{8,10},{10,12},{12... | collective-permute-start | bytes 786440 | tf_op jit(solution)/shard_map/ppermute | solution.py:31
  172.6 14.3 %collective-permute-start.34 = (bf16[512,256]{1,0:T(8,128)(2,1)}, bf16[512,256]{1,0:T(8,128)(2,1)S(1)}, u32[]{:S(2)}, u32[]{:S(2)}) collective-permute-start(bf16[512,256]{1,0:T(8,128)(2,1)} %get-tuple-element.144), channel_id=1, source_target_pairs={{0,4},{2,6},{4,0},{6,2},{1,5},{3,7},{5,1},{7,3},{8,12},{10,14},{12... | collective-permute-start | bytes 786440 | tf_op jit(solution)/shard_map/ppermute | solution.py:31
  176.6 11.1 %collective-permute-start.35 = (bf16[512,256]{1,0:T(8,128)(2,1)}, bf16[512,256]{1,0:T(8,128)(2,1)S(1)}, u32[]{:S(2)}, u32[]{:S(2)}) collective-permute-start(bf16[512,256]{1,0:T(8,128)(2,1)} %get-tuple-element.145), channel_id=1, source_target_pairs={{0,6},{2,0},{4,2},{6,4},{1,7},{3,1},{5,3},{7,5},{8,14},{10,8},{12,... | collective-permute-start | bytes 786440 | tf_op jit(solution)/shard_map/ppermute | solution.py:31
  (45 other events, 347.0 us)
Sparse Core Ops, SparseCore 0:
  10.3 76.7 all-gather.4
  93.1 58.5 all-gather.6

commit v4 on v3

--- a/solution.py
+++ b/solution.py
@@ -59,7 +59,7 @@
     return pl.pallas_call(
         scale_kernel,
         out_shape=jax.ShapeDtypeStruct((SEQ + 16, COLS), bf16),
-        compiler_params=pltpu.CompilerParams(vmem_limit_bytes=56 << 20),
+        compiler_params=pltpu.CompilerParams(vmem_limit_bytes=60 << 20),
         name="scale_tokens",
     )(tokens, gain)
 
@@ -98,7 +98,7 @@
 
 
 def project_key_value(place, gathered, weights, cosine, sine):
-    per_step = 8
+    per_step = 16
     steps = 32 // per_step
     return pl.pallas_call(
         functools.partial(key_value_kernel, steps, per_step),
@@ -116,7 +116,7 @@
             scratch_shapes=[pltpu.VMEM((COLS, 2 * HEAD), f32)],
         ),
         out_shape=jax.ShapeDtypeStruct((2, 2, BLOCK, HEAD), bf16),
-        compiler_params=pltpu.CompilerParams(vmem_limit_bytes=56 << 20),
+        compiler_params=pltpu.CompilerParams(vmem_limit_bytes=60 << 20),
         cost_estimate=pl.CostEstimate(
             flops=2 * COLS * WIDTH * 256, bytes_accessed=8 << 20, transcendentals=0
         ),
@@ -146,7 +146,7 @@
 
 
 def project_query(chunk, gathered, weights, cosine, sine):
-    per_step = 8
+    per_step = 16
     steps = 32 // per_step
     return pl.pallas_call(
         functools.partial(query_kernel, chunk, steps, per_step),
@@ -161,7 +161,7 @@
         out_specs=pl.BlockSpec((CHUNK, COLS), lambda k: (0, 0)),
         out_shape=jax.ShapeDtypeStruct((CHUNK, COLS), bf16),
         scratch_shapes=[pltpu.VMEM((CHUNK, COLS), f32)],
-        compiler_params=pltpu.CompilerParams(vmem_limit_bytes=56 << 20),
+        compiler_params=pltpu.CompilerParams(vmem_limit_bytes=60 << 20),
         cost_estimate=pl.CostEstimate(
             flops=2 * CHUNK * WIDTH * 256, bytes_accessed=12 << 20, transcendentals=0
         ),
@@ -217,7 +217,7 @@
             scratch_shapes=[pltpu.VMEM((SEQ, HEAD), bf16), pltpu.VMEM((SEQ, HEAD), bf16)],
         ),
         out_shape=jax.ShapeDtypeStruct((CHUNK, COLS), bf16),
-        compiler_params=pltpu.CompilerParams(vmem_limit_bytes=56 << 20),
+        compiler_params=pltpu.CompilerParams(vmem_limit_bytes=60 << 20),
         cost_estimate=pl.CostEstimate(flops=1024, bytes_accessed=1024, transcendentals=0),
         name="attend",
     )(scalars, queries, *kvs)
@@ -275,7 +275,7 @@
         ),
         out_shape=[jax.ShapeDtypeStruct((4, CHUNK, COLS), bf16)]
         + [jax.ShapeDtypeStruct((1, CHUNK, COLS), bf16)] * 4,
-        compiler_params=pltpu.CompilerParams(vmem_limit_bytes=56 << 20),
+        compiler_params=pltpu.CompilerParams(vmem_limit_bytes=60 << 20),
         cost_estimate=pl.CostEstimate(flops=1024, bytes_accessed=1024, transcendentals=0),
         name="project_out",
     )(scalars, *arrays)
@@ -292,7 +292,7 @@
     return pl.pallas_call(
         add_kernel,
         out_shape=[jax.ShapeDtypeStruct((CHUNK, COLS), bf16)] * 4,
-        compiler_params=pltpu.CompilerParams(vmem_limit_bytes=56 << 20),
+        compiler_params=pltpu.CompilerParams(vmem_limit_bytes=60 << 20),
         cost_estimate=pl.CostEstimate(flops=1024, bytes_accessed=1024, transcendentals=0),
         name="add_cores",
     )(keep, *got)
@@ -333,7 +333,7 @@
             scratch_shapes=[pltpu.SemaphoreType.DMA((8,))],
         ),
         out_shape=[jax.ShapeDtypeStruct(shape, bf16)] * 4,
-        compiler_params=pltpu.CompilerParams(vmem_limit_bytes=56 << 20),
+        compiler_params=pltpu.CompilerParams(vmem_limit_bytes=60 << 20),
         cost_estimate=pl.CostEstimate(flops=1024, bytes_accessed=1024, transcendentals=0),
         name="pick_blocks",
     )(index, valid, blocks)

time: 197 us -> 196 us (level)
  transfers between devices with their start and end apart: 41 -> 41, of which waited for: 16 -> 16; matrix products, arithmetic and copies ran while one was open for 14% -> 14% of each run, Pallas kernels for 24% -> 23%
where the time goes in v4:
time: 196 us; the launch traced here: 195 us
  Pallas kernels  53.1 us (27%)
  starting transfers between devices  48 us (24%)
  waiting for transfers between devices  45.6 us (23%)
  local copies, waits for them, and re-layouts  22.7 us (12%)
  between operations  14.7 us (8%)
  other arithmetic  11 us (6%)
    ppermute x25, waiting for transfers between devices, shift(): return lax.ppermute(value, axis, SHIFT[distance])  43 us
    ppermute x25, starting transfers between devices, shift(): return lax.ppermute(value, axis, SHIFT[distance])  42.5 us
    pallas_call x2, Pallas kernels, project_out(): pl.pallas_call(out_kernel, grid_spec=pltpu.PrefetchScalarGridSpec(num_sca...  15.3 us
    pallas_call x2, Pallas kernels, project_query(): pl.pallas_call(functools.partial(query_kernel, chunk, steps, per_step), g...  14.6 us
    unnamed x78, local copies, waits for them, and re-layouts  9.8 us
    pallas_call x2, Pallas kernels, attend(): pl.pallas_call(functools.partial(attention_kernel, chunk), grid_spec=pltp...  8.34 us
    pallas_call x1, Pallas kernels, project_key_value(): pl.pallas_call(functools.partial(key_value_kernel, steps, per_step), grid...  5.26 us
    pallas_call x2, Pallas kernels, add_cores(): pl.pallas_call(add_kernel, out_shape=[jax.ShapeDtypeStruct((CHUNK, COLS),...  5.09 us
  transfers between devices with their start and end apart: 41, of which 16 were waited for; matrix products, arithmetic and copies ran while one was open for 14% of the time, Pallas kernels for 23%

profile of v4, /device:TPU:0, one launch (start us, length us, event | category | flops | bytes accessed | tf_op | source)
XLA Modules:
  0.0 195.1 jit_solution(16354218012391772275)
XLA Ops:
  7.2 2.1 %scale_tokens.1 = bf16[1040,256]{1,0:T(8,128)(2,1)} custom-call(bf16[1024,256]{1,0:T(8,128)(2,1)} %tokens.1, bf16[256]{0:T(256)(128)(2,1)} %gain.1), custom_call_target="tpu_custom_call" | custom-call | tf_op jit(solution)/shard_map/scale_tokens/pallas_call | solution.py:59
  10.8 2.1 %collective-permute-start.2 = (bf16[256,512]{1,0:T(8,128)(2,1)S(1)}, bf16[256,512]{1,0:T(8,128)(2,1)S(1)}, u32[]{:S(2)}, u32[]{:S(2)}) collective-permute-start(bf16[256,512]{1,0:T(8,128)(2,1)S(1)} %get-tuple-element.169), channel_id=1, source_target_pairs={{0,8},{8,16},{16,24},{24,0},{1,9},{9,17},{17,25},{25,1},{2,10},{10... | collective-permute-start | bytes 786440 | tf_op jit(solution)/shard_map/ppermute | solution.py:31
  12.8 3.6 %collective-permute-start.3 = (bf16[256,512]{1,0:T(8,128)(2,1)S(1)}, bf16[256,512]{1,0:T(8,128)(2,1)S(1)}, u32[]{:S(2)}, u32[]{:S(2)}) collective-permute-start(bf16[256,512]{1,0:T(8,128)(2,1)S(1)} %get-tuple-element.171), channel_id=1, source_target_pairs={{0,16},{8,24},{16,0},{24,8},{1,17},{9,25},{17,1},{25,9},{2,18},{10... | collective-permute-start | bytes 786440 | tf_op jit(solution)/shard_map/ppermute | solution.py:31
  21.3 7.9 %collective-permute-done.3.refs_2_ = bf16[256,512]{1,0:T(8,128)(2,1)S(1)} collective-permute-done((bf16[256,512]{1,0:T(8,128)(2,1)S(1)}, bf16[256,512]{1,0:T(8,128)(2,1)S(1)}, u32[]{:S(2)}, u32[]{:S(2)}) %collective-permute-start.3) | collective-permute-done | bytes 262176 | tf_op jit(solution)/shard_map/ppermute | solution.py:31
  31.3 2.8 %collective-permute-start.5 = (bf16[2,32,2048]{2,1,0:T(8,128)(2,1)S(1)}, bf16[2,32,2048]{2,1,0:T(8,128)(2,1)S(1)}, u32[]{:S(2)}, u32[]{:S(2)}) collective-permute-start(bf16[2,32,2048]{2,1,0:T(8,128)(2,1)S(1)} %collective-permute-done.1), channel_id=1, source_target_pairs={{0,96},{32,0},{64,32},{96,64},{1,97},{33,1},{65,33},{97,65},{2,98}... | collective-permute-start | bytes 786440 | tf_op jit(solution)/shard_map/ppermute | solution.py:31
  40.5 3.8 %collective-permute-done.5 = bf16[2,32,2048]{2,1,0:T(8,128)(2,1)S(1)} collective-permute-done((bf16[2,32,2048]{2,1,0:T(8,128)(2,1)S(1)}, bf16[2,32,2048]{2,1,0:T(8,128)(2,1)S(1)}, u32[]{:S(2)}, u32[]{:S(2)}) %collective-permute-start.5) | collective-permute-done | bytes 262176 | tf_op jit(solution)/shard_map/ppermute | solution.py:31
  44.2 4.2 %collective-permute-start.11 = (bf16[1024,512]{1,0:T(8,128)(2,1)}, bf16[1024,512]{1,0:T(8,128)(2,1)S(1)}, u32[]{:S(2)}, u32[]{:S(2)}) collective-permute-start(bf16[1024,512]{1,0:T(8,128)(2,1)} %pad_maximum_fusion.1), channel_id=1, source_target_pairs={{0,96},{32,0},{64,32},{96,64},{1,97},{33,1},{65,33},{97,65},{2,98}... | collective-permute-start | bytes 3145736 | tf_op jit(solution)/shard_map/ppermute | solution.py:31
  55.6 2.3 %constant_dynamic-slice_fusion.5 = bf16[2,32,8192]{2,1,0:T(8,128)(2,1)} fusion(bf16[2,32,14336]{2,1,0:T(8,128)(2,1)} %constant_dynamic-update-slice_fusion, s32[]{:T(128)S(6)} %select_n.255), kind=kLoop, calls=%fused_computation.48 | loop fusion | bytes 2097156 | tf_op jit(solution)/shard_map/dynamic_slice | solution.py:358
  63.4 6.9 %collective-permute-done.9.refs_4_ = bf16[1024,512]{1,0:T(8,128)(2,1)S(1)} collective-permute-done((bf16[1024,512]{1,0:T(8,128)(2,1)}, bf16[1024,512]{1,0:T(8,128)(2,1)S(1)}, u32[]{:S(2)}, u32[]{:S(2)}) %collective-permute-start.9) | collective-permute-done | bytes 1048608 | tf_op jit(solution)/shard_map/ppermute | solution.py:31
  70.5 3.3 %collective-permute-start.12 = (bf16[512,512]{1,0:T(8,128)(2,1)S(1)}, bf16[512,512]{1,0:T(8,128)(2,1)S(1)}, u32[]{:S(2)}, u32[]{:S(2)}) collective-permute-start(bf16[512,512]{1,0:T(8,128)(2,1)S(1)} %slice.13), channel_id=1, source_target_pairs={{0,96},{32,0},{64,32},{96,64},{1,97},{33,1},{65,33},{97,65},{2,98}... | collective-permute-start | bytes 1572872 | tf_op jit(solution)/shard_map/ppermute | solution.py:31
  73.7 3.3 %select_bitcast_fusion.3 = (bf16[2,1,32,8192]{3,2,0,1:T(8,128)(2,1)S(1)}, bf16[2,1,32,8192]{3,2,0,1:T(8,128)(2,1)S(1)}, bf16[2,1,32,8192]{3,2,0,1:T(8,128)(2,1)S(1)}, bf16[2,1,32,8192]{3,2,0,1:T(8,128)(2,1)S(1)}) fusion(pred[]{:T(512)S(6)} %eq.86, bf16[2,32,8192]{2,1,0:T(8,128)(2,1)} %collective-permute-done, pred[]{:T(512)S(6)} %eq.87, ...), kind=kLoop, calls=%fused_computation.9 | loop fusion | flops 4194304 | bytes 8388614 | tf_op jit(solution)/shard_map/stack | solution.py:370
  77.6 2.3 %copy.12 = bf16[2,4,32,8192]{3,2,1,0:T(8,128)(2,1)} copy(bf16[2,4,32,8192]{3,2,0,1:T(8,128)(2,1)S(1)} %pad_maximum_fusion) | data formatting | bytes 8388608 | tf_op jit(solution)/shard_map/stack | solution.py:370
  79.9 5.6 %collective-permute-done.10.refs_5_ = bf16[512,512]{1,0:T(8,128)(2,1)S(1)} collective-permute-done((bf16[512,512]{1,0:T(8,128)(2,1)S(1)}, bf16[512,512]{1,0:T(8,128)(2,1)S(1)}, u32[]{:S(2)}, u32[]{:S(2)}) %collective-permute-start.10) | collective-permute-done | bytes 524320 | tf_op jit(solution)/shard_map/ppermute | solution.py:31
  87.0 5.3 %project_key_value.1.kv0 = bf16[2,2,128,128]{3,2,1,0:T(8,128)(2,1)} custom-call(s32[1]{0:T(128)} %bitcast.18.place, bf16[32,1040,256]{2,1,0:T(8,128)(2,1)} %bitcast.39, bf16[32,1040,256]{2,1,0:T(8,128)(2,1)} %bitcast.40, bf16[256,8192]{1,0:T(8,128)(2,1)} %bitcast.45, f32[1024,128]{1,0:T(8,128)} %get-tuple-element.98.cosine, f32[1024,128]{1,0:T(8,128)} %get-tuple-element.99.sine), custom_call_target="tpu_custom_call" | custom-call | flops 1073741824 | bytes 8388608 | tf_op jit(solution)/shard_map/project_key_value/pallas_call | solution.py:103
  93.9 7.3 %project_query.2.queries = bf16[512,256]{1,0:T(8,128)(2,1)} custom-call(bf16[32,1040,256]{2,1,0:T(8,128)(2,1)} %bitcast.41, bf16[32,1040,256]{2,1,0:T(8,128)(2,1)} %bitcast.42, bf16[8192,256]{1,0:T(8,128)(2,1)} %weights.3, f32[1024,128]{1,0:T(8,128)} %get-tuple-element.98.cosine, f32[1024,128]{1,0:T(8,128)} %get-tuple-element.99.sine), custom_call_target="tpu_custom_call" | custom-call | flops 2147483648 | bytes 12582912 | tf_op jit(solution)/shard_map/project_query/pallas_call | solution.py:151
  103.4 3.9 %attend.2.refs_8_ = bf16[512,256]{1,0:T(8,128)(2,1)} custom-call(s32[8]{0:T(128)} %concatenate.22.scalars, bf16[512,256]{1,0:T(8,128)(2,1)} %project_query.2.queries, bf16[2,2,128,128]{3,2,1,0:T(8,128)(2,1)} %project_key_value.1.kv0, bf16[2,2,128,128]{3,2,1,0:T(8,128)(2,1)} %copy-done.13, bf16[2,2,128,128]{3,2,1,0:T(8,128)(2,1)} %copy-done.12, ...), custom_call_target="tpu_custom_call" | custom-call | flops 1024 | bytes 1024 | tf_op jit(solution)/shard_map/attend/pallas_call | solution.py:210
  107.6 4.1 %collective-permute-start.17 = (bf16[512,256]{1,0:T(8,128)(2,1)}, bf16[512,256]{1,0:T(8,128)(2,1)S(1)}, u32[]{:S(2)}, u32[]{:S(2)}) collective-permute-start(bf16[512,256]{1,0:T(8,128)(2,1)} %attend.2.refs_8_), channel_id=1, source_target_pairs={{0,16},{8,24},{16,0},{24,8},{1,17},{9,25},{17,1},{25,9},{2,18},{10... | collective-permute-start | bytes 786440 | tf_op jit(solution)/shard_map/ppermute | solution.py:31
  111.7 7.3 %project_query.3.queries = bf16[512,256]{1,0:T(8,128)(2,1)} custom-call(bf16[32,1040,256]{2,1,0:T(8,128)(2,1)} %bitcast.43, bf16[32,1040,256]{2,1,0:T(8,128)(2,1)} %bitcast.44, bf16[8192,256]{1,0:T(8,128)(2,1)} %weights.3, f32[1024,128]{1,0:T(8,128)} %get-tuple-element.98.cosine, f32[1024,128]{1,0:T(8,128)} %get-tuple-element.99.sine), custom_call_target="tpu_custom_call" | custom-call | flops 2147483648 | bytes 12582912 | tf_op jit(solution)/shard_map/project_query/pallas_call | solution.py:151
  119.1 4.4 %attend.3.refs_8_ = bf16[512,256]{1,0:T(8,128)(2,1)} custom-call(s32[8]{0:T(128)} %concatenate.22.scalars, bf16[512,256]{1,0:T(8,128)(2,1)} %project_query.3.queries, bf16[2,2,128,128]{3,2,1,0:T(8,128)(2,1)} %project_key_value.1.kv0, bf16[2,2,128,128]{3,2,1,0:T(8,128)(2,1)} %copy-done.13, bf16[2,2,128,128]{3,2,1,0:T(8,128)(2,1)} %copy-done.12, ...), custom_call_target="tpu_custom_call" | custom-call | flops 1024 | bytes 1024 | tf_op jit(solution)/shard_map/attend/pallas_call | solution.py:210
  123.5 2.0 %collective-permute-start.23 = (bf16[512,256]{1,0:T(8,128)(2,1)}, bf16[512,256]{1,0:T(8,128)(2,1)S(1)}, u32[]{:S(2)}, u32[]{:S(2)}) collective-permute-start(bf16[512,256]{1,0:T(8,128)(2,1)} %attend.3.refs_8_), channel_id=1, source_target_pairs={{0,8},{8,16},{16,24},{24,0},{1,9},{9,17},{17,25},{25,1},{2,10},{10... | collective-permute-start | bytes 786440 | tf_op jit(solution)/shard_map/ppermute | solution.py:31
  125.5 2.6 %collective-permute-start.25 = (bf16[512,256]{1,0:T(8,128)(2,1)}, bf16[512,256]{1,0:T(8,128)(2,1)S(1)}, u32[]{:S(2)}, u32[]{:S(2)}) collective-permute-start(bf16[512,256]{1,0:T(8,128)(2,1)} %attend.3.refs_8_), channel_id=1, source_target_pairs={{0,24},{8,0},{16,8},{24,16},{1,25},{9,1},{17,9},{25,17},{2,26},{10... | collective-permute-start | bytes 786440 | tf_op jit(solution)/shard_map/ppermute | solution.py:31
  129.6 7.6 %project_out.2 = (bf16[4,512,256]{2,1,0:T(8,128)(2,1)}, bf16[1,512,256]{2,1,0:T(8,128)(2,1)}, bf16[1,512,256]{2,1,0:T(8,128)(2,1)}, bf16[1,512,256]{2,1,0:T(8,128)(2,1)}, bf16[1,512,256]{2,1,0:T(8,128)(2,1)}) custom-call(s32[5]{0:T(128)} %stack.77.scalars, bf16[256,512]{1,0:T(8,128)(2,1)} %copy-done.4, bf16[256,512]{1,0:T(8,128)(2,1)} %copy-done.6, ...), custom_call_target="tpu_custom_call" | custom-call | flops 1024 | bytes 1024 | tf_op jit(solution)/shard_map/project_out/pallas_call | solution.py:267
  137.7 2.6 %collective-permute-done.23.refs_9_ = bf16[512,256]{1,0:T(8,128)(2,1)S(1)} collective-permute-done((bf16[512,256]{1,0:T(8,128)(2,1)}, bf16[512,256]{1,0:T(8,128)(2,1)S(1)}, u32[]{:S(2)}, u32[]{:S(2)}) %collective-permute-start.23) | collective-permute-done | bytes 262176 | tf_op jit(solution)/shard_map/ppermute | solution.py:31
  140.2 3.6 %collective-permute-done.24.refs_10_ = bf16[512,256]{1,0:T(8,128)(2,1)S(1)} collective-permute-done((bf16[512,256]{1,0:T(8,128)(2,1)}, bf16[512,256]{1,0:T(8,128)(2,1)S(1)}, u32[]{:S(2)}, u32[]{:S(2)}) %collective-permute-start.24) | collective-permute-done | bytes 262176 | tf_op jit(solution)/shard_map/ppermute | solution.py:31
  143.8 2.3 %collective-permute-done.25.refs_11_ = bf16[512,256]{1,0:T(8,128)(2,1)S(1)} collective-permute-done((bf16[512,256]{1,0:T(8,128)(2,1)}, bf16[512,256]{1,0:T(8,128)(2,1)S(1)}, u32[]{:S(2)}, u32[]{:S(2)}) %collective-permute-start.25) | collective-permute-done | bytes 262176 | tf_op jit(solution)/shard_map/ppermute | solution.py:31
  146.8 7.7 %project_out.3 = (bf16[4,512,256]{2,1,0:T(8,128)(2,1)}, bf16[1,512,256]{2,1,0:T(8,128)(2,1)}, bf16[1,512,256]{2,1,0:T(8,128)(2,1)}, bf16[1,512,256]{2,1,0:T(8,128)(2,1)}, bf16[1,512,256]{2,1,0:T(8,128)(2,1)}) custom-call(s32[5]{0:T(128)} %stack.77.scalars, bf16[256,512]{1,0:T(8,128)(2,1)} %copy-done.4, bf16[256,512]{1,0:T(8,128)(2,1)} %copy-done.6, ...), custom_call_target="tpu_custom_call" | custom-call | flops 1024 | bytes 1024 | tf_op jit(solution)/shard_map/project_out/pallas_call | solution.py:267
  155.6 2.6 %add_cores.2 = (bf16[512,256]{1,0:T(8,128)(2,1)}, bf16[512,256]{1,0:T(8,128)(2,1)}, bf16[512,256]{1,0:T(8,128)(2,1)}, bf16[512,256]{1,0:T(8,128)(2,1)}) custom-call(bf16[4,512,256]{2,1,0:T(8,128)(2,1)} %get-tuple-element.110.keep, bf16[1,512,256]{2,1,0:T(8,128)(2,1)} %copy-done.17, bf16[1,512,256]{2,1,0:T(8,128)(2,1)} %copy-done.18, ...), custom_call_target="tpu_custom_call" | custom-call | flops 1024 | bytes 1024 | tf_op jit(solution)/shard_map/add_cores/pallas_call | solution.py:292
  163.9 2.4 %pick_blocks.1 = (bf16[2,2,128,128]{3,2,1,0:T(8,128)(2,1)}, bf16[2,2,128,128]{3,2,1,0:T(8,128)(2,1)}, bf16[2,2,128,128]{3,2,1,0:T(8,128)(2,1)}, bf16[2,2,128,128]{3,2,1,0:T(8,128)(2,1)}) custom-call(s32[8]{0:T(128)} %reduce_sum.42.index, s32[8]{0:T(128)} %reduce_sum.44.valid, bf16[64,2,128,128]{3,2,1,0:T(8,128)(2,1)} %all-gather.7.cloned.1.call-done.blocks), custom_call_target="tpu_custom_call" | custom-call | flops 1024 | bytes 1024 | tf_op jit(solution)/shard_map/pick_blocks/pallas_call | solution.py:326
  167.2 2.5 %add_cores.3 = (bf16[512,256]{1,0:T(8,128)(2,1)}, bf16[512,256]{1,0:T(8,128)(2,1)}, bf16[512,256]{1,0:T(8,128)(2,1)}, bf16[512,256]{1,0:T(8,128)(2,1)}) custom-call(bf16[4,512,256]{2,1,0:T(8,128)(2,1)} %get-tuple-element.127.keep, bf16[1,512,256]{2,1,0:T(8,128)(2,1)} %copy-done.19, bf16[1,512,256]{2,1,0:T(8,128)(2,1)} %copy-done.21, ...), custom_call_target="tpu_custom_call" | custom-call | flops 1024 | bytes 1024 | tf_op jit(solution)/shard_map/add_cores/pallas_call | solution.py:292
  170.9 2.7 %collective-permute-start.34 = (bf16[512,256]{1,0:T(8,128)(2,1)}, bf16[512,256]{1,0:T(8,128)(2,1)S(1)}, u32[]{:S(2)}, u32[]{:S(2)}) collective-permute-start(bf16[512,256]{1,0:T(8,128)(2,1)} %get-tuple-element.144), channel_id=1, source_target_pairs={{0,4},{2,6},{4,0},{6,2},{1,5},{3,7},{5,1},{7,3},{8,12},{10,14},{12... | collective-permute-start | bytes 786440 | tf_op jit(solution)/shard_map/ppermute | solution.py:31
  174.9 2.5 %collective-permute-start.37 = (bf16[2,2,128,128]{3,2,1,0:T(8,128)(2,1)S(1)}, bf16[2,2,128,128]{3,2,1,0:T(8,128)(2,1)S(1)}, u32[]{:S(2)}, u32[]{:S(2)}) collective-permute-start(bf16[2,2,128,128]{3,2,1,0:T(8,128)(2,1)S(1)} %copy-done.34), channel_id=1, source_target_pairs={{0,64},{32,96},{64,0},{96,32},{1,65},{33,97},{65,1},{97,33},{2,66}... | collective-permute-start | bytes 393224 | tf_op jit(solution)/shard_map/ppermute | solution.py:31
  178.4 3.1 %collective-permute-done.37 = bf16[2,2,128,128]{3,2,1,0:T(8,128)(2,1)S(1)} collective-permute-done((bf16[2,2,128,128]{3,2,1,0:T(8,128)(2,1)S(1)}, bf16[2,2,128,128]{3,2,1,0:T(8,128)(2,1)S(1)}, u32[]{:S(2)}, u32[]{:S(2)}) %collective-permute-start.37) | collective-permute-done | bytes 131104 | tf_op jit(solution)/shard_map/ppermute | solution.py:31
  (179 shorter events, 53.8 us)
Async XLA Ops:
  7.2 79.9 %all-gather.5.cloned.1.call-start = ((), (), s32[]{:S(2)}) async-start(), calls=%async_computation | async-start | bytes 17571840 | tf_op jit(solution)/shard_map/all_gather | solution.py:404
  9.3 154.5 %all-gather.7.cloned.1.call-start = ((), (), s32[]{:S(2)}) async-start(), calls=%async_computation.1 | async-start | bytes 4325376 | tf_op jit(solution)/shard_map/all_gather | solution.py:431
  10.8 10.5 %collective-permute-start.2 = (bf16[256,512]{1,0:T(8,128)(2,1)S(1)}, bf16[256,512]{1,0:T(8,128)(2,1)S(1)}, u32[]{:S(2)}, u32[]{:S(2)}) collective-permute-start(bf16[256,512]{1,0:T(8,128)(2,1)S(1)} %get-tuple-element.169), channel_id=1, source_target_pairs={{0,8},{8,16},{16,24},{24,0},{1,9},{9,17},{17,25},{25,1},{2,10},{10... | collective-permute-start | bytes 786440 | tf_op jit(solution)/shard_map/ppermute | solution.py:31
  12.8 16.3 %collective-permute-start.3 = (bf16[256,512]{1,0:T(8,128)(2,1)S(1)}, bf16[256,512]{1,0:T(8,128)(2,1)S(1)}, u32[]{:S(2)}, u32[]{:S(2)}) collective-permute-start(bf16[256,512]{1,0:T(8,128)(2,1)S(1)} %get-tuple-element.171), channel_id=1, source_target_pairs={{0,16},{8,24},{16,0},{24,8},{1,17},{9,25},{17,1},{25,9},{2,18},{10... | collective-permute-start | bytes 786440 | tf_op jit(solution)/shard_map/ppermute | solution.py:31
  16.4 13.8 %collective-permute-start.4 = (bf16[256,512]{1,0:T(8,128)(2,1)S(1)}, bf16[256,512]{1,0:T(8,128)(2,1)S(1)}, u32[]{:S(2)}, u32[]{:S(2)}) collective-permute-start(bf16[256,512]{1,0:T(8,128)(2,1)S(1)} %get-tuple-element.170), channel_id=1, source_target_pairs={{0,24},{8,0},{16,8},{24,16},{1,25},{9,1},{17,9},{25,17},{2,26},{10... | collective-permute-start | bytes 786440 | tf_op jit(solution)/shard_map/ppermute | solution.py:31
  18.4 12.9 %collective-permute-start.1 = (bf16[2,32,2048]{2,1,0:T(8,128)(2,1)S(1)}, bf16[2,32,2048]{2,1,0:T(8,128)(2,1)S(1)}, u32[]{:S(2)}, u32[]{:S(2)}) collective-permute-start(bf16[2,32,2048]{2,1,0:T(8,128)(2,1)S(1)} %dynamic-slice_bitcast_fusion), channel_id=1, source_target_pairs={{0,2},{2,0},{4,6},{6,4},{1,3},{3,1},{5,7},{7,5},{8,10},{10,8},{12,... | collective-permute-start | bytes 786440 | tf_op jit(solution)/shard_map/ppermute | solution.py:353
  20.0 53.7 %collective-permute-start = (bf16[2,32,8192]{2,1,0:T(8,128)(2,1)}, bf16[2,32,8192]{2,1,0:T(8,128)(2,1)}, u32[]{:S(2)}, u32[]{:S(2)}) collective-permute-start(bf16[2,32,8192]{2,1,0:T(8,128)(2,1)} %bitcast.1), channel_id=1, source_target_pairs={{0,1},{1,0},{2,3},{3,2},{4,5},{5,4},{6,7},{7,6},{8,9},{9,8},{10,11... | collective-permute-start | bytes 3145736 | tf_op jit(solution)/shard_map/ppermute | solution.py:35
  31.3 13.0 %collective-permute-start.5 = (bf16[2,32,2048]{2,1,0:T(8,128)(2,1)S(1)}, bf16[2,32,2048]{2,1,0:T(8,128)(2,1)S(1)}, u32[]{:S(2)}, u32[]{:S(2)}) collective-permute-start(bf16[2,32,2048]{2,1,0:T(8,128)(2,1)S(1)} %collective-permute-done.1), channel_id=1, source_target_pairs={{0,96},{32,0},{64,32},{96,64},{1,97},{33,1},{65,33},{97,65},{2,98}... | collective-permute-start | bytes 786440 | tf_op jit(solution)/shard_map/ppermute | solution.py:31
  34.1 15.0 %collective-permute-start.6 = (bf16[2,32,2048]{2,1,0:T(8,128)(2,1)S(1)}, bf16[2,32,2048]{2,1,0:T(8,128)(2,1)}, u32[]{:S(2)}, u32[]{:S(2)}) collective-permute-start(bf16[2,32,2048]{2,1,0:T(8,128)(2,1)S(1)} %collective-permute-done.1), channel_id=1, source_target_pairs={{0,64},{32,96},{64,0},{96,32},{1,65},{33,97},{65,1},{97,33},{2,66}... | collective-permute-start | bytes 786440 | tf_op jit(solution)/shard_map/ppermute | solution.py:31
  34.8 16.0 %collective-permute-start.7 = (bf16[2,32,2048]{2,1,0:T(8,128)(2,1)S(1)}, bf16[2,32,2048]{2,1,0:T(8,128)(2,1)}, u32[]{:S(2)}, u32[]{:S(2)}) collective-permute-start(bf16[2,32,2048]{2,1,0:T(8,128)(2,1)S(1)} %collective-permute-done.1), channel_id=1, source_target_pairs={{0,32},{32,64},{64,96},{96,0},{1,33},{33,65},{65,97},{97,1},{2,34}... | collective-permute-start | bytes 786440 | tf_op jit(solution)/shard_map/ppermute | solution.py:31
  38.5 31.8 %collective-permute-start.9 = (bf16[1024,512]{1,0:T(8,128)(2,1)}, bf16[1024,512]{1,0:T(8,128)(2,1)S(1)}, u32[]{:S(2)}, u32[]{:S(2)}) collective-permute-start(bf16[1024,512]{1,0:T(8,128)(2,1)} %pad_maximum_fusion.1), channel_id=1, source_target_pairs={{0,32},{32,64},{64,96},{96,0},{1,33},{33,65},{65,97},{97,1},{2,34}... | collective-permute-start | bytes 3145736 | tf_op jit(solution)/shard_map/ppermute | solution.py:31
  44.2 26.2 %collective-permute-start.11 = (bf16[1024,512]{1,0:T(8,128)(2,1)}, bf16[1024,512]{1,0:T(8,128)(2,1)S(1)}, u32[]{:S(2)}, u32[]{:S(2)}) collective-permute-start(bf16[1024,512]{1,0:T(8,128)(2,1)} %pad_maximum_fusion.1), channel_id=1, source_target_pairs={{0,96},{32,0},{64,32},{96,64},{1,97},{33,1},{65,33},{97,65},{2,98}... | collective-permute-start | bytes 3145736 | tf_op jit(solution)/shard_map/ppermute | solution.py:31
  57.9 15.8 %collective-permute-start.8 = (bf16[2,32,8192]{2,1,0:T(8,128)(2,1)}, bf16[2,32,8192]{2,1,0:T(8,128)(2,1)}, u32[]{:S(2)}, u32[]{:S(2)}) collective-permute-start(bf16[2,32,8192]{2,1,0:T(8,128)(2,1)} %constant_dynamic-slice_fusion.5), channel_id=1, source_target_pairs={{0,1},{1,0},{2,3},{3,2},{4,5},{5,4},{6,7},{7,6},{8,9},{9,8},{10,11... | collective-permute-start | bytes 3145736 | tf_op jit(solution)/shard_map/ppermute | solution.py:35
  70.3 15.2 %collective-permute-start.10 = (bf16[512,512]{1,0:T(8,128)(2,1)S(1)}, bf16[512,512]{1,0:T(8,128)(2,1)S(1)}, u32[]{:S(2)}, u32[]{:S(2)}) collective-permute-start(bf16[512,512]{1,0:T(8,128)(2,1)S(1)} %slice.12), channel_id=1, source_target_pairs={{0,32},{32,64},{64,96},{96,0},{1,33},{33,65},{65,97},{97,1},{2,34}... | collective-permute-start | bytes 1572872 | tf_op jit(solution)/shard_map/ppermute | solution.py:31
  70.5 15.1 %collective-permute-start.12 = (bf16[512,512]{1,0:T(8,128)(2,1)S(1)}, bf16[512,512]{1,0:T(8,128)(2,1)S(1)}, u32[]{:S(2)}, u32[]{:S(2)}) collective-permute-start(bf16[512,512]{1,0:T(8,128)(2,1)S(1)} %slice.13), channel_id=1, source_target_pairs={{0,96},{32,0},{64,32},{96,64},{1,97},{33,1},{65,33},{97,65},{2,98}... | collective-permute-start | bytes 1572872 | tf_op jit(solution)/shard_map/ppermute | solution.py:31
  92.3 8.9 %collective-permute-start.13 = (bf16[2,2,128,128]{3,2,1,0:T(8,128)(2,1)}, bf16[2,2,128,128]{3,2,1,0:T(8,128)(2,1)S(1)}, u32[]{:S(2)}, u32[]{:S(2)}) collective-permute-start(bf16[2,2,128,128]{3,2,1,0:T(8,128)(2,1)} %project_key_value.1.kv0), channel_id=1, source_target_pairs={{0,2},{2,0},{4,6},{6,4},{1,3},{3,1},{5,7},{7,5},{8,10},{10,8},{12,... | collective-permute-start | bytes 393224 | tf_op jit(solution)/shard_map/ppermute | solution.py:432
  107.4 18.1 %collective-permute-start.16 = (bf16[512,256]{1,0:T(8,128)(2,1)}, bf16[512,256]{1,0:T(8,128)(2,1)S(1)}, u32[]{:S(2)}, u32[]{:S(2)}) collective-permute-start(bf16[512,256]{1,0:T(8,128)(2,1)} %attend.2.refs_8_), channel_id=1, source_target_pairs={{0,8},{8,16},{16,24},{24,0},{1,9},{9,17},{17,25},{25,1},{2,10},{10... | collective-permute-start | bytes 786440 | tf_op jit(solution)/shard_map/ppermute | solution.py:31
  107.6 20.5 %collective-permute-start.17 = (bf16[512,256]{1,0:T(8,128)(2,1)}, bf16[512,256]{1,0:T(8,128)(2,1)S(1)}, u32[]{:S(2)}, u32[]{:S(2)}) collective-permute-start(bf16[512,256]{1,0:T(8,128)(2,1)} %attend.2.refs_8_), channel_id=1, source_target_pairs={{0,16},{8,24},{16,0},{24,8},{1,17},{9,25},{17,1},{25,9},{2,18},{10... | collective-permute-start | bytes 786440 | tf_op jit(solution)/shard_map/ppermute | solution.py:31
  111.7 16.4 %collective-permute-start.18 = (bf16[512,256]{1,0:T(8,128)(2,1)}, bf16[512,256]{1,0:T(8,128)(2,1)S(1)}, u32[]{:S(2)}, u32[]{:S(2)}) collective-permute-start(bf16[512,256]{1,0:T(8,128)(2,1)} %attend.2.refs_8_), channel_id=1, source_target_pairs={{0,24},{8,0},{16,8},{24,16},{1,25},{9,1},{17,9},{25,17},{2,26},{10... | collective-permute-start | bytes 786440 | tf_op jit(solution)/shard_map/ppermute | solution.py:31
  123.5 16.7 %collective-permute-start.23 = (bf16[512,256]{1,0:T(8,128)(2,1)}, bf16[512,256]{1,0:T(8,128)(2,1)S(1)}, u32[]{:S(2)}, u32[]{:S(2)}) collective-permute-start(bf16[512,256]{1,0:T(8,128)(2,1)} %attend.3.refs_8_), channel_id=1, source_target_pairs={{0,8},{8,16},{16,24},{24,0},{1,9},{9,17},{17,25},{25,1},{2,10},{10... | collective-permute-start | bytes 786440 | tf_op jit(solution)/shard_map/ppermute | solution.py:31
  125.4 18.4 %collective-permute-start.24 = (bf16[512,256]{1,0:T(8,128)(2,1)}, bf16[512,256]{1,0:T(8,128)(2,1)S(1)}, u32[]{:S(2)}, u32[]{:S(2)}) collective-permute-start(bf16[512,256]{1,0:T(8,128)(2,1)} %attend.3.refs_8_), channel_id=1, source_target_pairs={{0,16},{8,24},{16,0},{24,8},{1,17},{9,25},{17,1},{25,9},{2,18},{10... | collective-permute-start | bytes 786440 | tf_op jit(solution)/shard_map/ppermute | solution.py:31
  125.5 20.6 %collective-permute-start.25 = (bf16[512,256]{1,0:T(8,128)(2,1)}, bf16[512,256]{1,0:T(8,128)(2,1)S(1)}, u32[]{:S(2)}, u32[]{:S(2)}) collective-permute-start(bf16[512,256]{1,0:T(8,128)(2,1)} %attend.3.refs_8_), channel_id=1, source_target_pairs={{0,24},{8,0},{16,8},{24,16},{1,25},{9,1},{17,9},{25,17},{2,26},{10... | collective-permute-start | bytes 786440 | tf_op jit(solution)/shard_map/ppermute | solution.py:31
  137.1 9.0 %collective-permute-start.19 = (bf16[1,512,256]{2,1,0:T(8,128)(2,1)}, bf16[1,512,256]{2,1,0:T(8,128)(2,1)S(1)}, u32[]{:S(2)}, u32[]{:S(2)}) collective-permute-start(bf16[1,512,256]{2,1,0:T(8,128)(2,1)} %get-tuple-element.111), channel_id=1, source_target_pairs={{0,1},{1,0},{2,3},{3,2},{4,5},{5,4},{6,7},{7,6},{8,9},{9,8},{10,11... | collective-permute-start | bytes 786440 | tf_op jit(solution)/shard_map/ppermute | solution.py:35
  137.1 9.0 %collective-permute-start.20 = (bf16[1,512,256]{2,1,0:T(8,128)(2,1)}, bf16[1,512,256]{2,1,0:T(8,128)(2,1)S(1)}, u32[]{:S(2)}, u32[]{:S(2)}) collective-permute-start(bf16[1,512,256]{2,1,0:T(8,128)(2,1)} %get-tuple-element.112), channel_id=1, source_target_pairs={{0,1},{1,0},{2,3},{3,2},{4,5},{5,4},{6,7},{7,6},{8,9},{9,8},{10,11... | collective-permute-start | bytes 786440 | tf_op jit(solution)/shard_map/ppermute | solution.py:35
  155.1 11.3 %collective-permute-start.31 = (bf16[1,512,256]{2,1,0:T(8,128)(2,1)}, bf16[1,512,256]{2,1,0:T(8,128)(2,1)S(1)}, u32[]{:S(2)}, u32[]{:S(2)}) collective-permute-start(bf16[1,512,256]{2,1,0:T(8,128)(2,1)} %get-tuple-element.130), channel_id=1, source_target_pairs={{0,1},{1,0},{2,3},{3,2},{4,5},{5,4},{6,7},{7,6},{8,9},{9,8},{10,11... | collective-permute-start | bytes 786440 | tf_op jit(solution)/shard_map/ppermute | solution.py:35
  155.2 11.2 %collective-permute-start.32 = (bf16[1,512,256]{2,1,0:T(8,128)(2,1)}, bf16[1,512,256]{2,1,0:T(8,128)(2,1)S(1)}, u32[]{:S(2)}, u32[]{:S(2)}) collective-permute-start(bf16[1,512,256]{2,1,0:T(8,128)(2,1)} %get-tuple-element.131), channel_id=1, source_target_pairs={{0,1},{1,0},{2,3},{3,2},{4,5},{5,4},{6,7},{7,6},{8,9},{9,8},{10,11... | collective-permute-start | bytes 786440 | tf_op jit(solution)/shard_map/ppermute | solution.py:35
  158.2 12.7 %collective-permute-start.26 = (bf16[512,256]{1,0:T(8,128)(2,1)}, bf16[512,256]{1,0:T(8,128)(2,1)S(1)}, u32[]{:S(2)}, u32[]{:S(2)}) collective-permute-start(bf16[512,256]{1,0:T(8,128)(2,1)} %get-tuple-element.120), channel_id=1, source_target_pairs={{0,2},{2,4},{4,6},{6,0},{1,3},{3,5},{5,7},{7,1},{8,10},{10,12},{12... | collective-permute-start | bytes 786440 | tf_op jit(solution)/shard_map/ppermute | solution.py:31
  160.1 14.8 %collective-permute-start.27 = (bf16[512,256]{1,0:T(8,128)(2,1)}, bf16[512,256]{1,0:T(8,128)(2,1)S(1)}, u32[]{:S(2)}, u32[]{:S(2)}) collective-permute-start(bf16[512,256]{1,0:T(8,128)(2,1)} %get-tuple-element.121), channel_id=1, source_target_pairs={{0,4},{2,6},{4,0},{6,2},{1,5},{3,7},{5,1},{7,3},{8,12},{10,14},{12... | collective-permute-start | bytes 786440 | tf_op jit(solution)/shard_map/ppermute | solution.py:31
  162.0 13.0 %collective-permute-start.28 = (bf16[512,256]{1,0:T(8,128)(2,1)}, bf16[512,256]{1,0:T(8,128)(2,1)S(1)}, u32[]{:S(2)}, u32[]{:S(2)}) collective-permute-start(bf16[512,256]{1,0:T(8,128)(2,1)} %get-tuple-element.122), channel_id=1, source_target_pairs={{0,6},{2,0},{4,2},{6,4},{1,7},{3,1},{5,3},{7,5},{8,14},{10,8},{12,... | collective-permute-start | bytes 786440 | tf_op jit(solution)/shard_map/ppermute | solution.py:31
  169.7 13.6 %collective-permute-start.33 = (bf16[512,256]{1,0:T(8,128)(2,1)}, bf16[512,256]{1,0:T(8,128)(2,1)S(1)}, u32[]{:S(2)}, u32[]{:S(2)}) collective-permute-start(bf16[512,256]{1,0:T(8,128)(2,1)} %get-tuple-element.143), channel_id=1, source_target_pairs={{0,2},{2,4},{4,6},{6,0},{1,3},{3,5},{5,7},{7,1},{8,10},{10,12},{12... | collective-permute-start | bytes 786440 | tf_op jit(solution)/shard_map/ppermute | solution.py:31
  170.9 14.4 %collective-permute-start.34 = (bf16[512,256]{1,0:T(8,128)(2,1)}, bf16[512,256]{1,0:T(8,128)(2,1)S(1)}, u32[]{:S(2)}, u32[]{:S(2)}) collective-permute-start(bf16[512,256]{1,0:T(8,128)(2,1)} %get-tuple-element.144), channel_id=1, source_target_pairs={{0,4},{2,6},{4,0},{6,2},{1,5},{3,7},{5,1},{7,3},{8,12},{10,14},{12... | collective-permute-start | bytes 786440 | tf_op jit(solution)/shard_map/ppermute | solution.py:31
  174.9 11.1 %collective-permute-start.35 = (bf16[512,256]{1,0:T(8,128)(2,1)}, bf16[512,256]{1,0:T(8,128)(2,1)S(1)}, u32[]{:S(2)}, u32[]{:S(2)}) collective-permute-start(bf16[512,256]{1,0:T(8,128)(2,1)} %get-tuple-element.145), channel_id=1, source_target_pairs={{0,6},{2,0},{4,2},{6,4},{1,7},{3,1},{5,3},{7,5},{8,14},{10,8},{12,... | collective-permute-start | bytes 786440 | tf_op jit(solution)/shard_map/ppermute | solution.py:31
  (45 other events, 345.7 us)
Sparse Core Ops, SparseCore 0:
  10.3 76.7 all-gather.4
  92.5 57.7 all-gather.6

commit v5 on v4

--- a/solution.py
+++ b/solution.py
@@ -29,6 +29,10 @@
 
 def shift(value, axis, distance):
     return lax.ppermute(value, axis, SHIFT[distance])
+
+
+def shift_all(values, axis):
+    return [shift(values[d], axis, d) for d in (2, 1, 3)]
 
 
 def swap(value):
@@ -387,7 +391,7 @@
     before = jnp.arange(64)[None, :] < jnp.arange(64)[:, None]
     rank = jnp.sum((same & before).astype(jnp.int32), axis=1)
     slots = jnp.arange(64, dtype=jnp.int32)
-    z_of, y_of, rest = slots // 16, (slots // 4) % 4, slots % 4
+    y_of, z_of, rest = slots // 16, (slots // 4) % 4, slots % 4
     block = ((y_of % 2) * 4 + rest) * 8 + z_of * 2 + y_of // 2
     owner, slot = owners[block], rank[block]
     target = (((g + jnp.arange(4)) % 4) * 32 + z * 8 + y * 2 + c).astype(jnp.int32)
@@ -428,7 +432,7 @@
     )
 
     own = project_key_value(place, gathered, w_kv, cosine, sine)
-    everyone = lax.all_gather(own, ("z", "y", "c")).reshape(64, 2, BLOCK, HEAD)
+    everyone = lax.all_gather(own, ("y", "z", "c")).reshape(64, 2, BLOCK, HEAD)
     near = lax.ppermute(own, "y", PAIR)
     gathered, own = lax.optimization_barrier((gathered, own))
     queries = project_query(0, gathered, w_query, cosine, sine)
@@ -438,19 +442,19 @@
     gathered, attended[0] = lax.optimization_barrier((gathered, attended[0]))
     queries = project_query(1, gathered, w_query, cosine, sine)
     attended.append(attend(1, scalars, queries, kvs))
-    landed = [[shift(a, "z", d) for d in (1, 2, 3)] for a in attended]
+    landed = [shift_all([a] * 4, "z") for a in attended]
     landed[0], attended[1] = lax.optimization_barrier((landed[0], attended[1]))
     picked = pick_blocks(index, valid, everyone)
     sums = []
     for chunk in range(SEQ // CHUNK):
-        keep, *send = project_out(order, (attended[chunk], *landed[chunk]), *w_o)
+        keep, *send = project_out(order, (attended[chunk], *(landed[chunk][i] for i in (1, 0, 2))), *w_o)
         got = [swap(part) for part in send]
         if chunk == 0:
             got, landed[1] = lax.optimization_barrier((got, landed[1]))
         else:
             got, picked = lax.optimization_barrier((got, picked))
         parts = add_cores(keep, got)
-        sums.append([parts[0]] + [shift(parts[d], "y", d) for d in (1, 2, 3)])
+        sums.append([parts[0]] + shift_all(parts, "y"))
 
     arrived = [picked[0]] + [shift(picked[d], "g", d) for d in (1, 2, 3)]
     sums, arrived = lax.optimization_barrier((sums, arrived))

time: 196 us -> 195 us (level)
    ppermute x25, waiting for transfers between devices: 43 us -> 40 us  [shift(): return lax.ppermute(value, axis, SHIFT[distance])]
  transfers between devices with their start and end apart: 41 -> 41, of which waited for: 16 -> 14; matrix products, arithmetic and copies ran while one was open for 14% -> 14% of each run, Pallas kernels for 23% -> 24%
where the time goes in v5:
time: 195 us; the launch traced here: 194 us
  Pallas kernels  53.1 us (27%)
  starting transfers between devices  48.5 us (25%)
  waiting for transfers between devices  44.4 us (23%)
  local copies, waits for them, and re-layouts  22 us (11%)
  between operations  14.7 us (8%)
  other arithmetic  11 us (6%)
    ppermute x25, starting transfers between devices, shift(): return lax.ppermute(value, axis, SHIFT[distance])  42.9 us
    ppermute x25, waiting for transfers between devices, shift(): return lax.ppermute(value, axis, SHIFT[distance])  40 us
    pallas_call x2, Pallas kernels, project_out(): pl.pallas_call(out_kernel, grid_spec=pltpu.PrefetchScalarGridSpec(num_sca...  15.2 us
    pallas_call x2, Pallas kernels, project_query(): pl.pallas_call(functools.partial(query_kernel, chunk, steps, per_step), g...  14.6 us
    unnamed x78, local copies, waits for them, and re-layouts  9.15 us
    pallas_call x2, Pallas kernels, attend(): pl.pallas_call(functools.partial(attention_kernel, chunk), grid_spec=pltp...  8.34 us
    pallas_call x1, Pallas kernels, project_key_value(): pl.pallas_call(functools.partial(key_value_kernel, steps, per_step), grid...  5.26 us
    pallas_call x2, Pallas kernels, add_cores(): pl.pallas_call(add_kernel, out_shape=[jax.ShapeDtypeStruct((CHUNK, COLS),...  5.09 us
  transfers between devices with their start and end apart: 41, of which 14 were waited for; matrix products, arithmetic and copies ran while one was open for 14% of the time, Pallas kernels for 24%

profile of v5, /device:TPU:0, one launch (start us, length us, event | category | flops | bytes accessed | tf_op | source)
XLA Modules:
  0.0 193.7 jit_solution(10161357184242622923)
XLA Ops:
  7.2 2.1 %scale_tokens.1 = bf16[1040,256]{1,0:T(8,128)(2,1)} custom-call(bf16[1024,256]{1,0:T(8,128)(2,1)} %tokens.1, bf16[256]{0:T(256)(128)(2,1)} %gain.1), custom_call_target="tpu_custom_call" | custom-call | tf_op jit(solution)/shard_map/scale_tokens/pallas_call | solution.py:63
  10.8 2.1 %collective-permute-start.2 = (bf16[256,512]{1,0:T(8,128)(2,1)S(1)}, bf16[256,512]{1,0:T(8,128)(2,1)S(1)}, u32[]{:S(2)}, u32[]{:S(2)}) collective-permute-start(bf16[256,512]{1,0:T(8,128)(2,1)S(1)} %get-tuple-element.169), channel_id=1, source_target_pairs={{0,8},{8,16},{16,24},{24,0},{1,9},{9,17},{17,25},{25,1},{2,10},{10... | collective-permute-start | bytes 786440 | tf_op jit(solution)/shard_map/ppermute | solution.py:31
  12.8 3.6 %collective-permute-start.3 = (bf16[256,512]{1,0:T(8,128)(2,1)S(1)}, bf16[256,512]{1,0:T(8,128)(2,1)S(1)}, u32[]{:S(2)}, u32[]{:S(2)}) collective-permute-start(bf16[256,512]{1,0:T(8,128)(2,1)S(1)} %get-tuple-element.171), channel_id=1, source_target_pairs={{0,16},{8,24},{16,0},{24,8},{1,17},{9,25},{17,1},{25,9},{2,18},{10... | collective-permute-start | bytes 786440 | tf_op jit(solution)/shard_map/ppermute | solution.py:31
  21.3 7.9 %collective-permute-done.3.refs_2_ = bf16[256,512]{1,0:T(8,128)(2,1)S(1)} collective-permute-done((bf16[256,512]{1,0:T(8,128)(2,1)S(1)}, bf16[256,512]{1,0:T(8,128)(2,1)S(1)}, u32[]{:S(2)}, u32[]{:S(2)}) %collective-permute-start.3) | collective-permute-done | bytes 262176 | tf_op jit(solution)/shard_map/ppermute | solution.py:31
  31.3 2.8 %collective-permute-start.5 = (bf16[2,32,2048]{2,1,0:T(8,128)(2,1)S(1)}, bf16[2,32,2048]{2,1,0:T(8,128)(2,1)S(1)}, u32[]{:S(2)}, u32[]{:S(2)}) collective-permute-start(bf16[2,32,2048]{2,1,0:T(8,128)(2,1)S(1)} %collective-permute-done.1), channel_id=1, source_target_pairs={{0,96},{32,0},{64,32},{96,64},{1,97},{33,1},{65,33},{97,65},{2,98}... | collective-permute-start | bytes 786440 | tf_op jit(solution)/shard_map/ppermute | solution.py:31
  40.5 3.8 %collective-permute-done.5 = bf16[2,32,2048]{2,1,0:T(8,128)(2,1)S(1)} collective-permute-done((bf16[2,32,2048]{2,1,0:T(8,128)(2,1)S(1)}, bf16[2,32,2048]{2,1,0:T(8,128)(2,1)S(1)}, u32[]{:S(2)}, u32[]{:S(2)}) %collective-permute-start.5) | collective-permute-done | bytes 262176 | tf_op jit(solution)/shard_map/ppermute | solution.py:31
  44.2 4.2 %collective-permute-start.11 = (bf16[1024,512]{1,0:T(8,128)(2,1)}, bf16[1024,512]{1,0:T(8,128)(2,1)S(1)}, u32[]{:S(2)}, u32[]{:S(2)}) collective-permute-start(bf16[1024,512]{1,0:T(8,128)(2,1)} %pad_maximum_fusion.1), channel_id=1, source_target_pairs={{0,96},{32,0},{64,32},{96,64},{1,97},{33,1},{65,33},{97,65},{2,98}... | collective-permute-start | bytes 3145736 | tf_op jit(solution)/shard_map/ppermute | solution.py:31
  55.6 2.3 %constant_dynamic-slice_fusion.5 = bf16[2,32,8192]{2,1,0:T(8,128)(2,1)} fusion(bf16[2,32,14336]{2,1,0:T(8,128)(2,1)} %constant_dynamic-update-slice_fusion, s32[]{:T(128)S(6)} %select_n.255), kind=kLoop, calls=%fused_computation.48 | loop fusion | bytes 2097156 | tf_op jit(solution)/shard_map/dynamic_slice | solution.py:362
  63.4 6.9 %collective-permute-done.9.refs_4_ = bf16[1024,512]{1,0:T(8,128)(2,1)S(1)} collective-permute-done((bf16[1024,512]{1,0:T(8,128)(2,1)}, bf16[1024,512]{1,0:T(8,128)(2,1)S(1)}, u32[]{:S(2)}, u32[]{:S(2)}) %collective-permute-start.9) | collective-permute-done | bytes 1048608 | tf_op jit(solution)/shard_map/ppermute | solution.py:31
  70.5 3.3 %collective-permute-start.12 = (bf16[512,512]{1,0:T(8,128)(2,1)S(1)}, bf16[512,512]{1,0:T(8,128)(2,1)S(1)}, u32[]{:S(2)}, u32[]{:S(2)}) collective-permute-start(bf16[512,512]{1,0:T(8,128)(2,1)S(1)} %slice.13), channel_id=1, source_target_pairs={{0,96},{32,0},{64,32},{96,64},{1,97},{33,1},{65,33},{97,65},{2,98}... | collective-permute-start | bytes 1572872 | tf_op jit(solution)/shard_map/ppermute | solution.py:31
  73.7 3.3 %select_bitcast_fusion.3 = (bf16[2,1,32,8192]{3,2,0,1:T(8,128)(2,1)S(1)}, bf16[2,1,32,8192]{3,2,0,1:T(8,128)(2,1)S(1)}, bf16[2,1,32,8192]{3,2,0,1:T(8,128)(2,1)S(1)}, bf16[2,1,32,8192]{3,2,0,1:T(8,128)(2,1)S(1)}) fusion(pred[]{:T(512)S(6)} %eq.86, bf16[2,32,8192]{2,1,0:T(8,128)(2,1)} %collective-permute-done, pred[]{:T(512)S(6)} %eq.87, ...), kind=kLoop, calls=%fused_computation.9 | loop fusion | flops 4194304 | bytes 8388614 | tf_op jit(solution)/shard_map/stack | solution.py:374
  77.6 2.3 %copy.12 = bf16[2,4,32,8192]{3,2,1,0:T(8,128)(2,1)} copy(bf16[2,4,32,8192]{3,2,0,1:T(8,128)(2,1)S(1)} %pad_maximum_fusion) | data formatting | bytes 8388608 | tf_op jit(solution)/shard_map/stack | solution.py:374
  79.9 5.6 %collective-permute-done.10.refs_5_ = bf16[512,512]{1,0:T(8,128)(2,1)S(1)} collective-permute-done((bf16[512,512]{1,0:T(8,128)(2,1)S(1)}, bf16[512,512]{1,0:T(8,128)(2,1)S(1)}, u32[]{:S(2)}, u32[]{:S(2)}) %collective-permute-start.10) | collective-permute-done | bytes 524320 | tf_op jit(solution)/shard_map/ppermute | solution.py:31
  87.0 5.3 %project_key_value.1.kv0 = bf16[2,2,128,128]{3,2,1,0:T(8,128)(2,1)} custom-call(s32[1]{0:T(128)} %bitcast.18.place, bf16[32,1040,256]{2,1,0:T(8,128)(2,1)} %bitcast.39, bf16[32,1040,256]{2,1,0:T(8,128)(2,1)} %bitcast.40, bf16[256,8192]{1,0:T(8,128)(2,1)} %bitcast.45, f32[1024,128]{1,0:T(8,128)} %get-tuple-element.98.cosine, f32[1024,128]{1,0:T(8,128)} %get-tuple-element.99.sine), custom_call_target="tpu_custom_call" | custom-call | flops 1073741824 | bytes 8388608 | tf_op jit(solution)/shard_map/project_key_value/pallas_call | solution.py:107
  93.9 7.3 %project_query.2.queries = bf16[512,256]{1,0:T(8,128)(2,1)} custom-call(bf16[32,1040,256]{2,1,0:T(8,128)(2,1)} %bitcast.41, bf16[32,1040,256]{2,1,0:T(8,128)(2,1)} %bitcast.42, bf16[8192,256]{1,0:T(8,128)(2,1)} %weights.3, f32[1024,128]{1,0:T(8,128)} %get-tuple-element.98.cosine, f32[1024,128]{1,0:T(8,128)} %get-tuple-element.99.sine), custom_call_target="tpu_custom_call" | custom-call | flops 2147483648 | bytes 12582912 | tf_op jit(solution)/shard_map/project_query/pallas_call | solution.py:155
  103.4 3.9 %attend.2.refs_8_ = bf16[512,256]{1,0:T(8,128)(2,1)} custom-call(s32[8]{0:T(128)} %concatenate.22.scalars, bf16[512,256]{1,0:T(8,128)(2,1)} %project_query.2.queries, bf16[2,2,128,128]{3,2,1,0:T(8,128)(2,1)} %project_key_value.1.kv0, bf16[2,2,128,128]{3,2,1,0:T(8,128)(2,1)} %copy-done.13, bf16[2,2,128,128]{3,2,1,0:T(8,128)(2,1)} %copy-done.12, ...), custom_call_target="tpu_custom_call" | custom-call | flops 1024 | bytes 1024 | tf_op jit(solution)/shard_map/attend/pallas_call | solution.py:214
  108.9 2.2 %collective-permute-start.17 = (bf16[512,256]{1,0:T(8,128)(2,1)}, bf16[512,256]{1,0:T(8,128)(2,1)S(1)}, u32[]{:S(2)}, u32[]{:S(2)}) collective-permute-start(bf16[512,256]{1,0:T(8,128)(2,1)} %attend.2.refs_8_), channel_id=1, source_target_pairs={{0,8},{8,16},{16,24},{24,0},{1,9},{9,17},{17,25},{25,1},{2,10},{10... | collective-permute-start | bytes 786440 | tf_op jit(solution)/shard_map/ppermute | solution.py:31
  112.1 7.3 %project_query.3.queries = bf16[512,256]{1,0:T(8,128)(2,1)} custom-call(bf16[32,1040,256]{2,1,0:T(8,128)(2,1)} %bitcast.43, bf16[32,1040,256]{2,1,0:T(8,128)(2,1)} %bitcast.44, bf16[8192,256]{1,0:T(8,128)(2,1)} %weights.3, f32[1024,128]{1,0:T(8,128)} %get-tuple-element.98.cosine, f32[1024,128]{1,0:T(8,128)} %get-tuple-element.99.sine), custom_call_target="tpu_custom_call" | custom-call | flops 2147483648 | bytes 12582912 | tf_op jit(solution)/shard_map/project_query/pallas_call | solution.py:155
  119.4 4.4 %attend.3.refs_8_ = bf16[512,256]{1,0:T(8,128)(2,1)} custom-call(s32[8]{0:T(128)} %concatenate.22.scalars, bf16[512,256]{1,0:T(8,128)(2,1)} %project_query.3.queries, bf16[2,2,128,128]{3,2,1,0:T(8,128)(2,1)} %project_key_value.1.kv0, bf16[2,2,128,128]{3,2,1,0:T(8,128)(2,1)} %copy-done.13, bf16[2,2,128,128]{3,2,1,0:T(8,128)(2,1)} %copy-done.12, ...), custom_call_target="tpu_custom_call" | custom-call | flops 1024 | bytes 1024 | tf_op jit(solution)/shard_map/attend/pallas_call | solution.py:214
  124.9 3.2 %collective-permute-start.25 = (bf16[512,256]{1,0:T(8,128)(2,1)}, bf16[512,256]{1,0:T(8,128)(2,1)S(1)}, u32[]{:S(2)}, u32[]{:S(2)}) collective-permute-start(bf16[512,256]{1,0:T(8,128)(2,1)} %attend.3.refs_8_), channel_id=1, source_target_pairs={{0,24},{8,0},{16,8},{24,16},{1,25},{9,1},{17,9},{25,17},{2,26},{10... | collective-permute-start | bytes 786440 | tf_op jit(solution)/shard_map/ppermute | solution.py:31
  129.6 7.6 %project_out.2 = (bf16[4,512,256]{2,1,0:T(8,128)(2,1)}, bf16[1,512,256]{2,1,0:T(8,128)(2,1)}, bf16[1,512,256]{2,1,0:T(8,128)(2,1)}, bf16[1,512,256]{2,1,0:T(8,128)(2,1)}, bf16[1,512,256]{2,1,0:T(8,128)(2,1)}) custom-call(s32[5]{0:T(128)} %stack.77.scalars, bf16[256,512]{1,0:T(8,128)(2,1)} %copy-done.4, bf16[256,512]{1,0:T(8,128)(2,1)} %copy-done.6, ...), custom_call_target="tpu_custom_call" | custom-call | flops 1024 | bytes 1024 | tf_op jit(solution)/shard_map/project_out/pallas_call | solution.py:271
  137.8 6.6 %collective-permute-done.24.refs_9_ = bf16[512,256]{1,0:T(8,128)(2,1)S(1)} collective-permute-done((bf16[512,256]{1,0:T(8,128)(2,1)}, bf16[512,256]{1,0:T(8,128)(2,1)S(1)}, u32[]{:S(2)}, u32[]{:S(2)}) %collective-permute-start.24) | collective-permute-done | bytes 262176 | tf_op jit(solution)/shard_map/ppermute | solution.py:31
  146.4 7.7 %project_out.3 = (bf16[4,512,256]{2,1,0:T(8,128)(2,1)}, bf16[1,512,256]{2,1,0:T(8,128)(2,1)}, bf16[1,512,256]{2,1,0:T(8,128)(2,1)}, bf16[1,512,256]{2,1,0:T(8,128)(2,1)}, bf16[1,512,256]{2,1,0:T(8,128)(2,1)}) custom-call(s32[5]{0:T(128)} %stack.77.scalars, bf16[256,512]{1,0:T(8,128)(2,1)} %copy-done.4, bf16[256,512]{1,0:T(8,128)(2,1)} %copy-done.6, ...), custom_call_target="tpu_custom_call" | custom-call | flops 1024 | bytes 1024 | tf_op jit(solution)/shard_map/project_out/pallas_call | solution.py:271
  155.1 2.6 %add_cores.2 = (bf16[512,256]{1,0:T(8,128)(2,1)}, bf16[512,256]{1,0:T(8,128)(2,1)}, bf16[512,256]{1,0:T(8,128)(2,1)}, bf16[512,256]{1,0:T(8,128)(2,1)}) custom-call(bf16[4,512,256]{2,1,0:T(8,128)(2,1)} %get-tuple-element.110.keep, bf16[1,512,256]{2,1,0:T(8,128)(2,1)} %copy-done.17, bf16[1,512,256]{2,1,0:T(8,128)(2,1)} %copy-done.18, ...), custom_call_target="tpu_custom_call" | custom-call | flops 1024 | bytes 1024 | tf_op jit(solution)/shard_map/add_cores/pallas_call | solution.py:296
  157.7 2.3 %collective-permute-start.26 = (bf16[512,256]{1,0:T(8,128)(2,1)}, bf16[512,256]{1,0:T(8,128)(2,1)S(1)}, u32[]{:S(2)}, u32[]{:S(2)}) collective-permute-start(bf16[512,256]{1,0:T(8,128)(2,1)} %get-tuple-element.120), channel_id=1, source_target_pairs={{0,4},{2,6},{4,0},{6,2},{1,5},{3,7},{5,1},{7,3},{8,12},{10,14},{12... | collective-permute-start | bytes 786440 | tf_op jit(solution)/shard_map/ppermute | solution.py:31
  160.0 3.2 %collective-permute-start.28 = (bf16[512,256]{1,0:T(8,128)(2,1)}, bf16[512,256]{1,0:T(8,128)(2,1)S(1)}, u32[]{:S(2)}, u32[]{:S(2)}) collective-permute-start(bf16[512,256]{1,0:T(8,128)(2,1)} %get-tuple-element.122), channel_id=1, source_target_pairs={{0,6},{2,0},{4,2},{6,4},{1,7},{3,1},{5,3},{7,5},{8,14},{10,8},{12,... | collective-permute-start | bytes 786440 | tf_op jit(solution)/shard_map/ppermute | solution.py:31
  163.2 2.5 %pick_blocks.1 = (bf16[2,2,128,128]{3,2,1,0:T(8,128)(2,1)}, bf16[2,2,128,128]{3,2,1,0:T(8,128)(2,1)}, bf16[2,2,128,128]{3,2,1,0:T(8,128)(2,1)}, bf16[2,2,128,128]{3,2,1,0:T(8,128)(2,1)}) custom-call(s32[8]{0:T(128)} %reduce_sum.42.index, s32[8]{0:T(128)} %reduce_sum.44.valid, bf16[64,2,128,128]{3,2,1,0:T(8,128)(2,1)} %all-gather.7.cloned.1.call-done.blocks), custom_call_target="tpu_custom_call" | custom-call | flops 1024 | bytes 1024 | tf_op jit(solution)/shard_map/pick_blocks/pallas_call | solution.py:330
  166.6 2.5 %add_cores.3 = (bf16[512,256]{1,0:T(8,128)(2,1)}, bf16[512,256]{1,0:T(8,128)(2,1)}, bf16[512,256]{1,0:T(8,128)(2,1)}, bf16[512,256]{1,0:T(8,128)(2,1)}) custom-call(bf16[4,512,256]{2,1,0:T(8,128)(2,1)} %get-tuple-element.127.keep, bf16[1,512,256]{2,1,0:T(8,128)(2,1)} %copy-done.19, bf16[1,512,256]{2,1,0:T(8,128)(2,1)} %copy-done.21, ...), custom_call_target="tpu_custom_call" | custom-call | flops 1024 | bytes 1024 | tf_op jit(solution)/shard_map/add_cores/pallas_call | solution.py:296
  172.2 1.9 %collective-permute-done.27 = bf16[512,256]{1,0:T(8,128)(2,1)S(1)} collective-permute-done((bf16[512,256]{1,0:T(8,128)(2,1)}, bf16[512,256]{1,0:T(8,128)(2,1)S(1)}, u32[]{:S(2)}, u32[]{:S(2)}) %collective-permute-start.27) | collective-permute-done | bytes 262176 | tf_op jit(solution)/shard_map/ppermute | solution.py:31
  174.6 3.0 %collective-permute-start.37 = (bf16[2,2,128,128]{3,2,1,0:T(8,128)(2,1)S(1)}, bf16[2,2,128,128]{3,2,1,0:T(8,128)(2,1)S(1)}, u32[]{:S(2)}, u32[]{:S(2)}) collective-permute-start(bf16[2,2,128,128]{3,2,1,0:T(8,128)(2,1)S(1)} %copy-done.34), channel_id=1, source_target_pairs={{0,64},{32,96},{64,0},{96,32},{1,65},{33,97},{65,1},{97,33},{2,66}... | collective-permute-start | bytes 393224 | tf_op jit(solution)/shard_map/ppermute | solution.py:31
  178.8 2.3 %collective-permute-done.37 = bf16[2,2,128,128]{3,2,1,0:T(8,128)(2,1)S(1)} collective-permute-done((bf16[2,2,128,128]{3,2,1,0:T(8,128)(2,1)S(1)}, bf16[2,2,128,128]{3,2,1,0:T(8,128)(2,1)S(1)}, u32[]{:S(2)}, u32[]{:S(2)}) %collective-permute-start.37) | collective-permute-done | bytes 131104 | tf_op jit(solution)/shard_map/ppermute | solution.py:31
  181.1 2.6 %collective-permute-done.38 = bf16[2,2,128,128]{3,2,1,0:T(8,128)(2,1)S(1)} collective-permute-done((bf16[2,2,128,128]{3,2,1,0:T(8,128)(2,1)S(1)}, bf16[2,2,128,128]{3,2,1,0:T(8,128)(2,1)S(1)}, u32[]{:S(2)}, u32[]{:S(2)}) %collective-permute-start.38) | collective-permute-done | bytes 131104 | tf_op jit(solution)/shard_map/ppermute | solution.py:31
  (179 shorter events, 50.6 us)
Async XLA Ops:
  7.2 79.9 %all-gather.5.cloned.1.call-start = ((), (), s32[]{:S(2)}) async-start(), calls=%async_computation | async-start | bytes 17571840 | tf_op jit(solution)/shard_map/all_gather | solution.py:408
  9.3 153.9 %all-gather.7.cloned.1.call-start = ((), (), s32[]{:S(2)}) async-start(), calls=%async_computation.1 | async-start | bytes 4325376 | tf_op jit(solution)/shard_map/all_gather | solution.py:435
  10.8 10.5 %collective-permute-start.2 = (bf16[256,512]{1,0:T(8,128)(2,1)S(1)}, bf16[256,512]{1,0:T(8,128)(2,1)S(1)}, u32[]{:S(2)}, u32[]{:S(2)}) collective-permute-start(bf16[256,512]{1,0:T(8,128)(2,1)S(1)} %get-tuple-element.169), channel_id=1, source_target_pairs={{0,8},{8,16},{16,24},{24,0},{1,9},{9,17},{17,25},{25,1},{2,10},{10... | collective-permute-start | bytes 786440 | tf_op jit(solution)/shard_map/ppermute | solution.py:31
  12.8 16.3 %collective-permute-start.3 = (bf16[256,512]{1,0:T(8,128)(2,1)S(1)}, bf16[256,512]{1,0:T(8,128)(2,1)S(1)}, u32[]{:S(2)}, u32[]{:S(2)}) collective-permute-start(bf16[256,512]{1,0:T(8,128)(2,1)S(1)} %get-tuple-element.171), channel_id=1, source_target_pairs={{0,16},{8,24},{16,0},{24,8},{1,17},{9,25},{17,1},{25,9},{2,18},{10... | collective-permute-start | bytes 786440 | tf_op jit(solution)/shard_map/ppermute | solution.py:31
  16.4 13.8 %collective-permute-start.4 = (bf16[256,512]{1,0:T(8,128)(2,1)S(1)}, bf16[256,512]{1,0:T(8,128)(2,1)S(1)}, u32[]{:S(2)}, u32[]{:S(2)}) collective-permute-start(bf16[256,512]{1,0:T(8,128)(2,1)S(1)} %get-tuple-element.170), channel_id=1, source_target_pairs={{0,24},{8,0},{16,8},{24,16},{1,25},{9,1},{17,9},{25,17},{2,26},{10... | collective-permute-start | bytes 786440 | tf_op jit(solution)/shard_map/ppermute | solution.py:31
  18.4 12.9 %collective-permute-start.1 = (bf16[2,32,2048]{2,1,0:T(8,128)(2,1)S(1)}, bf16[2,32,2048]{2,1,0:T(8,128)(2,1)S(1)}, u32[]{:S(2)}, u32[]{:S(2)}) collective-permute-start(bf16[2,32,2048]{2,1,0:T(8,128)(2,1)S(1)} %dynamic-slice_bitcast_fusion), channel_id=1, source_target_pairs={{0,2},{2,0},{4,6},{6,4},{1,3},{3,1},{5,7},{7,5},{8,10},{10,8},{12,... | collective-permute-start | bytes 786440 | tf_op jit(solution)/shard_map/ppermute | solution.py:357
  20.0 53.7 %collective-permute-start = (bf16[2,32,8192]{2,1,0:T(8,128)(2,1)}, bf16[2,32,8192]{2,1,0:T(8,128)(2,1)}, u32[]{:S(2)}, u32[]{:S(2)}) collective-permute-start(bf16[2,32,8192]{2,1,0:T(8,128)(2,1)} %bitcast.1), channel_id=1, source_target_pairs={{0,1},{1,0},{2,3},{3,2},{4,5},{5,4},{6,7},{7,6},{8,9},{9,8},{10,11... | collective-permute-start | bytes 3145736 | tf_op jit(solution)/shard_map/ppermute | solution.py:39
  31.3 13.0 %collective-permute-start.5 = (bf16[2,32,2048]{2,1,0:T(8,128)(2,1)S(1)}, bf16[2,32,2048]{2,1,0:T(8,128)(2,1)S(1)}, u32[]{:S(2)}, u32[]{:S(2)}) collective-permute-start(bf16[2,32,2048]{2,1,0:T(8,128)(2,1)S(1)} %collective-permute-done.1), channel_id=1, source_target_pairs={{0,96},{32,0},{64,32},{96,64},{1,97},{33,1},{65,33},{97,65},{2,98}... | collective-permute-start | bytes 786440 | tf_op jit(solution)/shard_map/ppermute | solution.py:31
  34.1 15.0 %collective-permute-start.6 = (bf16[2,32,2048]{2,1,0:T(8,128)(2,1)S(1)}, bf16[2,32,2048]{2,1,0:T(8,128)(2,1)}, u32[]{:S(2)}, u32[]{:S(2)}) collective-permute-start(bf16[2,32,2048]{2,1,0:T(8,128)(2,1)S(1)} %collective-permute-done.1), channel_id=1, source_target_pairs={{0,64},{32,96},{64,0},{96,32},{1,65},{33,97},{65,1},{97,33},{2,66}... | collective-permute-start | bytes 786440 | tf_op jit(solution)/shard_map/ppermute | solution.py:31
  34.8 16.0 %collective-permute-start.7 = (bf16[2,32,2048]{2,1,0:T(8,128)(2,1)S(1)}, bf16[2,32,2048]{2,1,0:T(8,128)(2,1)}, u32[]{:S(2)}, u32[]{:S(2)}) collective-permute-start(bf16[2,32,2048]{2,1,0:T(8,128)(2,1)S(1)} %collective-permute-done.1), channel_id=1, source_target_pairs={{0,32},{32,64},{64,96},{96,0},{1,33},{33,65},{65,97},{97,1},{2,34}... | collective-permute-start | bytes 786440 | tf_op jit(solution)/shard_map/ppermute | solution.py:31
  38.5 31.8 %collective-permute-start.9 = (bf16[1024,512]{1,0:T(8,128)(2,1)}, bf16[1024,512]{1,0:T(8,128)(2,1)S(1)}, u32[]{:S(2)}, u32[]{:S(2)}) collective-permute-start(bf16[1024,512]{1,0:T(8,128)(2,1)} %pad_maximum_fusion.1), channel_id=1, source_target_pairs={{0,32},{32,64},{64,96},{96,0},{1,33},{33,65},{65,97},{97,1},{2,34}... | collective-permute-start | bytes 3145736 | tf_op jit(solution)/shard_map/ppermute | solution.py:31
  44.2 26.2 %collective-permute-start.11 = (bf16[1024,512]{1,0:T(8,128)(2,1)}, bf16[1024,512]{1,0:T(8,128)(2,1)S(1)}, u32[]{:S(2)}, u32[]{:S(2)}) collective-permute-start(bf16[1024,512]{1,0:T(8,128)(2,1)} %pad_maximum_fusion.1), channel_id=1, source_target_pairs={{0,96},{32,0},{64,32},{96,64},{1,97},{33,1},{65,33},{97,65},{2,98}... | collective-permute-start | bytes 3145736 | tf_op jit(solution)/shard_map/ppermute | solution.py:31
  57.9 15.8 %collective-permute-start.8 = (bf16[2,32,8192]{2,1,0:T(8,128)(2,1)}, bf16[2,32,8192]{2,1,0:T(8,128)(2,1)}, u32[]{:S(2)}, u32[]{:S(2)}) collective-permute-start(bf16[2,32,8192]{2,1,0:T(8,128)(2,1)} %constant_dynamic-slice_fusion.5), channel_id=1, source_target_pairs={{0,1},{1,0},{2,3},{3,2},{4,5},{5,4},{6,7},{7,6},{8,9},{9,8},{10,11... | collective-permute-start | bytes 3145736 | tf_op jit(solution)/shard_map/ppermute | solution.py:39
  70.3 15.2 %collective-permute-start.10 = (bf16[512,512]{1,0:T(8,128)(2,1)S(1)}, bf16[512,512]{1,0:T(8,128)(2,1)S(1)}, u32[]{:S(2)}, u32[]{:S(2)}) collective-permute-start(bf16[512,512]{1,0:T(8,128)(2,1)S(1)} %slice.12), channel_id=1, source_target_pairs={{0,32},{32,64},{64,96},{96,0},{1,33},{33,65},{65,97},{97,1},{2,34}... | collective-permute-start | bytes 1572872 | tf_op jit(solution)/shard_map/ppermute | solution.py:31
  70.5 15.1 %collective-permute-start.12 = (bf16[512,512]{1,0:T(8,128)(2,1)S(1)}, bf16[512,512]{1,0:T(8,128)(2,1)S(1)}, u32[]{:S(2)}, u32[]{:S(2)}) collective-permute-start(bf16[512,512]{1,0:T(8,128)(2,1)S(1)} %slice.13), channel_id=1, source_target_pairs={{0,96},{32,0},{64,32},{96,64},{1,97},{33,1},{65,33},{97,65},{2,98}... | collective-permute-start | bytes 1572872 | tf_op jit(solution)/shard_map/ppermute | solution.py:31
  92.3 8.9 %collective-permute-start.13 = (bf16[2,2,128,128]{3,2,1,0:T(8,128)(2,1)}, bf16[2,2,128,128]{3,2,1,0:T(8,128)(2,1)S(1)}, u32[]{:S(2)}, u32[]{:S(2)}) collective-permute-start(bf16[2,2,128,128]{3,2,1,0:T(8,128)(2,1)} %project_key_value.1.kv0), channel_id=1, source_target_pairs={{0,2},{2,0},{4,6},{6,4},{1,3},{3,1},{5,7},{7,5},{8,10},{10,8},{12,... | collective-permute-start | bytes 393224 | tf_op jit(solution)/shard_map/ppermute | solution.py:436
  93.9 7.9 %collective-permute-start.14 = (bf16[2,2,128,128]{3,2,1,0:T(8,128)(2,1)}, bf16[2,2,128,128]{3,2,1,0:T(8,128)(2,1)S(1)}, u32[]{:S(2)}, u32[]{:S(2)}) collective-permute-start(bf16[2,2,128,128]{3,2,1,0:T(8,128)(2,1)} %project_key_value.1.kv0), channel_id=1, source_target_pairs={{0,1},{1,0},{2,3},{3,2},{4,5},{5,4},{6,7},{7,6},{8,9},{9,8},{10,11... | collective-permute-start | bytes 393224 | tf_op jit(solution)/shard_map/ppermute | solution.py:39
  107.4 17.6 %collective-permute-start.16 = (bf16[512,256]{1,0:T(8,128)(2,1)}, bf16[512,256]{1,0:T(8,128)(2,1)S(1)}, u32[]{:S(2)}, u32[]{:S(2)}) collective-permute-start(bf16[512,256]{1,0:T(8,128)(2,1)} %attend.2.refs_8_), channel_id=1, source_target_pairs={{0,16},{8,24},{16,0},{24,8},{1,17},{9,25},{17,1},{25,9},{2,18},{10... | collective-permute-start | bytes 786440 | tf_op jit(solution)/shard_map/ppermute | solution.py:31
  108.9 19.3 %collective-permute-start.17 = (bf16[512,256]{1,0:T(8,128)(2,1)}, bf16[512,256]{1,0:T(8,128)(2,1)S(1)}, u32[]{:S(2)}, u32[]{:S(2)}) collective-permute-start(bf16[512,256]{1,0:T(8,128)(2,1)} %attend.2.refs_8_), channel_id=1, source_target_pairs={{0,8},{8,16},{16,24},{24,0},{1,9},{9,17},{17,25},{25,1},{2,10},{10... | collective-permute-start | bytes 786440 | tf_op jit(solution)/shard_map/ppermute | solution.py:31
  111.1 17.1 %collective-permute-start.18 = (bf16[512,256]{1,0:T(8,128)(2,1)}, bf16[512,256]{1,0:T(8,128)(2,1)S(1)}, u32[]{:S(2)}, u32[]{:S(2)}) collective-permute-start(bf16[512,256]{1,0:T(8,128)(2,1)} %attend.2.refs_8_), channel_id=1, source_target_pairs={{0,24},{8,0},{16,8},{24,16},{1,25},{9,1},{17,9},{25,17},{2,26},{10... | collective-permute-start | bytes 786440 | tf_op jit(solution)/shard_map/ppermute | solution.py:31
  123.8 13.9 %collective-permute-start.23 = (bf16[512,256]{1,0:T(8,128)(2,1)}, bf16[512,256]{1,0:T(8,128)(2,1)S(1)}, u32[]{:S(2)}, u32[]{:S(2)}) collective-permute-start(bf16[512,256]{1,0:T(8,128)(2,1)} %attend.3.refs_8_), channel_id=1, source_target_pairs={{0,16},{8,24},{16,0},{24,8},{1,17},{9,25},{17,1},{25,9},{2,18},{10... | collective-permute-start | bytes 786440 | tf_op jit(solution)/shard_map/ppermute | solution.py:31
  124.9 19.5 %collective-permute-start.24 = (bf16[512,256]{1,0:T(8,128)(2,1)}, bf16[512,256]{1,0:T(8,128)(2,1)S(1)}, u32[]{:S(2)}, u32[]{:S(2)}) collective-permute-start(bf16[512,256]{1,0:T(8,128)(2,1)} %attend.3.refs_8_), channel_id=1, source_target_pairs={{0,8},{8,16},{16,24},{24,0},{1,9},{9,17},{17,25},{25,1},{2,10},{10... | collective-permute-start | bytes 786440 | tf_op jit(solution)/shard_map/ppermute | solution.py:31
  124.9 19.5 %collective-permute-start.25 = (bf16[512,256]{1,0:T(8,128)(2,1)}, bf16[512,256]{1,0:T(8,128)(2,1)S(1)}, u32[]{:S(2)}, u32[]{:S(2)}) collective-permute-start(bf16[512,256]{1,0:T(8,128)(2,1)} %attend.3.refs_8_), channel_id=1, source_target_pairs={{0,24},{8,0},{16,8},{24,16},{1,25},{9,1},{17,9},{25,17},{2,26},{10... | collective-permute-start | bytes 786440 | tf_op jit(solution)/shard_map/ppermute | solution.py:31
  154.6 11.1 %collective-permute-start.31 = (bf16[1,512,256]{2,1,0:T(8,128)(2,1)}, bf16[1,512,256]{2,1,0:T(8,128)(2,1)S(1)}, u32[]{:S(2)}, u32[]{:S(2)}) collective-permute-start(bf16[1,512,256]{2,1,0:T(8,128)(2,1)} %get-tuple-element.130), channel_id=1, source_target_pairs={{0,1},{1,0},{2,3},{3,2},{4,5},{5,4},{6,7},{7,6},{8,9},{9,8},{10,11... | collective-permute-start | bytes 786440 | tf_op jit(solution)/shard_map/ppermute | solution.py:39
  154.8 11.0 %collective-permute-start.32 = (bf16[1,512,256]{2,1,0:T(8,128)(2,1)}, bf16[1,512,256]{2,1,0:T(8,128)(2,1)S(1)}, u32[]{:S(2)}, u32[]{:S(2)}) collective-permute-start(bf16[1,512,256]{2,1,0:T(8,128)(2,1)} %get-tuple-element.131), channel_id=1, source_target_pairs={{0,1},{1,0},{2,3},{3,2},{4,5},{5,4},{6,7},{7,6},{8,9},{9,8},{10,11... | collective-permute-start | bytes 786440 | tf_op jit(solution)/shard_map/ppermute | solution.py:39
  157.7 13.0 %collective-permute-start.26 = (bf16[512,256]{1,0:T(8,128)(2,1)}, bf16[512,256]{1,0:T(8,128)(2,1)S(1)}, u32[]{:S(2)}, u32[]{:S(2)}) collective-permute-start(bf16[512,256]{1,0:T(8,128)(2,1)} %get-tuple-element.120), channel_id=1, source_target_pairs={{0,4},{2,6},{4,0},{6,2},{1,5},{3,7},{5,1},{7,3},{8,12},{10,14},{12... | collective-permute-start | bytes 786440 | tf_op jit(solution)/shard_map/ppermute | solution.py:31
  160.0 14.1 %collective-permute-start.27 = (bf16[512,256]{1,0:T(8,128)(2,1)}, bf16[512,256]{1,0:T(8,128)(2,1)S(1)}, u32[]{:S(2)}, u32[]{:S(2)}) collective-permute-start(bf16[512,256]{1,0:T(8,128)(2,1)} %get-tuple-element.121), channel_id=1, source_target_pairs={{0,2},{2,4},{4,6},{6,0},{1,3},{3,5},{5,7},{7,1},{8,10},{10,12},{12... | collective-permute-start | bytes 786440 | tf_op jit(solution)/shard_map/ppermute | solution.py:31
  160.0 14.6 %collective-permute-start.28 = (bf16[512,256]{1,0:T(8,128)(2,1)}, bf16[512,256]{1,0:T(8,128)(2,1)S(1)}, u32[]{:S(2)}, u32[]{:S(2)}) collective-permute-start(bf16[512,256]{1,0:T(8,128)(2,1)} %get-tuple-element.122), channel_id=1, source_target_pairs={{0,6},{2,0},{4,2},{6,4},{1,7},{3,1},{5,3},{7,5},{8,14},{10,8},{12,... | collective-permute-start | bytes 786440 | tf_op jit(solution)/shard_map/ppermute | solution.py:31
  169.1 14.5 %collective-permute-start.33 = (bf16[512,256]{1,0:T(8,128)(2,1)}, bf16[512,256]{1,0:T(8,128)(2,1)S(1)}, u32[]{:S(2)}, u32[]{:S(2)}) collective-permute-start(bf16[512,256]{1,0:T(8,128)(2,1)} %get-tuple-element.143), channel_id=1, source_target_pairs={{0,4},{2,6},{4,0},{6,2},{1,5},{3,7},{5,1},{7,3},{8,12},{10,14},{12... | collective-permute-start | bytes 786440 | tf_op jit(solution)/shard_map/ppermute | solution.py:31
  169.3 8.3 %collective-permute-start.36 = (bf16[2,2,128,128]{3,2,1,0:T(8,128)(2,1)S(1)}, bf16[2,2,128,128]{3,2,1,0:T(8,128)(2,1)S(1)}, u32[]{:S(2)}, u32[]{:S(2)}) collective-permute-start(bf16[2,2,128,128]{3,2,1,0:T(8,128)(2,1)S(1)} %copy-done.35), channel_id=1, source_target_pairs={{0,32},{32,64},{64,96},{96,0},{1,33},{33,65},{65,97},{97,1},{2,34}... | collective-permute-start | bytes 393224 | tf_op jit(solution)/shard_map/ppermute | solution.py:31
  170.7 13.9 %collective-permute-start.34 = (bf16[512,256]{1,0:T(8,128)(2,1)}, bf16[512,256]{1,0:T(8,128)(2,1)S(1)}, u32[]{:S(2)}, u32[]{:S(2)}) collective-permute-start(bf16[512,256]{1,0:T(8,128)(2,1)} %get-tuple-element.144), channel_id=1, source_target_pairs={{0,2},{2,4},{4,6},{6,0},{1,3},{3,5},{5,7},{7,1},{8,10},{10,12},{12... | collective-permute-start | bytes 786440 | tf_op jit(solution)/shard_map/ppermute | solution.py:31
  174.1 10.5 %collective-permute-start.35 = (bf16[512,256]{1,0:T(8,128)(2,1)}, bf16[512,256]{1,0:T(8,128)(2,1)S(1)}, u32[]{:S(2)}, u32[]{:S(2)}) collective-permute-start(bf16[512,256]{1,0:T(8,128)(2,1)} %get-tuple-element.145), channel_id=1, source_target_pairs={{0,6},{2,0},{4,2},{6,4},{1,7},{3,1},{5,3},{7,5},{8,14},{10,8},{12,... | collective-permute-start | bytes 786440 | tf_op jit(solution)/shard_map/ppermute | solution.py:31
  (45 other events, 351.3 us)
Sparse Core Ops, SparseCore 0:
  10.3 76.7 all-gather.4
  92.5 57.7 all-gather.6
